TPU v7x, 512 devices: a whole 4x4x16 slice. The times are simulated.
512 devices in a mesh: gx: 8 (over y, core), gy: 8 (over z_hi, x), gz: 8 (over z_lo).
Axes of the slice: x: 4, y: 4, z: 16 (z_hi: 2, z_lo: 8; z = z_hi * 8 + z_lo), core: 2. Of those that a mesh axis runs over, the one named last changes fastest.
Arguments:
- inputs: bfloat16 [1024, 12288], P(('gx', 'gz'), 'gy'), may hold values from -60 to 60
- ln_gain: float32 [12288], P('gy'), may hold values from 0.5 to 1.5
- ln_bias: float32 [12288], P('gy'), may hold values from -3 to 3
- weight_in: bfloat16 [12288, 24576], P(('gy', 'gx'), 'gz'), may hold values from -0.0546875 to 0.0546875
- up_bias: float32 [24576], P('gz'), may hold values from -3 to 3
- grad_hidden: bfloat16 [1024, 24576], P(('gx', 'gy'), 'gz'), may hold values from -24 to 24
Outputs:
- grad_inputs: bfloat16 [1024, 12288], P(('gx', 'gz'), 'gy')
- grad_weight: bfloat16 [12288, 24576], P(('gy', 'gx'), 'gz')
- grad_up_bias: float32 [24576], P('gz')
- grad_ln_gain: float32 [12288], P('gy')
- grad_ln_bias: float32 [12288], P('gy')
All inputs are finite; a program needn't handle non-finite values.
Results may differ from a plain program's by a relative error of at most 0.019.
Values may be sent and summed in bfloat16 or wider, within the bound.
No kernel may reach another device: no remote copies, remote signals or barrier semaphores. Data moves between devices by JAX's collectives and lax.ppermute only.
A program may use at most 64 MiB of HBM per device.

v0:
```python
import math

import jax
import jax.numpy as jnp
from jax import lax
from jax.sharding import PartitionSpec as P

D = 12288


gelu_scale = math.sqrt(2.0 / math.pi)
cubic = 0.044715
epsilon = 1e-05


def gelu_slope(value):
    inner = gelu_scale * (value + cubic * value * value * value)
    tangent = jnp.tanh(inner)
    return 0.5 * (1.0 + tangent) + 0.5 * value * (1.0 - tangent * tangent) * gelu_scale * (
        1.0 + 3.0 * cubic * value * value
    )


def shards(inputs, ln_gain, ln_bias, weight_in, up_bias, grad_hidden):
    x_float = inputs.astype(jnp.float32)
    feature_total = lax.psum(jnp.sum(x_float, axis=1), "gy")
    mean = feature_total / D
    centered = x_float - mean[:, None]
    variance = lax.psum(jnp.sum(centered * centered, axis=1), "gy") / D
    inv_std = lax.rsqrt(variance + epsilon)[:, None]
    x_hat = centered * inv_std
    normed = (x_hat * ln_gain + ln_bias).astype(jnp.bfloat16)
    gathered = lax.all_gather(normed, "gz", axis=0, tiled=True)
    partial_hidden = jnp.dot(
        gathered,
        lax.all_gather(weight_in, "gx", axis=0, tiled=True),
        preferred_element_type=jnp.float32,
    )
    hidden = (
        lax.psum_scatter(
            partial_hidden.astype(jnp.bfloat16), "gy", scatter_dimension=0, tiled=True
        ).astype(jnp.float32)
        + up_bias
    )
    grad_pre = (grad_hidden.astype(jnp.float32) * gelu_slope(hidden)).astype(jnp.bfloat16)
    grad_up_bias = lax.psum(jnp.sum(grad_pre.astype(jnp.float32), axis=0), ("gx", "gy"))
    feature_rows = lax.all_to_all(gathered, "gx", split_axis=1, concat_axis=0, tiled=True)
    token_count = feature_rows.shape[0]
    sub_width = weight_in.shape[0]
    grad_local = lax.all_gather(grad_pre, "gy", axis=0, tiled=True)
    portion = lax.all_gather(grad_local, "gx", axis=0, tiled=True)
    weight_sum = lax.dot_general(
        feature_rows, portion, (((0,), (0,)), ((), ())), preferred_element_type=jnp.float32
    )
    back_part = lax.dot_general(
        portion, weight_in, (((1,), (1,)), ((), ())), preferred_element_type=jnp.float32
    )
    input_sum = back_part
    weight_sum, input_sum = (weight_sum, input_sum)
    grad_weight = weight_sum.astype(jnp.bfloat16)
    group_count = lax.axis_size("gx")
    depth_count = lax.axis_size("gz")
    reshaped = input_sum.reshape(
        group_count, depth_count, token_count // (group_count * depth_count), sub_width
    )
    own_part = lax.psum_scatter(
        reshaped.astype(jnp.bfloat16), "gz", scatter_dimension=1, tiled=True
    ).astype(jnp.float32)
    arranged = lax.all_to_all(
        own_part[:, 0].astype(jnp.bfloat16), "gx", split_axis=0, concat_axis=2, tiled=True
    )
    grad_float = arranged[0].astype(jnp.float32)
    scaled = grad_float * ln_gain
    first_total, second_total = lax.psum(
        (jnp.sum(scaled, axis=1), jnp.sum(scaled * x_hat, axis=1)), "gy"
    )
    grad_inputs = (
        inv_std * (scaled - first_total[:, None] / D - x_hat * (second_total[:, None] / D))
    ).astype(jnp.bfloat16)
    grad_ln_gain, grad_ln_bias = lax.psum(
        (jnp.sum(grad_float * x_hat, axis=0), jnp.sum(grad_float, axis=0)), ("gx", "gz")
    )
    return (grad_inputs, grad_weight, grad_up_bias, grad_ln_gain, grad_ln_bias)


def solution(mesh):
    return jax.shard_map(
        shards,
        mesh=mesh,
        in_specs=(
            P(("gx", "gz"), "gy"),
            P("gy"),
            P("gy"),
            P(("gy", "gx"), "gz"),
            P("gz"),
            P(("gx", "gy"), "gz"),
        ),
        out_specs=(P(("gx", "gz"), "gy"), P(("gy", "gx"), "gz"), P("gz"), P("gy"), P("gy")),
        check_vma=False,
    )
```

profile of v0, /device:TPU:1, one launch (start us, length us, event | category | flops | bytes accessed | tf_op | source)
XLA Modules:
  0.0 1396.5 jit_solution(2842227654196051304)
XLA Ops:
  7.2 0.7 all-gather.3.cloned.1.call-update
  7.9 0.9 convert_reduce_fusion.1
  8.9 46.4 %psum.49 = f32[16]{0:T(128)S(1)} all-reduce(f32[16]{0:T(128)S(1)} %convert_reduce_fusion.1), channel_id=1, replica_groups=mesh['gx'=8,'gy'=8,'gz'=8] {'gy'}, use_global_device_ids=true, to_apply=%region_1.0 | all-reduce | flops 16 | bytes 128 | tf_op jit(solution)/shard_map/psum | solution.py:26
  55.3 1.0 fusion.22
  56.3 29.9 %psum.50 = f32[16]{0:T(128)S(1)} all-reduce(f32[16]{0:T(128)S(1)} %fusion.22), channel_id=1, replica_groups=mesh['gx'=8,'gy'=8,'gz'=8] {'gy'}, use_global_device_ids=true, to_apply=%region_3.0 | all-reduce | flops 16 | bytes 128 | tf_op jit(solution)/shard_map/psum | solution.py:29
  86.2 0.9 fusion.16
  87.1 41.7 %all_gather.12 = bf16[128,1536]{1,0:T(8,128)(2,1)S(1)} all-gather(bf16[16,1536]{1,0:T(8,128)(2,1)S(1)} %fusion.16), channel_id=1, replica_groups=mesh['gx'=8,'gy'=8,'gz'=8] {'gz'}, dimensions={0}, use_global_device_ids=true | all-gather | bytes 442368 | tf_op jit(solution)/shard_map/all_gather | solution.py:33
  128.8 6.1 convolution_convert_fusion.1
  135.0 120.6 %reduce-scatter.5.cloned.1.call-done = bf16[16,3072]{1,0:T(8,128)(2,1)} async-done(((bf16[128,3072]{1,0:T(8,128)(2,1)}), bf16[16,3072]{1,0:T(8,128)(2,1)}) %reduce-scatter.5.cloned.1.call-update) | async-done | bytes 98320 | tf_op jit(solution)/shard_map/reduce_scatter | solution.py:40
  255.5 1.1 convert_reduce_fusion
  256.6 63.0 %all_gather.14 = bf16[128,3072]{1,0:T(8,128)(2,1)} all-gather(bf16[16,3072]{1,0:T(8,128)(2,1)S(1)} %get-tuple-element.19), channel_id=1, replica_groups=mesh['gx'=8,'gy'=8,'gz'=8] {'gy'}, dimensions={0}, use_global_device_ids=true | all-gather | bytes 884736 | tf_op jit(solution)/shard_map/all_gather | solution.py:50
  319.7 50.5 %all-gather.5.cloned.1.call-done = bf16[1024,3072]{1,0:T(8,128)(2,1)} async-done(((bf16[128,3072]{1,0:T(8,128)(2,1)}), bf16[1024,3072]{1,0:T(8,128)(2,1)}) %all-gather.5.cloned.1.call-update) | async-done | bytes 6291472 | tf_op jit(solution)/shard_map/all_gather | solution.py:51
  370.2 5.0 convolution_convert_fusion.2
  375.2 1.0 copy.20
  376.3 0.9 copy.22
  377.2 3.6 all-to-all-start.1
  380.9 1.3 dynamic-slice
  382.1 532.0 %psum.53 = f32[3072]{0:T(1024)} all-reduce(f32[3072]{0:T(1024)S(1)} %get-tuple-element.18), channel_id=1, replica_groups=mesh['gx'=8,'gy'=8,'gz'=8] {'gx','gy'}, use_global_device_ids=true, to_apply=%region_11.0 | all-reduce | flops 3072 | bytes 24576 | tf_op jit(solution)/shard_map/psum | solution.py:46
  914.1 2.1 dynamic-slice_bitcast_fusion
  916.2 41.4 %all-to-all-start = ((bf16[8,16,192]{2,1,0:T(8,128)(2,1)}), bf16[8,16,192]{2,1,0:T(8,128)(2,1)S(1)}, u32[]{:S(2)}, u32[]{:S(2)}) async-start(bf16[8,16,192]{2,1,0:T(8,128)(2,1)} %dynamic-slice_bitcast_fusion), calls=%async_computation.1 | async-start | bytes 131072 | tf_op jit(solution)/shard_map/all_to_all | solution.py:69
  957.6 5.3 convolution_convert_fusion
  963.5 30.0 %all-reduce.2 = (f32[16]{0:T(128)S(1)}, f32[16]{0:T(128)S(1)}) all-reduce(f32[16]{0:T(128)S(1)} %get-tuple-element.11, f32[16]{0:T(128)S(1)} %get-tuple-element.13), channel_id=1, replica_groups=mesh['gx'=8,'gy'=8,'gz'=8] {'gy'}, use_global_device_ids=true, to_apply=%region_9.0 | all-reduce | flops 32 | bytes 256 | tf_op jit(solution)/shard_map/psum | solution.py:74
  993.5 0.7 fusion.20
  994.3 395.7 %all-reduce.1 = (f32[1536]{0:T(1024)}, f32[1536]{0:T(1024)}) all-reduce(f32[1536]{0:T(1024)S(1)} %get-tuple-element.10, f32[1536]{0:T(1024)S(1)} %reduce_sum.72), channel_id=1, replica_groups=mesh['gx'=8,'gy'=8,'gz'=8] {'gx','gz'}, use_global_device_ids=true, to_apply=%region_13.0 | all-reduce | flops 3072 | bytes 24576 | tf_op jit(solution)/shard_map/psum | solution.py:80
  (31 shorter events, 1.0 us)
Async XLA Ops:
  7.2 121.7 %all-gather.3.cloned.1.call-start = ((), (), s32[]{:S(2)}) async-start(), calls=%async_computation.3 | async-start | bytes 10616832 | tf_op jit(solution)/shard_map/all_gather | solution.py:36
  7.9 247.6 %reduce-scatter.5.cloned.1.call-start = ((), (), s32[]{:S(2)}) async-start(), calls=%async_computation.4 | async-start | bytes 884736 | tf_op jit(solution)/shard_map/reduce_scatter | solution.py:40
  128.8 126.7 %copy-start.3 = (bf16[16,3072]{1,0:T(8,128)(2,1)S(1)}, bf16[16,3072]{1,0:T(8,128)(2,1)}, u32[]{:S(2)}) copy-start(bf16[16,3072]{1,0:T(8,128)(2,1)} %param.11) | copy-start | bytes 294916
  128.8 126.7 %copy-start.4 = (f32[3072]{0:T(1024)S(1)}, f32[3072]{0:T(1024)}, u32[]{:S(2)}) copy-start(f32[3072]{0:T(1024)} %param.10) | copy-start | bytes 36868
  128.8 241.4 %copy-start.1 = (bf16[192,3072]{1,0:T(8,128)(2,1)S(1)}, bf16[192,3072]{1,0:T(8,128)(2,1)}, u32[]{:S(2)}) copy-start(bf16[192,3072]{1,0:T(8,128)(2,1)} %param.9) | copy-start | bytes 3538948
  134.9 235.3 %all-gather.5.cloned.1.call-start = ((), (), s32[]{:S(2)}) async-start(), calls=%async_computation.5 | async-start | bytes 7077888 | tf_op jit(solution)/shard_map/all_gather | solution.py:51
  319.6 61.1 %copy-start.2 = (f32[1536]{0:T(1024)S(1)}, f32[1536]{0:T(1024)}, u32[]{:S(2)}) copy-start(f32[1536]{0:T(1024)} %param.7) | copy-start | bytes 18436
  319.7 594.5 %all-reduce.5.cloned.1.call-start = ((), (), s32[]{:S(2)}) async-start(), calls=%async_computation.6 | async-start | bytes 1048576
  377.2 539.1 %all-to-all-start.1 = ((bf16[128,8,192]{0,2,1:T(8,128)(2,1)}), bf16[128,8,192]{0,2,1:T(8,128)(2,1)S(1)}, u32[]{:S(2)}, u32[]{:S(2)}) async-start(bf16[128,8,192]{0,2,1:T(8,128)(2,1)} %bitcast.5), calls=%async_computation.2 | async-start | bytes 786432 | tf_op jit(solution)/shard_map/all_to_all | solution.py:47
  916.2 46.6 %all-to-all-start = ((bf16[8,16,192]{2,1,0:T(8,128)(2,1)}), bf16[8,16,192]{2,1,0:T(8,128)(2,1)S(1)}, u32[]{:S(2)}, u32[]{:S(2)}) async-start(bf16[8,16,192]{2,1,0:T(8,128)(2,1)} %dynamic-slice_bitcast_fusion), calls=%async_computation.1 | async-start | bytes 131072 | tf_op jit(solution)/shard_map/all_to_all | solution.py:69
  957.6 5.5 copy-start
Sparse Core Ops, SparseCore 0:
  10.1 67.5 all-gather.2
  135.0 120.4 reduce-scatter.4
  319.8 50.3 all-gather.4
  376.4 118.0 all-reduce.4
where the time goes:
time: 1420 us; the launch traced here: 1400 us
  blocking collectives  1140 us (80%)
  waiting for transfers between devices  172 us (12%)
  starting transfers between devices  45.1 us (3%)
  matrix products  16.4 us (1%)
    psum x1, blocking collectives, shards(): lax.psum(jnp.sum(grad_pre.astype(jnp.float32), axis=0), ('gx', 'gy'))  532 us
    psum x1, blocking collectives, shards(): lax.psum((jnp.sum(grad_float * x_hat, axis=0), jnp.sum(grad_float, axis=0...  396 us
    reduce_scatter x1, waiting for transfers between devices, shards(): lax.psum_scatter(partial_hidden.astype(jnp.bfloat16), 'gy', scatter_dimen...  121 us
    all_gather x1, blocking collectives, shards(): grad_local = lax.all_gather(grad_pre, 'gy', axis=0, tiled=True)  63 us
    all_gather x1, waiting for transfers between devices, shards(): portion = lax.all_gather(grad_local, 'gx', axis=0, tiled=True)  50.5 us
    psum x1, blocking collectives, shards(): feature_total = lax.psum(jnp.sum(x_float, axis=1), 'gy')  46.4 us
    all_gather x1, blocking collectives, shards(): gathered = lax.all_gather(normed, 'gz', axis=0, tiled=True)  41.7 us
    all_to_all x1, starting transfers between devices, shards(): lax.all_to_all(own_part[:, 0].astype(jnp.bfloat16), 'gx', split_axis=0, c...  41.4 us
  transfers between devices with their start and end apart: 6, of which 2 were waited for; matrix products, arithmetic and copies ran while one was open for 1% of the time, Pallas kernels for 0%

commit v1 on v0

v1 whole, which is shorter than its diff:
```python
import math

import jax
import jax.numpy as jnp
from jax import lax
from jax.sharding import Mesh, PartitionSpec as P

D = 12288


gelu_scale = math.sqrt(2.0 / math.pi)
cubic = 0.044715
epsilon = 1e-05

gx = ("y", "core")
gy = ("zh", "x")


def gelu_slope(value):
    inner = gelu_scale * (value + cubic * value * value * value)
    tangent = jnp.tanh(inner)
    return 0.5 * (1.0 + tangent) + 0.5 * value * (1.0 - tangent * tangent) * gelu_scale * (
        1.0 + 3.0 * cubic * value * value
    )


def exchange(blocks, axis):
    return lax.all_to_all(blocks, axis, split_axis=0, concat_axis=0, tiled=True)


def spread(block, axis):
    count = lax.axis_size(axis)
    return exchange(jnp.broadcast_to(block[None], (count,) + block.shape), axis)


def swap(block):
    return lax.ppermute(block, "zh", [(0, 1), (1, 0)])


def split_float(value):
    high = lax.reduce_precision(value, 8, 7)
    return high.astype(jnp.bfloat16), (value - high).astype(jnp.bfloat16)


def shards(inputs, ln_gain, ln_bias, weight_in, up_bias, grad_hidden):
    f32, bf16 = jnp.float32, jnp.bfloat16
    rows, width = inputs.shape
    hidden_width = weight_in.shape[1]
    sub_width = weight_in.shape[0]
    depth = lax.axis_size("gz")
    halves, around = lax.axis_size("zh"), lax.axis_size("x")
    local = depth * rows

    weight = lax.all_gather(weight_in, gx, axis=0, tiled=True)

    x_float = (
        spread(inputs, "gz")
        .reshape(halves, around, rows, width)
        .transpose(1, 0, 2, 3)
        .reshape(local, width)
        .astype(f32)
    )
    own_mean = jnp.mean(x_float, axis=1)
    own_centered = x_float - own_mean[:, None]
    own_square = jnp.sum(own_centered * own_centered, axis=1)
    moments = spread(jnp.stack([own_mean, own_square]), gy)
    mean = jnp.mean(moments[:, 0], axis=0)
    shift = moments[:, 0] - mean
    variance = (jnp.sum(moments[:, 1], axis=0) + width * jnp.sum(shift * shift, axis=0)) / D
    inv_std = lax.rsqrt(variance + epsilon)
    x_hat = (x_float - mean[:, None]) * inv_std[:, None]
    normed = (x_hat * ln_gain + ln_bias).astype(bf16)

    other_cotangent = swap(grad_hidden)
    upper = lax.axis_index("zh") == 1
    cotangent = jnp.concatenate(
        [
            jnp.where(upper, other_cotangent, grad_hidden),
            jnp.where(upper, grad_hidden, other_cotangent),
        ]
    ).astype(f32)

    partial_hidden = jnp.dot(normed, weight, preferred_element_type=f32).astype(bf16)
    arrived = exchange(partial_hidden.reshape(around, halves * rows, hidden_width), "x")
    half_sum = lax.reduce_precision(jnp.sum(arrived.astype(f32), axis=0), 8, 7)
    hidden = half_sum + swap(half_sum.astype(bf16)).astype(f32) + up_bias
    grad_pre = (cotangent * gelu_slope(hidden)).astype(bf16)
    grad_local = spread(grad_pre, "x").reshape(local, hidden_width)
    portion = lax.all_gather(grad_local, gx, axis=0, tiled=True)

    feature_rows = exchange(
        normed.reshape(local, width // sub_width, sub_width).transpose(1, 0, 2), gx
    ).reshape(-1, sub_width)
    grad_weight = lax.dot_general(
        feature_rows, portion, (((0,), (0,)), ((), ())), preferred_element_type=f32
    ).astype(bf16)
    grad_up_bias = jnp.sum(portion.astype(f32), axis=0)

    back = lax.dot_general(
        grad_local, weight, (((1,), (1,)), ((), ())), preferred_element_type=f32
    )
    sums = jnp.stack([jnp.sum(back * x_hat, axis=0), jnp.sum(back, axis=0)])
    high, low = split_float(sums)
    extra = jnp.concatenate([high, low, jnp.zeros((4, width), bf16)])
    ordered = (
        back.astype(bf16)
        .reshape(around, halves, rows, width)
        .transpose(1, 0, 2, 3)
        .reshape(depth, rows, width)
    )
    landed = exchange(
        jnp.concatenate([ordered, jnp.broadcast_to(extra[None], (depth,) + extra.shape)], axis=1),
        "gz",
    ).astype(f32)
    total = jnp.sum(landed, axis=0)
    grad_float = total[:rows].astype(bf16).astype(f32)
    depth_sums = total[rows : rows + 2] + total[rows + 2 : rows + 4]
    grad_ln_gain, grad_ln_bias = jnp.sum(spread(depth_sums, gx), axis=0)

    def mine(value):
        ordered = value.reshape(around, halves, rows).transpose(1, 0, 2).reshape(depth, rows)
        return lax.dynamic_index_in_dim(ordered, lax.axis_index("gz"), 0, keepdims=False)[:, None]

    own_inv = mine(inv_std)
    own_hat = (inputs.astype(f32) - mine(mean)) * own_inv
    scaled = grad_float * ln_gain
    token_sums = jnp.stack([jnp.sum(scaled, axis=1), jnp.sum(scaled * own_hat, axis=1)])
    first_total, second_total = jnp.sum(spread(token_sums, gy), axis=0)
    grad_inputs = (
        own_inv * (scaled - first_total[:, None] / D - own_hat * (second_total[:, None] / D))
    ).astype(bf16)
    return (grad_inputs, grad_weight, grad_up_bias, grad_ln_gain, grad_ln_bias)


def solution(mesh):
    cube = Mesh(mesh.devices.reshape(4, 2, 2, 4, 8), ("y", "core", "zh", "x", "gz"))
    return jax.shard_map(
        shards,
        mesh=cube,
        in_specs=(
            P(("y", "core", "gz"), gy),
            P(gy),
            P(gy),
            P(("zh", "x", "y", "core"), "gz"),
            P("gz"),
            P(("y", "core", "zh", "x"), "gz"),
        ),
        out_specs=(
            P(("y", "core", "gz"), gy),
            P(("zh", "x", "y", "core"), "gz"),
            P("gz"),
            P(gy),
            P(gy),
        ),
        check_vma=False,
    )
```

time: 1420 us -> 251 us (0.18); the launches traced: 1400 us -> 250 us
  blocking collectives: 1140 us -> 60.5 us
  waiting for transfers between devices: 172 us -> 72 us
  starting transfers between devices: 45.1 us -> 70.3 us
    psum x5 -> x0, blocking collectives: 1030 us -> none  [the longest x1 532 us: shards(): lax.psum(jnp.sum(grad_pre.astype(jnp.float32), axis=0), ('gx', 'gy'))]
    reduce_scatter x1 -> x0, waiting for transfers between devices: 121 us -> none  [shards(): lax.psum_scatter(partial_hidden.astype(jnp.bfloat16), 'gy', scatter_dimen...]
    all_gather x2 -> x0, blocking collectives: 105 us -> none  [the longest x1 63 us: shards(): grad_local = lax.all_gather(grad_pre, 'gy', axis=0, tiled=True)]
    all_to_all x0 -> x2, blocking collectives: none -> 60.5 us  [exchange(): return lax.all_to_all(blocks, axis, split_axis=0, concat_axis=0, tiled=True)]
    all_to_all x2 -> x6, waiting for transfers between devices: 0.01 us -> 55 us  [exchange(): return lax.all_to_all(blocks, axis, split_axis=0, concat_axis=0, tiled=True)]
    all_gather x2, waiting for transfers between devices: 50.5 us -> 11.1 us  [the longest x1 11.1 us: shards(): weight = lax.all_gather(weight_in, gx, axis=0, tiled=True)]
    ppermute x0 -> x2, starting transfers between devices: none -> 24.4 us  [swap(): return lax.ppermute(block, 'zh', [(0, 1), (1, 0)])]
    all_to_all x2 -> x6, starting transfers between devices: 45 us -> 45.9 us  [exchange(): return lax.all_to_all(blocks, axis, split_axis=0, concat_axis=0, tiled=True)]
  transfers between devices with their start and end apart: 6 -> 10, of which waited for: 2 -> 7; matrix products, arithmetic and copies ran while one was open for 1% -> 8% of each run, Pallas kernels for 0% -> 0%
where the time goes in v1:
time: 251 us; the launch traced here: 250 us
  waiting for transfers between devices  72 us (29%)
  starting transfers between devices  70.3 us (28%)
  blocking collectives  60.5 us (24%)
  matrix products  18.4 us (7%)
  between operations  14.3 us (6%)
  other arithmetic  8.6 us (3%)
  local copies, waits for them, and re-layouts  5.58 us (2%)
    all_to_all x2, blocking collectives, exchange(): return lax.all_to_all(blocks, axis, split_axis=0, concat_axis=0, tiled=True)  60.5 us
    all_to_all x6, waiting for transfers between devices, exchange(): return lax.all_to_all(blocks, axis, split_axis=0, concat_axis=0, tiled=True)  55 us
    all_to_all x6, starting transfers between devices, exchange(): return lax.all_to_all(blocks, axis, split_axis=0, concat_axis=0, tiled=True)  45.9 us
    ppermute x2, starting transfers between devices, swap(): return lax.ppermute(block, 'zh', [(0, 1), (1, 0)])  24.4 us
    all_gather x1, waiting for transfers between devices, shards(): weight = lax.all_gather(weight_in, gx, axis=0, tiled=True)  11.1 us
    dot_general x1, matrix products, shards(): lax.dot_general(grad_local, weight, (((1,), (1,)), ((), ())), preferred_e...  7.24 us
    dot_general x1, matrix products, shards(): jnp.dot(normed, weight, preferred_element_type=f32).astype(bf16)  5.96 us
    dot_general x1, matrix products, shards(): lax.dot_general(feature_rows, portion, (((0,), (0,)), ((), ())), preferre...  5.19 us
  transfers between devices with their start and end apart: 10, of which 7 were waited for; matrix products, arithmetic and copies ran while one was open for 8% of the time, Pallas kernels for 0%

profile of v1, /device:TPU:1, one launch (start us, length us, event | category | flops | bytes accessed | tf_op | source)
XLA Modules:
  0.0 249.6 jit_solution(11550751290276575126)
XLA Ops:
  8.7 32.1 %all_to_all.40 = bf16[8,16,1536]{2,1,0:T(8,128)(2,1)S(1)} all-to-all(bf16[8,16,1536]{2,1,0:T(8,128)(2,1)S(1)} %broadcast_in_dim.14), channel_id=1, replica_groups=mesh['y'=4,'core'=2,'zh'=2,'x'=4,'gz'=8] {'gz'}, dimensions={0} | all-to-all | bytes 786432 | tf_op jit(solution)/shard_map/all_to_all | solution.py:28
  42.0 9.8 %all-to-all-start.1 = ((f32[8,2,128]{2,1,0:T(2,128)}), f32[8,2,128]{2,1,0:T(2,128)S(1)}, u32[]{:S(2)}, u32[]{:S(2)}) async-start(f32[8,2,128]{2,1,0:T(2,128)} %broadcast_in_dim.15), calls=%async_computation.1 | async-start | bytes 16384 | tf_op jit(solution)/shard_map/all_to_all | solution.py:28
  51.9 13.6 %all-to-all-done.1 = f32[8,2,128]{2,1,0:T(2,128)S(1)} async-done(((f32[8,2,128]{2,1,0:T(2,128)}), f32[8,2,128]{2,1,0:T(2,128)S(1)}, u32[]{:S(2)}, u32[]{:S(2)}) %all-to-all-start.1) | async-done | bytes 8224 | tf_op jit(solution)/shard_map/all_to_all | solution.py:28
  65.6 0.9 add_convert_fusion.1
  66.6 11.1 %all-gather.3.cloned.1.call-done = bf16[1536,3072]{1,0:T(8,128)(2,1)} async-done(((bf16[192,3072]{1,0:T(8,128)(2,1)}), bf16[1536,3072]{1,0:T(8,128)(2,1)}) %all-gather.3.cloned.1.call-update) | async-done | bytes 9437200 | tf_op jit(solution)/shard_map/all_gather | solution.py:54
  77.7 6.0 %convolution_convert_fusion.1 = bf16[128,3072]{1,0:T(8,128)(2,1)} fusion(bf16[128,1536]{1,0:T(8,128)(2,1)S(1)} %add_convert_fusion.1, bf16[1536,3072]{1,0:T(8,128)(2,1)} %all-gather.3.cloned.1.call-done), kind=kOutput, calls=%fused_computation.2 | convolution fusion | flops 1208352768 | bytes 10616832 | tf_op jit(solution)/shard_map/dot_general | solution.py:83
  83.7 4.0 %all-to-all-start.2 = ((bf16[4,32,3072]{2,1,0:T(8,128)(2,1)}), bf16[4,32,3072]{2,1,0:T(8,128)(2,1)S(1)}, u32[]{:S(2)}, u32[]{:S(2)}) async-start(bf16[4,32,3072]{2,1,0:T(8,128)(2,1)} %bitcast.10), calls=%async_computation.2 | async-start | bytes 1572864 | tf_op jit(solution)/shard_map/all_to_all | solution.py:28
  87.6 12.5 %collective-permute-start = (bf16[16,3072]{1,0:T(8,128)(2,1)S(1)}, bf16[16,3072]{1,0:T(8,128)(2,1)S(1)}, u32[]{:S(2)}, u32[]{:S(2)}) collective-permute-start(bf16[16,3072]{1,0:T(8,128)(2,1)S(1)} %copy-done.2), channel_id=1, source_target_pairs={{0,32},{32,0},{1,33},{33,1},{2,34},{34,2},{3,35},{35,3},{4,36},{36... | collective-permute-start | bytes 294920 | tf_op jit(solution)/shard_map/ppermute | solution.py:37
  100.3 11.8 %collective-permute-start.1 = (bf16[32,3072]{1,0:T(8,128)(2,1)S(1)}, bf16[32,3072]{1,0:T(8,128)(2,1)S(1)}, u32[]{:S(2)}, u32[]{:S(2)}) collective-permute-start(bf16[32,3072]{1,0:T(8,128)(2,1)S(1)} %reduce-precision_convert_fusion), channel_id=1, source_target_pairs={{0,32},{32,0},{1,33},{33,1},{2,34},{34,2},{3,35},{35,3},{4,36},{36... | collective-permute-start | bytes 589832 | tf_op jit(solution)/shard_map/ppermute | solution.py:37
  112.2 5.2 %collective-permute-done.1 = bf16[32,3072]{1,0:T(8,128)(2,1)S(1)} collective-permute-done((bf16[32,3072]{1,0:T(8,128)(2,1)S(1)}, bf16[32,3072]{1,0:T(8,128)(2,1)S(1)}, u32[]{:S(2)}, u32[]{:S(2)}) %collective-permute-start.1) | collective-permute-done | bytes 196640 | tf_op jit(solution)/shard_map/ppermute | solution.py:37
  117.8 28.4 %all_to_all.41 = bf16[4,32,3072]{2,1,0:T(8,128)(2,1)} all-to-all(bf16[4,32,3072]{2,1,0:T(8,128)(2,1)S(1)} %broadcast_in_dim.16), channel_id=1, replica_groups=mesh['y'=4,'core'=2,'zh'=2,'x'=4,'gz'=8] {'x'}, dimensions={0} | all-to-all | bytes 1572864 | tf_op jit(solution)/shard_map/all_to_all | solution.py:28
  146.3 7.2 %multiply_reduce_fusion = (f32[1536]{0:T(1024)S(1)}, f32[1536]{0:T(1024)S(1)}, bf16[128,1536]{1,0:T(8,128)(2,1)S(1)}) fusion(f32[4,2,16,1536]{3,2,1,0:T(8,128)S(1)} %copy.43, f32[128]{0:T(128)S(1)} %add_rsqrt_fusion, f32[128]{0:T(128)S(1)} %broadcast_multiply_fusion.1, bf16[128,3072]{1,0:T(8,128)(2,1)} %bitcast.57, ...), kind=kOutput, calls=%fused_computation.9 | convolution fusion | flops 1209136128 | bytes 11416576 | tf_op jit(solution)/shard_map/dot_general | solution.py:99
  153.8 0.9 pad_maximum_fusion
  154.6 7.2 %all-to-all-start.4 = ((bf16[8,24,1536]{2,1,0:T(8,128)(2,1)}), bf16[8,24,1536]{2,1,0:T(8,128)(2,1)S(1)}, u32[]{:S(2)}, u32[]{:S(2)}) async-start(bf16[8,24,1536]{2,1,0:T(8,128)(2,1)} %pad_maximum_fusion), calls=%async_computation.4 | async-start | bytes 1179648 | tf_op jit(solution)/shard_map/all_to_all | solution.py:28
  162.9 1.1 copy.48
  164.0 20.2 %all-to-all-done.4 = bf16[8,24,1536]{2,1,0:T(8,128)(2,1)S(1)} async-done(((bf16[8,24,1536]{2,1,0:T(8,128)(2,1)}), bf16[8,24,1536]{2,1,0:T(8,128)(2,1)S(1)}, u32[]{:S(2)}, u32[]{:S(2)}) %all-to-all-start.4) | async-done | bytes 589856 | tf_op jit(solution)/shard_map/all_to_all | solution.py:28
  185.1 5.9 %all-to-all-start.5 = ((f32[8,2,16]{2,1,0:T(2,128)}), f32[8,2,16]{2,1,0:T(2,128)S(1)}, u32[]{:S(2)}, u32[]{:S(2)}) async-start(f32[8,2,16]{2,1,0:T(2,128)} %broadcast_in_dim.19), calls=%async_computation.5 | async-start | bytes 16384 | tf_op jit(solution)/shard_map/all_to_all | solution.py:28
  191.1 13.7 %all-to-all-done.5 = f32[8,2,16]{2,1,0:T(2,128)S(1)} async-done(((f32[8,2,16]{2,1,0:T(2,128)}), f32[8,2,16]{2,1,0:T(2,128)S(1)}, u32[]{:S(2)}, u32[]{:S(2)}) %all-to-all-start.5) | async-done | bytes 1056 | tf_op jit(solution)/shard_map/all_to_all | solution.py:28
  205.5 14.8 %all-to-all-start.7 = ((f32[8,2,1536]{2,1,0:T(2,128)}), f32[8,2,1536]{2,1,0:T(2,128)S(1)}, u32[]{:S(2)}, u32[]{:S(2)}) async-start(f32[8,2,1536]{2,1,0:T(2,128)} %broadcast_in_dim.20), calls=%async_computation.7 | async-start | bytes 196608 | tf_op jit(solution)/shard_map/all_to_all | solution.py:28
  221.1 4.3 %all-to-all-done.7 = f32[8,2,1536]{2,1,0:T(2,128)S(1)} async-done(((f32[8,2,1536]{2,1,0:T(2,128)}), f32[8,2,1536]{2,1,0:T(2,128)S(1)}, u32[]{:S(2)}, u32[]{:S(2)}) %all-to-all-start.7) | async-done | bytes 98336 | tf_op jit(solution)/shard_map/all_to_all | solution.py:28
  225.3 4.2 %all-to-all-start.6 = ((bf16[8,128,192]{1,2,0:T(8,128)(2,1)}), bf16[8,128,192]{1,2,0:T(8,128)(2,1)S(1)}, u32[]{:S(2)}, u32[]{:S(2)}) async-start(bf16[8,128,192]{1,2,0:T(8,128)(2,1)} %copy.48), calls=%async_computation.6 | async-start | bytes 786432 | tf_op jit(solution)/shard_map/all_to_all | solution.py:28
  230.2 4.3 %convert_reduce_fusion = f32[3072]{0:T(1024)} fusion(bf16[1024,3072]{1,0:T(8,128)(2,1)} %all-gather.5.cloned.1.call-done), kind=kLoop, calls=%fused_computation | loop fusion | flops 6288384 | bytes 6303744 | tf_op jit(solution)/shard_map/reduce_sum | solution.py:97
  234.5 3.1 %all-to-all-done.6 = bf16[8,128,192]{1,2,0:T(8,128)(2,1)S(1)} async-done(((bf16[8,128,192]{1,2,0:T(8,128)(2,1)}), bf16[8,128,192]{1,2,0:T(8,128)(2,1)S(1)}, u32[]{:S(2)}, u32[]{:S(2)}) %all-to-all-start.6) | async-done | bytes 393248 | tf_op jit(solution)/shard_map/all_to_all | solution.py:28
  237.6 5.2 %convolution_convert_fusion = bf16[192,3072]{1,0:T(8,128)(2,1)} fusion(bf16[1024,3072]{1,0:T(8,128)(2,1)} %all-gather.5.cloned.1.call-done, bf16[8,128,192]{1,2,0:T(8,128)(2,1)S(1)} %all-to-all-done.6), kind=kOutput, calls=%fused_computation.1 | convolution fusion | flops 1208549376 | bytes 7864320 | tf_op jit(solution)/shard_map/dot_general | solution.py:94
  (68 shorter events, 7.7 us)
Async XLA Ops:
  7.2 70.5 %all-gather.3.cloned.1.call-start = ((), (), s32[]{:S(2)}) async-start(), calls=%async_computation.8 | async-start | bytes 10616832 | tf_op jit(solution)/shard_map/all_gather | solution.py:54
  42.0 23.5 %all-to-all-start.1 = ((f32[8,2,128]{2,1,0:T(2,128)}), f32[8,2,128]{2,1,0:T(2,128)S(1)}, u32[]{:S(2)}, u32[]{:S(2)}) async-start(f32[8,2,128]{2,1,0:T(2,128)} %broadcast_in_dim.15), calls=%async_computation.1 | async-start | bytes 16384 | tf_op jit(solution)/shard_map/all_to_all | solution.py:28
  66.6 21.1 %copy-start.2 = (bf16[16,3072]{1,0:T(8,128)(2,1)S(1)}, bf16[16,3072]{1,0:T(8,128)(2,1)}, u32[]{:S(2)}) copy-start(bf16[16,3072]{1,0:T(8,128)(2,1)} %param.11) | copy-start | bytes 294916
  66.6 50.8 %copy-start.4 = (f32[3072]{0:T(1024)S(1)}, f32[3072]{0:T(1024)}, u32[]{:S(2)}) copy-start(f32[3072]{0:T(1024)} %param.10) | copy-start | bytes 36868
  83.7 16.5 %all-to-all-start.2 = ((bf16[4,32,3072]{2,1,0:T(8,128)(2,1)}), bf16[4,32,3072]{2,1,0:T(8,128)(2,1)S(1)}, u32[]{:S(2)}, u32[]{:S(2)}) async-start(bf16[4,32,3072]{2,1,0:T(8,128)(2,1)} %bitcast.10), calls=%async_computation.2 | async-start | bytes 1572864 | tf_op jit(solution)/shard_map/all_to_all | solution.py:28
  87.6 142.6 %all-gather.5.cloned.1.call-start = ((), (), s32[]{:S(2)}) async-start(), calls=%async_computation.9 | async-start | bytes 7077888 | tf_op jit(solution)/shard_map/all_gather | solution.py:89
  87.6 24.5 %collective-permute-start = (bf16[16,3072]{1,0:T(8,128)(2,1)S(1)}, bf16[16,3072]{1,0:T(8,128)(2,1)S(1)}, u32[]{:S(2)}, u32[]{:S(2)}) collective-permute-start(bf16[16,3072]{1,0:T(8,128)(2,1)S(1)} %copy-done.2), channel_id=1, source_target_pairs={{0,32},{32,0},{1,33},{33,1},{2,34},{34,2},{3,35},{35,3},{4,36},{36... | collective-permute-start | bytes 294920 | tf_op jit(solution)/shard_map/ppermute | solution.py:37
  100.3 17.0 %collective-permute-start.1 = (bf16[32,3072]{1,0:T(8,128)(2,1)S(1)}, bf16[32,3072]{1,0:T(8,128)(2,1)S(1)}, u32[]{:S(2)}, u32[]{:S(2)}) collective-permute-start(bf16[32,3072]{1,0:T(8,128)(2,1)S(1)} %reduce-precision_convert_fusion), channel_id=1, source_target_pairs={{0,32},{32,0},{1,33},{33,1},{2,34},{34,2},{3,35},{35,3},{4,36},{36... | collective-permute-start | bytes 589832 | tf_op jit(solution)/shard_map/ppermute | solution.py:37
  146.3 15.5 %copy-start.3 = (f32[1536]{0:T(1024)S(1)}, f32[1536]{0:T(1024)}, u32[]{:S(2)}) copy-start(f32[1536]{0:T(1024)} %param.8) | copy-start | bytes 18436
  146.3 15.6 %copy-start.1 = (f32[1536]{0:T(1024)S(1)}, f32[1536]{0:T(1024)}, u32[]{:S(2)}) copy-start(f32[1536]{0:T(1024)} %param.7) | copy-start | bytes 18436
  153.6 30.7 %copy-start = (bf16[16,1536]{1,0:T(8,128)(2,1)S(1)}, bf16[16,1536]{1,0:T(8,128)(2,1)}, u32[]{:S(2)}) copy-start(bf16[16,1536]{1,0:T(8,128)(2,1)} %param.6) | copy-start | bytes 147460
  154.6 29.6 %all-to-all-start.4 = ((bf16[8,24,1536]{2,1,0:T(8,128)(2,1)}), bf16[8,24,1536]{2,1,0:T(8,128)(2,1)S(1)}, u32[]{:S(2)}, u32[]{:S(2)}) async-start(bf16[8,24,1536]{2,1,0:T(8,128)(2,1)} %pad_maximum_fusion), calls=%async_computation.4 | async-start | bytes 1179648 | tf_op jit(solution)/shard_map/all_to_all | solution.py:28
  185.1 19.7 %all-to-all-start.5 = ((f32[8,2,16]{2,1,0:T(2,128)}), f32[8,2,16]{2,1,0:T(2,128)S(1)}, u32[]{:S(2)}, u32[]{:S(2)}) async-start(f32[8,2,16]{2,1,0:T(2,128)} %broadcast_in_dim.19), calls=%async_computation.5 | async-start | bytes 16384 | tf_op jit(solution)/shard_map/all_to_all | solution.py:28
  205.5 19.8 %all-to-all-start.7 = ((f32[8,2,1536]{2,1,0:T(2,128)}), f32[8,2,1536]{2,1,0:T(2,128)S(1)}, u32[]{:S(2)}, u32[]{:S(2)}) async-start(f32[8,2,1536]{2,1,0:T(2,128)} %broadcast_in_dim.20), calls=%async_computation.7 | async-start | bytes 196608 | tf_op jit(solution)/shard_map/all_to_all | solution.py:28
  225.3 12.3 %all-to-all-start.6 = ((bf16[8,128,192]{1,2,0:T(8,128)(2,1)}), bf16[8,128,192]{1,2,0:T(8,128)(2,1)S(1)}, u32[]{:S(2)}, u32[]{:S(2)}) async-start(bf16[8,128,192]{1,2,0:T(8,128)(2,1)} %copy.48), calls=%async_computation.6 | async-start | bytes 786432 | tf_op jit(solution)/shard_map/all_to_all | solution.py:28
Sparse Core Ops, SparseCore 0:
  10.1 67.5 all-gather.2
  146.4 45.6 all-gather.4

commit v2 on v1

--- a/solution.py
+++ b/solution.py
@@ -37,11 +37,6 @@
     return lax.ppermute(block, "zh", [(0, 1), (1, 0)])
 
 
-def split_float(value):
-    high = lax.reduce_precision(value, 8, 7)
-    return high.astype(jnp.bfloat16), (value - high).astype(jnp.bfloat16)
-
-
 def shards(inputs, ln_gain, ln_bias, weight_in, up_bias, grad_hidden):
     f32, bf16 = jnp.float32, jnp.bfloat16
     rows, width = inputs.shape
@@ -63,6 +58,8 @@
     own_mean = jnp.mean(x_float, axis=1)
     own_centered = x_float - own_mean[:, None]
     own_square = jnp.sum(own_centered * own_centered, axis=1)
+    other_cotangent = swap(grad_hidden)
+    own_square = own_square + 0.0 * other_cotangent[0, 0].astype(f32)
     moments = spread(jnp.stack([own_mean, own_square]), gy)
     mean = jnp.mean(moments[:, 0], axis=0)
     shift = moments[:, 0] - mean
@@ -71,7 +68,6 @@
     x_hat = (x_float - mean[:, None]) * inv_std[:, None]
     normed = (x_hat * ln_gain + ln_bias).astype(bf16)
 
-    other_cotangent = swap(grad_hidden)
     upper = lax.axis_index("zh") == 1
     cotangent = jnp.concatenate(
         [
@@ -86,36 +82,44 @@
     hidden = half_sum + swap(half_sum.astype(bf16)).astype(f32) + up_bias
     grad_pre = (cotangent * gelu_slope(hidden)).astype(bf16)
     grad_local = spread(grad_pre, "x").reshape(local, hidden_width)
-    portion = lax.all_gather(grad_local, gx, axis=0, tiled=True)
 
-    feature_rows = exchange(
-        normed.reshape(local, width // sub_width, sub_width).transpose(1, 0, 2), gx
-    ).reshape(-1, sub_width)
-    grad_weight = lax.dot_general(
-        feature_rows, portion, (((0,), (0,)), ((), ())), preferred_element_type=f32
+    groups = lax.axis_size(gx)
+    all_normed = lax.all_gather(normed, gx, axis=0, tiled=True)
+    columns = exchange(
+        grad_local.reshape(local, groups, hidden_width // groups).transpose(1, 0, 2), gx
+    ).reshape(groups * local, hidden_width // groups)
+    block_weight = lax.dot_general(
+        all_normed, columns, (((0,), (0,)), ((), ())), preferred_element_type=f32
     ).astype(bf16)
-    grad_up_bias = jnp.sum(portion.astype(f32), axis=0)
+    grad_weight = (
+        exchange(block_weight.reshape(groups, sub_width, hidden_width // groups), gx)
+        .transpose(1, 0, 2)
+        .reshape(sub_width, hidden_width)
+    )
 
     back = lax.dot_general(
         grad_local, weight, (((1,), (1,)), ((), ())), preferred_element_type=f32
     )
-    sums = jnp.stack([jnp.sum(back * x_hat, axis=0), jnp.sum(back, axis=0)])
-    high, low = split_float(sums)
-    extra = jnp.concatenate([high, low, jnp.zeros((4, width), bf16)])
-    ordered = (
+    sums = jnp.concatenate(
+        [
+            jnp.sum(back * x_hat, axis=0),
+            jnp.sum(back, axis=0),
+            jnp.sum(grad_local.astype(f32), axis=0),
+        ]
+    )
+    sums = jnp.sum(spread(sums.reshape(-1, 128), gx), axis=0)
+    norm_rows = 2 * width // 128
+    grad_up_bias = sums[norm_rows:].reshape(hidden_width)
+    norm_sums = jnp.sum(spread(sums[:norm_rows], "gz"), axis=0).reshape(2, width)
+    grad_ln_gain, grad_ln_bias = norm_sums[0], norm_sums[1]
+    landed = exchange(
         back.astype(bf16)
         .reshape(around, halves, rows, width)
         .transpose(1, 0, 2, 3)
-        .reshape(depth, rows, width)
+        .reshape(depth, rows, width),
+        "gz",
     )
-    landed = exchange(
-        jnp.concatenate([ordered, jnp.broadcast_to(extra[None], (depth,) + extra.shape)], axis=1),
-        "gz",
-    ).astype(f32)
-    total = jnp.sum(landed, axis=0)
-    grad_float = total[:rows].astype(bf16).astype(f32)
-    depth_sums = total[rows : rows + 2] + total[rows + 2 : rows + 4]
-    grad_ln_gain, grad_ln_bias = jnp.sum(spread(depth_sums, gx), axis=0)
+    grad_float = jnp.sum(landed.astype(f32), axis=0).astype(bf16).astype(f32)
 
     def mine(value):
         ordered = value.reshape(around, halves, rows).transpose(1, 0, 2).reshape(depth, rows)

time: 251 us -> 277 us (1.10)
  waiting for transfers between devices: 72 us -> 109 us
  blocking collectives: 60.5 us -> 29.7 us
  starting transfers between devices: 70.3 us -> 93.5 us
  other arithmetic: 8.6 us -> 2.4 us
  local copies, waits for them, and re-layouts: 5.58 us -> 8.78 us
    all_to_all x6 -> x8, waiting for transfers between devices: 55 us -> 88.7 us  [exchange(): return lax.all_to_all(blocks, axis, split_axis=0, concat_axis=0, tiled=True)]
    all_to_all x2, blocking collectives: 60.5 us -> 29.7 us  [exchange(): return lax.all_to_all(blocks, axis, split_axis=0, concat_axis=0, tiled=True)]
    all_to_all x6 -> x8, starting transfers between devices: 45.9 us -> 69.7 us  [exchange(): return lax.all_to_all(blocks, axis, split_axis=0, concat_axis=0, tiled=True)]
    ppermute x2, waiting for transfers between devices: 5.17 us -> 11.4 us  [swap(): return lax.ppermute(block, 'zh', [(0, 1), (1, 0)])]
    reduce_sum x3 -> x4, other arithmetic: 4.42 us -> 0.21 us  [the longest x1 0.13 us: shards(): jnp.sum(grad_local.astype(f32), axis=0)]
    all_gather x1, waiting for transfers between devices: 11.1 us -> 7.53 us  [shards(): weight = lax.all_gather(weight_in, gx, axis=0, tiled=True)]
  transfers between devices with their start and end apart: 10 -> 12, of which waited for: 7 -> 11; matrix products, arithmetic and copies ran while one was open for 8% -> 8% of each run, Pallas kernels for 0% -> 0%
where the time goes in v2:
time: 277 us; the launch traced here: 276 us
  waiting for transfers between devices  109 us (39%)
  starting transfers between devices  93.5 us (34%)
  blocking collectives  29.7 us (11%)
  matrix products  17.8 us (6%)
  between operations  14.9 us (5%)
  local copies, waits for them, and re-layouts  8.78 us (3%)
    all_to_all x8, waiting for transfers between devices, exchange(): return lax.all_to_all(blocks, axis, split_axis=0, concat_axis=0, tiled=True)  88.7 us
    all_to_all x8, starting transfers between devices, exchange(): return lax.all_to_all(blocks, axis, split_axis=0, concat_axis=0, tiled=True)  69.7 us
    all_to_all x2, blocking collectives, exchange(): return lax.all_to_all(blocks, axis, split_axis=0, concat_axis=0, tiled=True)  29.7 us
    ppermute x2, starting transfers between devices, swap(): return lax.ppermute(block, 'zh', [(0, 1), (1, 0)])  23.8 us
    ppermute x2, waiting for transfers between devices, swap(): return lax.ppermute(block, 'zh', [(0, 1), (1, 0)])  11.4 us
    all_gather x1, waiting for transfers between devices, shards(): weight = lax.all_gather(weight_in, gx, axis=0, tiled=True)  7.53 us
    dot_general x1, matrix products, shards(): lax.dot_general(grad_local, weight, (((1,), (1,)), ((), ())), preferred_e...  6.95 us
    dot_general x1, matrix products, shards(): jnp.dot(normed, weight, preferred_element_type=f32).astype(bf16)  6.12 us
  transfers between devices with their start and end apart: 12, of which 11 were waited for; matrix products, arithmetic and copies ran while one was open for 8% of the time, Pallas kernels for 0%

profile of v2, /device:TPU:1, one launch (start us, length us, event | category | flops | bytes accessed | tf_op | source)
XLA Modules:
  0.0 276.3 jit_solution(114541061159650377)
XLA Ops:
  9.5 13.1 %all-to-all-start = ((bf16[8,16,1536]{2,1,0:T(8,128)(2,1)}), bf16[8,16,1536]{2,1,0:T(8,128)(2,1)S(1)}, u32[]{:S(2)}, u32[]{:S(2)}) async-start(bf16[8,16,1536]{2,1,0:T(8,128)(2,1)} %broadcast_in_dim.14), calls=%async_computation | async-start | bytes 786432 | tf_op jit(solution)/shard_map/all_to_all | solution.py:28
  22.6 7.9 %collective-permute-start = (bf16[16,3072]{1,0:T(8,128)(2,1)}, bf16[16,3072]{1,0:T(8,128)(2,1)S(1)}, u32[]{:S(2)}, u32[]{:S(2)}) collective-permute-start(bf16[16,3072]{1,0:T(8,128)(2,1)} %param.11), channel_id=1, source_target_pairs={{0,32},{32,0},{1,33},{33,1},{2,34},{34,2},{3,35},{35,3},{4,36},{36... | collective-permute-start | bytes 294920 | tf_op jit(solution)/shard_map/ppermute | solution.py:37
  30.5 7.7 %collective-permute-done = bf16[16,3072]{1,0:T(8,128)(2,1)S(1)} collective-permute-done((bf16[16,3072]{1,0:T(8,128)(2,1)}, bf16[16,3072]{1,0:T(8,128)(2,1)S(1)}, u32[]{:S(2)}, u32[]{:S(2)}) %collective-permute-start) | collective-permute-done | bytes 98336 | tf_op jit(solution)/shard_map/ppermute | solution.py:37
  39.3 5.8 %all-to-all-done = bf16[8,16,1536]{2,1,0:T(8,128)(2,1)S(1)} async-done(((bf16[8,16,1536]{2,1,0:T(8,128)(2,1)}), bf16[8,16,1536]{2,1,0:T(8,128)(2,1)S(1)}, u32[]{:S(2)}, u32[]{:S(2)}) %all-to-all-start) | async-done | bytes 393248 | tf_op jit(solution)/shard_map/all_to_all | solution.py:28
  46.3 9.8 %all-to-all-start.1 = ((f32[8,2,128]{2,1,0:T(2,128)}), f32[8,2,128]{2,1,0:T(2,128)S(1)}, u32[]{:S(2)}, u32[]{:S(2)}) async-start(f32[8,2,128]{2,1,0:T(2,128)} %broadcast_in_dim.15), calls=%async_computation.1 | async-start | bytes 16384 | tf_op jit(solution)/shard_map/all_to_all | solution.py:28
  56.3 13.6 %all-to-all-done.1 = f32[8,2,128]{2,1,0:T(2,128)S(1)} async-done(((f32[8,2,128]{2,1,0:T(2,128)}), f32[8,2,128]{2,1,0:T(2,128)S(1)}, u32[]{:S(2)}, u32[]{:S(2)}) %all-to-all-start.1) | async-done | bytes 8224 | tf_op jit(solution)/shard_map/all_to_all | solution.py:28
  70.2 7.5 %all-gather.3.cloned.1.call-done = bf16[1536,3072]{1,0:T(8,128)(2,1)} async-done(((bf16[192,3072]{1,0:T(8,128)(2,1)}), bf16[1536,3072]{1,0:T(8,128)(2,1)}) %all-gather.3.cloned.1.call-update) | async-done | bytes 9437200 | tf_op jit(solution)/shard_map/all_gather | solution.py:49
  77.7 6.1 %convolution_convert_fusion = bf16[128,3072]{1,0:T(8,128)(2,1)} fusion(bf16[128,1536]{1,0:T(8,128)(2,1)S(1)} %add_convert_fusion, bf16[1536,3072]{1,0:T(8,128)(2,1)} %all-gather.3.cloned.1.call-done), kind=kOutput, calls=%fused_computation | convolution fusion | flops 1208352768 | bytes 10616832 | tf_op jit(solution)/shard_map/dot_general | solution.py:79
  88.7 7.8 %all-to-all-done.2 = bf16[4,32,3072]{2,1,0:T(8,128)(2,1)S(1)} async-done(((bf16[4,32,3072]{2,1,0:T(8,128)(2,1)}), bf16[4,32,3072]{2,1,0:T(8,128)(2,1)S(1)}, u32[]{:S(2)}, u32[]{:S(2)}) %all-to-all-start.2) | async-done | bytes 786464 | tf_op jit(solution)/shard_map/all_to_all | solution.py:28
  96.6 15.8 %collective-permute-start.1 = (bf16[32,3072]{1,0:T(8,128)(2,1)S(1)}, bf16[32,3072]{1,0:T(8,128)(2,1)S(1)}, u32[]{:S(2)}, u32[]{:S(2)}) collective-permute-start(bf16[32,3072]{1,0:T(8,128)(2,1)S(1)} %reduce-precision_convert_fusion), channel_id=1, source_target_pairs={{0,32},{32,0},{1,33},{33,1},{2,34},{34,2},{3,35},{35,3},{4,36},{36... | collective-permute-start | bytes 589832 | tf_op jit(solution)/shard_map/ppermute | solution.py:37
  116.7 10.7 %all_to_all.50 = bf16[4,32,3072]{2,1,0:T(8,128)(2,1)S(1)} all-to-all(bf16[4,32,3072]{2,1,0:T(8,128)(2,1)S(1)} %broadcast_in_dim.16), channel_id=1, replica_groups=mesh['y'=4,'core'=2,'zh'=2,'x'=4,'gz'=8] {'x'}, dimensions={0} | all-to-all | bytes 1572864 | tf_op jit(solution)/shard_map/all_to_all | solution.py:28
  127.6 6.9 %multiply_reduce_fusion = (f32[1536]{0:T(1024)S(1)}, f32[1536]{0:T(1024)S(1)}, bf16[128,1536]{1,0:T(8,128)(2,1)S(1)}) fusion(f32[4,2,16,1536]{3,2,1,0:T(8,128)S(1)} %copy.48, f32[128]{0:T(128)S(1)} %add_rsqrt_fusion, f32[128]{0:T(128)S(1)} %broadcast_multiply_fusion.1, bf16[128,3072]{1,0:T(8,128)(2,1)S(1)} %bitcast.67, ...), kind=kOutput, calls=%fused_computation.7 | convolution fusion | flops 1209136128 | bytes 11416576 | tf_op jit(solution)/shard_map/dot_general | solution.py:100
  134.6 19.0 %all_to_all.51 = f32[8,48,128]{2,1,0:T(8,128)S(1)} all-to-all(f32[8,48,128]{2,1,0:T(8,128)S(1)} %broadcast_in_dim.19), channel_id=1, replica_groups=mesh['y'=4,'core'=2,'zh'=2,'x'=4,'gz'=8] {'y','core'}, dimensions={0} | all-to-all | bytes 393216 | tf_op jit(solution)/shard_map/all_to_all | solution.py:28
  154.9 15.5 %all-to-all-start.9 = ((f32[8,24,128]{2,1,0:T(8,128)}), f32[8,24,128]{2,1,0:T(8,128)S(1)}, u32[]{:S(2)}, u32[]{:S(2)}) async-start(f32[8,24,128]{2,1,0:T(8,128)} %broadcast_in_dim.20), calls=%async_computation.9 | async-start | bytes 196608 | tf_op jit(solution)/shard_map/all_to_all | solution.py:28
  171.2 9.3 %all-to-all-done.9 = f32[8,24,128]{2,1,0:T(8,128)S(1)} async-done(((f32[8,24,128]{2,1,0:T(8,128)}), f32[8,24,128]{2,1,0:T(8,128)S(1)}, u32[]{:S(2)}, u32[]{:S(2)}) %all-to-all-start.9) | async-done | bytes 98336 | tf_op jit(solution)/shard_map/all_to_all | solution.py:28
  180.4 4.5 %all-to-all-start.4 = ((bf16[8,16,1536]{2,1,0:T(8,128)(2,1)}), bf16[8,16,1536]{2,1,0:T(8,128)(2,1)S(1)}, u32[]{:S(2)}, u32[]{:S(2)}) async-start(bf16[8,16,1536]{2,1,0:T(8,128)(2,1)} %bitcast.15), calls=%async_computation.4 | async-start | bytes 786432 | tf_op jit(solution)/shard_map/all_to_all | solution.py:28
  186.1 16.2 %all-to-all-done.4 = bf16[8,16,1536]{2,1,0:T(8,128)(2,1)S(1)} async-done(((bf16[8,16,1536]{2,1,0:T(8,128)(2,1)}), bf16[8,16,1536]{2,1,0:T(8,128)(2,1)S(1)}, u32[]{:S(2)}, u32[]{:S(2)}) %all-to-all-start.4) | async-done | bytes 393248 | tf_op jit(solution)/shard_map/all_to_all | solution.py:28
  202.3 10.2 %all-to-all-start.6 = ((bf16[8,128,384]{2,1,0:T(8,128)(2,1)}), bf16[8,128,384]{2,1,0:T(8,128)(2,1)S(1)}, u32[]{:S(2)}, u32[]{:S(2)}) async-start(bf16[8,128,384]{2,1,0:T(8,128)(2,1)} %copy.52), calls=%async_computation.6 | async-start | bytes 1572864 | tf_op jit(solution)/shard_map/all_to_all | solution.py:28
  213.0 11.8 %all-to-all-done.6 = bf16[8,128,384]{2,1,0:T(8,128)(2,1)S(1)} async-done(((bf16[8,128,384]{2,1,0:T(8,128)(2,1)}), bf16[8,128,384]{2,1,0:T(8,128)(2,1)S(1)}, u32[]{:S(2)}, u32[]{:S(2)}) %all-to-all-start.6) | async-done | bytes 786464 | tf_op jit(solution)/shard_map/all_to_all | solution.py:28
  225.4 6.8 %all-to-all-start.5 = ((f32[8,2,16]{2,1,0:T(2,128)}), f32[8,2,16]{2,1,0:T(2,128)S(1)}, u32[]{:S(2)}, u32[]{:S(2)}) async-start(f32[8,2,16]{2,1,0:T(2,128)} %broadcast_in_dim.17), calls=%async_computation.5 | async-start | bytes 16384 | tf_op jit(solution)/shard_map/all_to_all | solution.py:28
  232.2 4.7 %convolution_convert_fusion.1 = bf16[1536,384]{1,0:T(8,128)(2,1)} fusion(bf16[1024,1536]{1,0:T(8,128)(2,1)} %all-gather.5.cloned.1.call-done, bf16[1024,384]{1,0:T(8,128)(2,1)S(1)} %bitcast.75), kind=kOutput, calls=%fused_computation.1 | convolution fusion | flops 1208549376 | bytes 5111808 | tf_op jit(solution)/shard_map/dot_general | solution.py:91
  236.9 9.0 %all-to-all-done.5 = f32[8,2,16]{2,1,0:T(2,128)S(1)} async-done(((f32[8,2,16]{2,1,0:T(2,128)}), f32[8,2,16]{2,1,0:T(2,128)S(1)}, u32[]{:S(2)}, u32[]{:S(2)}) %all-to-all-start.5) | async-done | bytes 1056 | tf_op jit(solution)/shard_map/all_to_all | solution.py:28
  245.9 5.8 %all-to-all-start.7 = ((bf16[8,192,384]{2,1,0:T(8,128)(2,1)}), bf16[8,192,384]{2,1,0:T(8,128)(2,1)S(1)}, u32[]{:S(2)}, u32[]{:S(2)}) async-start(bf16[8,192,384]{2,1,0:T(8,128)(2,1)} %bitcast.25), calls=%async_computation.7 | async-start | bytes 2359296 | tf_op jit(solution)/shard_map/all_to_all | solution.py:28
  253.0 15.2 %all-to-all-done.7 = bf16[8,192,384]{2,1,0:T(8,128)(2,1)S(1)} async-done(((bf16[8,192,384]{2,1,0:T(8,128)(2,1)}), bf16[8,192,384]{2,1,0:T(8,128)(2,1)S(1)}, u32[]{:S(2)}, u32[]{:S(2)}) %all-to-all-start.7) | async-done | bytes 1179680 | tf_op jit(solution)/shard_map/all_to_all | solution.py:28
  (69 shorter events, 20.5 us)
Async XLA Ops:
  7.2 62.8 %copy-start.3 = (f32[1536]{0:T(1024)S(1)}, f32[1536]{0:T(1024)}, u32[]{:S(2)}) copy-start(f32[1536]{0:T(1024)} %param.7) | copy-start | bytes 18436
  7.2 62.8 %copy-start.5 = (f32[1536]{0:T(1024)S(1)}, f32[1536]{0:T(1024)}, u32[]{:S(2)}) copy-start(f32[1536]{0:T(1024)} %param.8) | copy-start | bytes 18436
  7.2 70.5 %all-gather.3.cloned.1.call-start = ((), (), s32[]{:S(2)}) async-start(), calls=%async_computation.10 | async-start | bytes 10616832 | tf_op jit(solution)/shard_map/all_gather | solution.py:49
  9.5 35.6 %all-to-all-start = ((bf16[8,16,1536]{2,1,0:T(8,128)(2,1)}), bf16[8,16,1536]{2,1,0:T(8,128)(2,1)S(1)}, u32[]{:S(2)}, u32[]{:S(2)}) async-start(bf16[8,16,1536]{2,1,0:T(8,128)(2,1)} %broadcast_in_dim.14), calls=%async_computation | async-start | bytes 786432 | tf_op jit(solution)/shard_map/all_to_all | solution.py:28
  22.6 15.6 %collective-permute-start = (bf16[16,3072]{1,0:T(8,128)(2,1)}, bf16[16,3072]{1,0:T(8,128)(2,1)S(1)}, u32[]{:S(2)}, u32[]{:S(2)}) collective-permute-start(bf16[16,3072]{1,0:T(8,128)(2,1)} %param.11), channel_id=1, source_target_pairs={{0,32},{32,0},{1,33},{33,1},{2,34},{34,2},{3,35},{35,3},{4,36},{36... | collective-permute-start | bytes 294920 | tf_op jit(solution)/shard_map/ppermute | solution.py:37
  46.3 23.5 %all-to-all-start.1 = ((f32[8,2,128]{2,1,0:T(2,128)}), f32[8,2,128]{2,1,0:T(2,128)S(1)}, u32[]{:S(2)}, u32[]{:S(2)}) async-start(f32[8,2,128]{2,1,0:T(2,128)} %broadcast_in_dim.15), calls=%async_computation.1 | async-start | bytes 16384 | tf_op jit(solution)/shard_map/all_to_all | solution.py:28
  70.2 13.7 %copy-start = (bf16[128,1536]{1,0:T(8,128)(2,1)}, bf16[128,1536]{1,0:T(8,128)(2,1)S(1)}, u32[]{:S(2)}) copy-start(bf16[128,1536]{1,0:T(8,128)(2,1)S(1)} %add_convert_fusion) | copy-start | bytes 1179652
  83.9 28.7 %copy-start.2 = (bf16[16,3072]{1,0:T(8,128)(2,1)S(1)}, bf16[16,3072]{1,0:T(8,128)(2,1)}, u32[]{:S(2)}) copy-start(bf16[16,3072]{1,0:T(8,128)(2,1)} %param.11) | copy-start | bytes 294916
  83.9 32.5 %copy-start.4 = (f32[3072]{0:T(1024)S(1)}, f32[3072]{0:T(1024)}, u32[]{:S(2)}) copy-start(f32[3072]{0:T(1024)} %param.10) | copy-start | bytes 36868
  83.9 12.6 %all-to-all-start.2 = ((bf16[4,32,3072]{2,1,0:T(8,128)(2,1)}), bf16[4,32,3072]{2,1,0:T(8,128)(2,1)S(1)}, u32[]{:S(2)}, u32[]{:S(2)}) async-start(bf16[4,32,3072]{2,1,0:T(8,128)(2,1)} %bitcast.11), calls=%async_computation.2 | async-start | bytes 1572864 | tf_op jit(solution)/shard_map/all_to_all | solution.py:28
  88.0 144.2 %all-gather.5.cloned.1.call-start = ((), (), s32[]{:S(2)}) async-start(), calls=%async_computation.11 | async-start | bytes 3538944 | tf_op jit(solution)/shard_map/all_gather | solution.py:87
  96.6 19.7 %collective-permute-start.1 = (bf16[32,3072]{1,0:T(8,128)(2,1)S(1)}, bf16[32,3072]{1,0:T(8,128)(2,1)S(1)}, u32[]{:S(2)}, u32[]{:S(2)}) collective-permute-start(bf16[32,3072]{1,0:T(8,128)(2,1)S(1)} %reduce-precision_convert_fusion), channel_id=1, source_target_pairs={{0,32},{32,0},{1,33},{33,1},{2,34},{34,2},{3,35},{35,3},{4,36},{36... | collective-permute-start | bytes 589832 | tf_op jit(solution)/shard_map/ppermute | solution.py:37
  154.9 25.5 %all-to-all-start.9 = ((f32[8,24,128]{2,1,0:T(8,128)}), f32[8,24,128]{2,1,0:T(8,128)S(1)}, u32[]{:S(2)}, u32[]{:S(2)}) async-start(f32[8,24,128]{2,1,0:T(8,128)} %broadcast_in_dim.20), calls=%async_computation.9 | async-start | bytes 196608 | tf_op jit(solution)/shard_map/all_to_all | solution.py:28
  171.2 41.6 %copy-start.1 = (bf16[16,1536]{1,0:T(8,128)(2,1)S(1)}, bf16[16,1536]{1,0:T(8,128)(2,1)}, u32[]{:S(2)}) copy-start(bf16[16,1536]{1,0:T(8,128)(2,1)} %param.6) | copy-start | bytes 147460
  180.4 21.9 %all-to-all-start.4 = ((bf16[8,16,1536]{2,1,0:T(8,128)(2,1)}), bf16[8,16,1536]{2,1,0:T(8,128)(2,1)S(1)}, u32[]{:S(2)}, u32[]{:S(2)}) async-start(bf16[8,16,1536]{2,1,0:T(8,128)(2,1)} %bitcast.15), calls=%async_computation.4 | async-start | bytes 786432 | tf_op jit(solution)/shard_map/all_to_all | solution.py:28
  202.3 22.5 %all-to-all-start.6 = ((bf16[8,128,384]{2,1,0:T(8,128)(2,1)}), bf16[8,128,384]{2,1,0:T(8,128)(2,1)S(1)}, u32[]{:S(2)}, u32[]{:S(2)}) async-start(bf16[8,128,384]{2,1,0:T(8,128)(2,1)} %copy.52), calls=%async_computation.6 | async-start | bytes 1572864 | tf_op jit(solution)/shard_map/all_to_all | solution.py:28
  225.4 20.5 %all-to-all-start.5 = ((f32[8,2,16]{2,1,0:T(2,128)}), f32[8,2,16]{2,1,0:T(2,128)S(1)}, u32[]{:S(2)}, u32[]{:S(2)}) async-start(f32[8,2,16]{2,1,0:T(2,128)} %broadcast_in_dim.17), calls=%async_computation.5 | async-start | bytes 16384 | tf_op jit(solution)/shard_map/all_to_all | solution.py:28
  245.9 22.3 %all-to-all-start.7 = ((bf16[8,192,384]{2,1,0:T(8,128)(2,1)}), bf16[8,192,384]{2,1,0:T(8,128)(2,1)S(1)}, u32[]{:S(2)}, u32[]{:S(2)}) async-start(bf16[8,192,384]{2,1,0:T(8,128)(2,1)} %bitcast.25), calls=%async_computation.7 | async-start | bytes 2359296 | tf_op jit(solution)/shard_map/all_to_all | solution.py:28
Sparse Core Ops, SparseCore 0:
  10.1 67.5 all-gather.2
  90.9 36.5 all-gather.4

commit v3 on v1

--- a/solution.py
+++ b/solution.py
@@ -37,11 +37,6 @@
     return lax.ppermute(block, "zh", [(0, 1), (1, 0)])
 
 
-def split_float(value):
-    high = lax.reduce_precision(value, 8, 7)
-    return high.astype(jnp.bfloat16), (value - high).astype(jnp.bfloat16)
-
-
 def shards(inputs, ln_gain, ln_bias, weight_in, up_bias, grad_hidden):
     f32, bf16 = jnp.float32, jnp.bfloat16
     rows, width = inputs.shape
@@ -63,6 +58,8 @@
     own_mean = jnp.mean(x_float, axis=1)
     own_centered = x_float - own_mean[:, None]
     own_square = jnp.sum(own_centered * own_centered, axis=1)
+    other_cotangent = swap(grad_hidden)
+    own_square = own_square + 0.0 * other_cotangent[0, 0].astype(f32)
     moments = spread(jnp.stack([own_mean, own_square]), gy)
     mean = jnp.mean(moments[:, 0], axis=0)
     shift = moments[:, 0] - mean
@@ -71,7 +68,6 @@
     x_hat = (x_float - mean[:, None]) * inv_std[:, None]
     normed = (x_hat * ln_gain + ln_bias).astype(bf16)
 
-    other_cotangent = swap(grad_hidden)
     upper = lax.axis_index("zh") == 1
     cotangent = jnp.concatenate(
         [
@@ -86,22 +82,17 @@
     hidden = half_sum + swap(half_sum.astype(bf16)).astype(f32) + up_bias
     grad_pre = (cotangent * gelu_slope(hidden)).astype(bf16)
     grad_local = spread(grad_pre, "x").reshape(local, hidden_width)
+
+    all_normed = lax.all_gather(normed, gx, axis=0, tiled=True)
     portion = lax.all_gather(grad_local, gx, axis=0, tiled=True)
-
-    feature_rows = exchange(
-        normed.reshape(local, width // sub_width, sub_width).transpose(1, 0, 2), gx
-    ).reshape(-1, sub_width)
-    grad_weight = lax.dot_general(
-        feature_rows, portion, (((0,), (0,)), ((), ())), preferred_element_type=f32
-    ).astype(bf16)
-    grad_up_bias = jnp.sum(portion.astype(f32), axis=0)
 
     back = lax.dot_general(
         grad_local, weight, (((1,), (1,)), ((), ())), preferred_element_type=f32
     )
-    sums = jnp.stack([jnp.sum(back * x_hat, axis=0), jnp.sum(back, axis=0)])
-    high, low = split_float(sums)
-    extra = jnp.concatenate([high, low, jnp.zeros((4, width), bf16)])
+    sums = jnp.stack([jnp.sum(back * x_hat, axis=0), jnp.sum(back, axis=0)]).astype(bf16)
+    packed = 2 * width // rows
+    padding = -packed % 128
+    extra = jnp.pad(sums.reshape(rows, packed), ((0, 0), (0, padding)))
     ordered = (
         back.astype(bf16)
         .reshape(around, halves, rows, width)
@@ -109,13 +100,23 @@
         .reshape(depth, rows, width)
     )
     landed = exchange(
-        jnp.concatenate([ordered, jnp.broadcast_to(extra[None], (depth,) + extra.shape)], axis=1),
+        jnp.concatenate([ordered, jnp.broadcast_to(extra[None], (depth,) + extra.shape)], axis=2),
         "gz",
-    ).astype(f32)
-    total = jnp.sum(landed, axis=0)
-    grad_float = total[:rows].astype(bf16).astype(f32)
-    depth_sums = total[rows : rows + 2] + total[rows + 2 : rows + 4]
-    grad_ln_gain, grad_ln_bias = jnp.sum(spread(depth_sums, gx), axis=0)
+    )
+    total = jnp.sum(landed.astype(f32), axis=0)
+    grad_float = total[:, :width].astype(bf16).astype(f32)
+    small = jnp.concatenate(
+        [
+            total[:, width : width + packed].reshape(2 * width),
+            jnp.sum(grad_local.astype(f32), axis=0),
+        ]
+    ).reshape(-1, 128)
+    small = small + lax.ppermute(small, "core", [(0, 1), (1, 0)])
+    small = small + lax.ppermute(small, "y", [(0, 1), (1, 0), (2, 3), (3, 2)])
+    small = small + lax.ppermute(small, "y", [(0, 3), (3, 0), (1, 2), (2, 1)])
+    small = small.reshape(-1)
+    grad_ln_gain, grad_ln_bias = small[:width], small[width : 2 * width]
+    grad_up_bias = small[2 * width :]
 
     def mine(value):
         ordered = value.reshape(around, halves, rows).transpose(1, 0, 2).reshape(depth, rows)
@@ -128,6 +129,12 @@
     first_total, second_total = jnp.sum(spread(token_sums, gy), axis=0)
     grad_inputs = (
         own_inv * (scaled - first_total[:, None] / D - own_hat * (second_total[:, None] / D))
+    ).astype(bf16)
+    feature_rows = lax.dynamic_slice_in_dim(
+        all_normed, lax.axis_index(gx) * sub_width, sub_width, axis=1
+    )
+    grad_weight = lax.dot_general(
+        feature_rows, portion, (((0,), (0,)), ((), ())), preferred_element_type=f32
     ).astype(bf16)
     return (grad_inputs, grad_weight, grad_up_bias, grad_ln_gain, grad_ln_bias)
 

time: 251 us -> 237 us (0.944)
  blocking collectives: 60.5 us -> 11.5 us
  starting transfers between devices: 70.3 us -> 96.7 us
  waiting for transfers between devices: 72 us -> 82.9 us
  other arithmetic: 8.6 us -> 4.67 us
    all_to_all x2 -> x1, blocking collectives: 60.5 us -> 11.5 us  [exchange(): return lax.all_to_all(blocks, axis, split_axis=0, concat_axis=0, tiled=True)]
    ppermute x0 -> x3, starting transfers between devices: none -> 14.3 us  [the longest x1 9.75 us: shards(): small = small + lax.ppermute(small, 'core', [(0, 1), (1, 0)])]
    all_to_all x6 -> x5, starting transfers between devices: 45.9 us -> 58.4 us  [exchange(): return lax.all_to_all(blocks, axis, split_axis=0, concat_axis=0, tiled=True)]
    ppermute x2, waiting for transfers between devices: 5.17 us -> 11 us  [swap(): return lax.ppermute(block, 'zh', [(0, 1), (1, 0)])]
    all_to_all x6 -> x5, waiting for transfers between devices: 55 us -> 60.1 us  [exchange(): return lax.all_to_all(blocks, axis, split_axis=0, concat_axis=0, tiled=True)]
    all_gather x1, waiting for transfers between devices: 11.1 us -> 6.05 us  [shards(): weight = lax.all_gather(weight_in, gx, axis=0, tiled=True)]
    ppermute x0 -> x3, waiting for transfers between devices: none -> 5.07 us  [the longest x1 2.63 us: shards(): small = small + lax.ppermute(small, 'y', [(0, 1), (1, 0), (2, 3), (3, 2)])]
    reduce_sum x3 -> x2, other arithmetic: 4.42 us -> 0.19 us  [the longest x1 0.13 us: shards(): jnp.sum(grad_local.astype(f32), axis=0)]
  transfers between devices with their start and end apart: 10 -> 13, of which waited for: 7 -> 10; matrix products, arithmetic and copies ran while one was open for 8% -> 10% of each run, Pallas kernels for 0% -> 0%
where the time goes in v3:
time: 237 us; the launch traced here: 235 us
  starting transfers between devices  96.7 us (41%)
  waiting for transfers between devices  82.9 us (35%)
  matrix products  19 us (8%)
  between operations  14.7 us (6%)
  blocking collectives  11.5 us (5%)
  local copies, waits for them, and re-layouts  5.26 us (2%)
  other arithmetic  4.67 us (2%)
    all_to_all x5, waiting for transfers between devices, exchange(): return lax.all_to_all(blocks, axis, split_axis=0, concat_axis=0, tiled=True)  60.1 us
    all_to_all x5, starting transfers between devices, exchange(): return lax.all_to_all(blocks, axis, split_axis=0, concat_axis=0, tiled=True)  58.4 us
    ppermute x2, starting transfers between devices, swap(): return lax.ppermute(block, 'zh', [(0, 1), (1, 0)])  24 us
    all_to_all x1, blocking collectives, exchange(): return lax.all_to_all(blocks, axis, split_axis=0, concat_axis=0, tiled=True)  11.5 us
    ppermute x2, waiting for transfers between devices, swap(): return lax.ppermute(block, 'zh', [(0, 1), (1, 0)])  11 us
    ppermute x1, starting transfers between devices, shards(): small = small + lax.ppermute(small, 'core', [(0, 1), (1, 0)])  9.75 us
    dot_general x1, matrix products, shards(): lax.dot_general(grad_local, weight, (((1,), (1,)), ((), ())), preferred_e...  7.28 us
    dot_general x1, matrix products, shards(): jnp.dot(normed, weight, preferred_element_type=f32).astype(bf16)  6.1 us
  transfers between devices with their start and end apart: 13, of which 10 were waited for; matrix products, arithmetic and copies ran while one was open for 10% of the time, Pallas kernels for 0%

profile of v3, /device:TPU:1, one launch (start us, length us, event | category | flops | bytes accessed | tf_op | source)
XLA Modules:
  0.0 234.7 jit_solution(13600598920928755167)
XLA Ops:
  9.5 13.1 %all-to-all-start = ((bf16[8,16,1536]{2,1,0:T(8,128)(2,1)}), bf16[8,16,1536]{2,1,0:T(8,128)(2,1)S(1)}, u32[]{:S(2)}, u32[]{:S(2)}) async-start(bf16[8,16,1536]{2,1,0:T(8,128)(2,1)} %broadcast_in_dim.10), calls=%async_computation | async-start | bytes 786432 | tf_op jit(solution)/shard_map/all_to_all | solution.py:28
  22.5 7.9 %collective-permute-start = (bf16[16,3072]{1,0:T(8,128)(2,1)}, bf16[16,3072]{1,0:T(8,128)(2,1)S(1)}, u32[]{:S(2)}, u32[]{:S(2)}) collective-permute-start(bf16[16,3072]{1,0:T(8,128)(2,1)} %param.11), channel_id=1, source_target_pairs={{0,32},{32,0},{1,33},{33,1},{2,34},{34,2},{3,35},{35,3},{4,36},{36... | collective-permute-start | bytes 294920 | tf_op jit(solution)/shard_map/ppermute | solution.py:37
  30.5 7.7 %collective-permute-done = bf16[16,3072]{1,0:T(8,128)(2,1)S(1)} collective-permute-done((bf16[16,3072]{1,0:T(8,128)(2,1)}, bf16[16,3072]{1,0:T(8,128)(2,1)S(1)}, u32[]{:S(2)}, u32[]{:S(2)}) %collective-permute-start) | collective-permute-done | bytes 98336 | tf_op jit(solution)/shard_map/ppermute | solution.py:37
  39.3 5.8 %all-to-all-done = bf16[8,16,1536]{2,1,0:T(8,128)(2,1)S(1)} async-done(((bf16[8,16,1536]{2,1,0:T(8,128)(2,1)}), bf16[8,16,1536]{2,1,0:T(8,128)(2,1)S(1)}, u32[]{:S(2)}, u32[]{:S(2)}) %all-to-all-start) | async-done | bytes 393248 | tf_op jit(solution)/shard_map/all_to_all | solution.py:28
  46.3 9.8 %all-to-all-start.1 = ((f32[8,2,128]{2,1,0:T(2,128)}), f32[8,2,128]{2,1,0:T(2,128)S(1)}, u32[]{:S(2)}, u32[]{:S(2)}) async-start(f32[8,2,128]{2,1,0:T(2,128)} %broadcast_in_dim.11), calls=%async_computation.1 | async-start | bytes 16384 | tf_op jit(solution)/shard_map/all_to_all | solution.py:28
  56.3 13.6 %all-to-all-done.1 = f32[8,2,128]{2,1,0:T(2,128)S(1)} async-done(((f32[8,2,128]{2,1,0:T(2,128)}), f32[8,2,128]{2,1,0:T(2,128)S(1)}, u32[]{:S(2)}, u32[]{:S(2)}) %all-to-all-start.1) | async-done | bytes 8224 | tf_op jit(solution)/shard_map/all_to_all | solution.py:28
  71.7 6.0 %all-gather.4.cloned.1.call-done = bf16[1536,3072]{1,0:T(8,128)(2,1)} async-done(((bf16[192,3072]{1,0:T(8,128)(2,1)}), bf16[1536,3072]{1,0:T(8,128)(2,1)}) %all-gather.4.cloned.1.call-update) | async-done | bytes 9437200 | tf_op jit(solution)/shard_map/all_gather | solution.py:49
  77.7 6.1 %convolution_convert_fusion.1 = bf16[128,3072]{1,0:T(8,128)(2,1)} fusion(bf16[128,1536]{1,0:T(8,128)(2,1)} %add_convert_fusion, bf16[1536,3072]{1,0:T(8,128)(2,1)} %all-gather.4.cloned.1.call-done), kind=kOutput, calls=%fused_computation.1 | convolution fusion | flops 1208352768 | bytes 10616832 | tf_op jit(solution)/shard_map/dot_general | solution.py:79
  83.8 4.0 %all-to-all-start.2 = ((bf16[4,32,3072]{2,1,0:T(8,128)(2,1)}), bf16[4,32,3072]{2,1,0:T(8,128)(2,1)S(1)}, u32[]{:S(2)}, u32[]{:S(2)}) async-start(bf16[4,32,3072]{2,1,0:T(8,128)(2,1)} %bitcast.11), calls=%async_computation.2 | async-start | bytes 1572864 | tf_op jit(solution)/shard_map/all_to_all | solution.py:28
  87.8 8.3 %all-to-all-done.2 = bf16[4,32,3072]{2,1,0:T(8,128)(2,1)S(1)} async-done(((bf16[4,32,3072]{2,1,0:T(8,128)(2,1)}), bf16[4,32,3072]{2,1,0:T(8,128)(2,1)S(1)}, u32[]{:S(2)}, u32[]{:S(2)}) %all-to-all-start.2) | async-done | bytes 786464 | tf_op jit(solution)/shard_map/all_to_all | solution.py:28
  96.3 16.1 %collective-permute-start.1 = (bf16[32,3072]{1,0:T(8,128)(2,1)S(1)}, bf16[32,3072]{1,0:T(8,128)(2,1)S(1)}, u32[]{:S(2)}, u32[]{:S(2)}) collective-permute-start(bf16[32,3072]{1,0:T(8,128)(2,1)S(1)} %reduce-precision_convert_fusion), channel_id=1, source_target_pairs={{0,32},{32,0},{1,33},{33,1},{2,34},{34,2},{3,35},{35,3},{4,36},{36... | collective-permute-start | bytes 589832 | tf_op jit(solution)/shard_map/ppermute | solution.py:37
  112.4 3.3 %collective-permute-done.1 = bf16[32,3072]{1,0:T(8,128)(2,1)S(1)} collective-permute-done((bf16[32,3072]{1,0:T(8,128)(2,1)S(1)}, bf16[32,3072]{1,0:T(8,128)(2,1)S(1)}, u32[]{:S(2)}, u32[]{:S(2)}) %collective-permute-start.1) | collective-permute-done | bytes 196640 | tf_op jit(solution)/shard_map/ppermute | solution.py:37
  116.1 11.5 %all_to_all.30 = bf16[4,32,3072]{2,1,0:T(8,128)(2,1)} all-to-all(bf16[4,32,3072]{2,1,0:T(8,128)(2,1)S(1)} %broadcast_in_dim.12), channel_id=1, replica_groups=mesh['y'=4,'core'=2,'zh'=2,'x'=4,'gz'=8] {'x'}, dimensions={0} | all-to-all | bytes 1572864 | tf_op jit(solution)/shard_map/all_to_all | solution.py:28
  127.6 7.3 %multiply_reduce_fusion = (bf16[1536]{0:T(1024)(128)(2,1)S(1)}, bf16[1536]{0:T(1024)(128)(2,1)S(1)}, bf16[128,1536]{1,0:T(8,128)(2,1)S(1)}) fusion(f32[4,2,16,1536]{3,2,1,0:T(8,128)S(1)} %copy.35, f32[128]{0:T(128)S(1)} %add_rsqrt_fusion, f32[128]{0:T(128)S(1)} %broadcast_multiply_fusion.1, bf16[128,3072]{1,0:T(8,128)(2,1)} %bitcast.56, ...), kind=kOutput, calls=%fused_computation.8 | convolution fusion | flops 1209136128 | bytes 11410432 | tf_op jit(solution)/shard_map/dot_general | solution.py:89
  135.9 24.3 %all-to-all-start.4 = ((bf16[8,16,1792]{2,1,0:T(8,128)(2,1)}), bf16[8,16,1792]{2,1,0:T(8,128)(2,1)S(1)}, u32[]{:S(2)}, u32[]{:S(2)}) async-start(bf16[8,16,1792]{2,1,0:T(8,128)(2,1)} %pad_maximum_fusion), calls=%async_computation.4 | async-start | bytes 917504 | tf_op jit(solution)/shard_map/all_to_all | solution.py:28
  160.5 18.7 %all-to-all-done.4 = bf16[8,16,1792]{2,1,0:T(8,128)(2,1)S(1)} async-done(((bf16[8,16,1792]{2,1,0:T(8,128)(2,1)}), bf16[8,16,1792]{2,1,0:T(8,128)(2,1)S(1)}, u32[]{:S(2)}, u32[]{:S(2)}) %all-to-all-start.4) | async-done | bytes 458784 | tf_op jit(solution)/shard_map/all_to_all | solution.py:28
  179.4 9.8 %collective-permute-start.2 = (f32[48,128]{1,0:T(8,128)S(1)}, f32[48,128]{1,0:T(8,128)S(1)}, u32[]{:S(2)}, u32[]{:S(2)}) collective-permute-start(f32[48,128]{1,0:T(8,128)S(1)} %pad_maximum_fusion.1), channel_id=1, source_target_pairs={{0,64},{64,0},{1,65},{65,1},{2,66},{66,2},{3,67},{67,3},{4,68},{68... | collective-permute-start | bytes 73736 | tf_op jit(solution)/shard_map/ppermute | solution.py:114
  190.0 7.3 %all-to-all-start.5 = ((f32[8,2,16]{2,1,0:T(2,128)}), f32[8,2,16]{2,1,0:T(2,128)S(1)}, u32[]{:S(2)}, u32[]{:S(2)}) async-start(f32[8,2,16]{2,1,0:T(2,128)} %broadcast_in_dim.14), calls=%async_computation.5 | async-start | bytes 16384 | tf_op jit(solution)/shard_map/all_to_all | solution.py:28
  197.2 13.8 %all-to-all-done.5 = f32[8,2,16]{2,1,0:T(2,128)S(1)} async-done(((f32[8,2,16]{2,1,0:T(2,128)}), f32[8,2,16]{2,1,0:T(2,128)S(1)}, u32[]{:S(2)}, u32[]{:S(2)}) %all-to-all-start.5) | async-done | bytes 1056 | tf_op jit(solution)/shard_map/all_to_all | solution.py:28
  211.0 1.9 collective-permute-start.3
  213.0 2.6 %collective-permute-done.3 = f32[48,128]{1,0:T(8,128)S(1)} collective-permute-done((f32[48,128]{1,0:T(8,128)S(1)}, f32[48,128]{1,0:T(8,128)S(1)}, u32[]{:S(2)}, u32[]{:S(2)}) %collective-permute-start.3) | collective-permute-done | bytes 24608 | tf_op jit(solution)/shard_map/ppermute | solution.py:115
  215.6 2.6 %collective-permute-start.4 = (f32[48,128]{1,0:T(8,128)S(1)}, f32[48,128]{1,0:T(8,128)S(1)}, u32[]{:S(2)}, u32[]{:S(2)}) collective-permute-start(f32[48,128]{1,0:T(8,128)S(1)} %add.112), channel_id=1, source_target_pairs={{0,384},{384,0},{128,256},{256,128},{1,385},{385,1},{129,257},{257... | collective-permute-start | bytes 73736 | tf_op jit(solution)/shard_map/ppermute | solution.py:116
  218.9 2.4 %collective-permute-done.4 = f32[48,128]{1,0:T(8,128)S(1)} collective-permute-done((f32[48,128]{1,0:T(8,128)S(1)}, f32[48,128]{1,0:T(8,128)S(1)}, u32[]{:S(2)}, u32[]{:S(2)}) %collective-permute-start.4) | collective-permute-done | bytes 24608 | tf_op jit(solution)/shard_map/ppermute | solution.py:116
  222.6 5.6 %convolution_convert_fusion = bf16[192,3072]{1,0:T(8,128)(2,1)} fusion(bf16[1024,3072]{1,0:T(8,128)(2,1)} %all-gather.8.cloned.1.call-done, bf16[1024,1536]{1,0:T(8,128)(2,1)} %all-gather.6.cloned.1.call-done, s32[]{:T(128)S(6)} %select_n.24), kind=kOutput, calls=%fused_computation | convolution fusion | flops 1208549376 | bytes 7995396 | tf_op jit(solution)/shard_map/dot_general | solution.py:136
  (74 shorter events, 10.7 us)
Async XLA Ops:
  7.2 70.5 %all-gather.4.cloned.1.call-start = ((), (), s32[]{:S(2)}) async-start(), calls=%async_computation.6 | async-start | bytes 10616832 | tf_op jit(solution)/shard_map/all_gather | solution.py:49
  9.5 35.6 %all-to-all-start = ((bf16[8,16,1536]{2,1,0:T(8,128)(2,1)}), bf16[8,16,1536]{2,1,0:T(8,128)(2,1)S(1)}, u32[]{:S(2)}, u32[]{:S(2)}) async-start(bf16[8,16,1536]{2,1,0:T(8,128)(2,1)} %broadcast_in_dim.10), calls=%async_computation | async-start | bytes 786432 | tf_op jit(solution)/shard_map/all_to_all | solution.py:28
  22.5 15.6 %collective-permute-start = (bf16[16,3072]{1,0:T(8,128)(2,1)}, bf16[16,3072]{1,0:T(8,128)(2,1)S(1)}, u32[]{:S(2)}, u32[]{:S(2)}) collective-permute-start(bf16[16,3072]{1,0:T(8,128)(2,1)} %param.11), channel_id=1, source_target_pairs={{0,32},{32,0},{1,33},{33,1},{2,34},{34,2},{3,35},{35,3},{4,36},{36... | collective-permute-start | bytes 294920 | tf_op jit(solution)/shard_map/ppermute | solution.py:37
  46.3 23.5 %all-to-all-start.1 = ((f32[8,2,128]{2,1,0:T(2,128)}), f32[8,2,128]{2,1,0:T(2,128)S(1)}, u32[]{:S(2)}, u32[]{:S(2)}) async-start(f32[8,2,128]{2,1,0:T(2,128)} %broadcast_in_dim.11), calls=%async_computation.1 | async-start | bytes 16384 | tf_op jit(solution)/shard_map/all_to_all | solution.py:28
  56.1 166.5 %all-gather.6.cloned.1.call-start = ((), (), s32[]{:S(2)}) async-start(), calls=%async_computation.7 | async-start | bytes 3538944 | tf_op jit(solution)/shard_map/all_gather | solution.py:86
  71.6 40.7 %copy-start.2 = (bf16[16,3072]{1,0:T(8,128)(2,1)S(1)}, bf16[16,3072]{1,0:T(8,128)(2,1)}, u32[]{:S(2)}) copy-start(bf16[16,3072]{1,0:T(8,128)(2,1)} %param.11) | copy-start | bytes 294916
  71.6 44.0 %copy-start.4 = (f32[3072]{0:T(1024)S(1)}, f32[3072]{0:T(1024)}, u32[]{:S(2)}) copy-start(f32[3072]{0:T(1024)} %param.10) | copy-start | bytes 36868
  83.8 12.3 %all-to-all-start.2 = ((bf16[4,32,3072]{2,1,0:T(8,128)(2,1)}), bf16[4,32,3072]{2,1,0:T(8,128)(2,1)S(1)}, u32[]{:S(2)}, u32[]{:S(2)}) async-start(bf16[4,32,3072]{2,1,0:T(8,128)(2,1)} %bitcast.11), calls=%async_computation.2 | async-start | bytes 1572864 | tf_op jit(solution)/shard_map/all_to_all | solution.py:28
  87.8 134.8 %all-gather.8.cloned.1.call-start = ((), (), s32[]{:S(2)}) async-start(), calls=%async_computation.8 | async-start | bytes 7077888 | tf_op jit(solution)/shard_map/all_gather | solution.py:87
  96.3 19.4 %collective-permute-start.1 = (bf16[32,3072]{1,0:T(8,128)(2,1)S(1)}, bf16[32,3072]{1,0:T(8,128)(2,1)S(1)}, u32[]{:S(2)}, u32[]{:S(2)}) collective-permute-start(bf16[32,3072]{1,0:T(8,128)(2,1)S(1)} %reduce-precision_convert_fusion), channel_id=1, source_target_pairs={{0,32},{32,0},{1,33},{33,1},{2,34},{34,2},{3,35},{35,3},{4,36},{36... | collective-permute-start | bytes 589832 | tf_op jit(solution)/shard_map/ppermute | solution.py:37
  127.6 32.8 %copy-start = (bf16[4,32,3072]{2,1,0:T(8,128)(2,1)S(1)}, bf16[4,32,3072]{2,1,0:T(8,128)(2,1)}, u32[]{:S(2)}) copy-start(bf16[4,32,3072]{2,1,0:T(8,128)(2,1)} %all_to_all.30) | copy-start | bytes 2359300
  127.6 61.6 %copy-start.1 = (bf16[16,1536]{1,0:T(8,128)(2,1)S(1)}, bf16[16,1536]{1,0:T(8,128)(2,1)}, u32[]{:S(2)}) copy-start(bf16[16,1536]{1,0:T(8,128)(2,1)} %param.6) | copy-start | bytes 147460
  127.6 61.5 %copy-start.3 = (f32[1536]{0:T(1024)S(1)}, f32[1536]{0:T(1024)}, u32[]{:S(2)}) copy-start(f32[1536]{0:T(1024)} %param.7) | copy-start | bytes 18436
  135.9 43.3 %all-to-all-start.4 = ((bf16[8,16,1792]{2,1,0:T(8,128)(2,1)}), bf16[8,16,1792]{2,1,0:T(8,128)(2,1)S(1)}, u32[]{:S(2)}, u32[]{:S(2)}) async-start(bf16[8,16,1792]{2,1,0:T(8,128)(2,1)} %pad_maximum_fusion), calls=%async_computation.4 | async-start | bytes 917504 | tf_op jit(solution)/shard_map/all_to_all | solution.py:28
  179.4 31.6 %collective-permute-start.2 = (f32[48,128]{1,0:T(8,128)S(1)}, f32[48,128]{1,0:T(8,128)S(1)}, u32[]{:S(2)}, u32[]{:S(2)}) collective-permute-start(f32[48,128]{1,0:T(8,128)S(1)} %pad_maximum_fusion.1), channel_id=1, source_target_pairs={{0,64},{64,0},{1,65},{65,1},{2,66},{66,2},{3,67},{67,3},{4,68},{68... | collective-permute-start | bytes 73736 | tf_op jit(solution)/shard_map/ppermute | solution.py:114
  190.0 21.0 %all-to-all-start.5 = ((f32[8,2,16]{2,1,0:T(2,128)}), f32[8,2,16]{2,1,0:T(2,128)S(1)}, u32[]{:S(2)}, u32[]{:S(2)}) async-start(f32[8,2,16]{2,1,0:T(2,128)} %broadcast_in_dim.14), calls=%async_computation.5 | async-start | bytes 16384 | tf_op jit(solution)/shard_map/all_to_all | solution.py:28
  211.0 4.6 %collective-permute-start.3 = (f32[48,128]{1,0:T(8,128)S(1)}, f32[48,128]{1,0:T(8,128)S(1)}, u32[]{:S(2)}, u32[]{:S(2)}) collective-permute-start(f32[48,128]{1,0:T(8,128)S(1)} %fusion.14), channel_id=1, source_target_pairs={{0,128},{128,0},{256,384},{384,256},{1,129},{129,1},{257,385},{385... | collective-permute-start | bytes 73736 | tf_op jit(solution)/shard_map/ppermute | solution.py:115
  215.6 5.8 %collective-permute-start.4 = (f32[48,128]{1,0:T(8,128)S(1)}, f32[48,128]{1,0:T(8,128)S(1)}, u32[]{:S(2)}, u32[]{:S(2)}) collective-permute-start(f32[48,128]{1,0:T(8,128)S(1)} %add.112), channel_id=1, source_target_pairs={{0,384},{384,0},{128,256},{256,128},{1,385},{385,1},{129,257},{257... | collective-permute-start | bytes 73736 | tf_op jit(solution)/shard_map/ppermute | solution.py:116
Sparse Core Ops, SparseCore 0:
  10.1 67.5 all-gather.3
  79.8 35.7 all-gather.5
  127.7 61.8 all-gather.7

commit v4 on v3

--- a/solution.py
+++ b/solution.py
@@ -35,6 +35,11 @@
 
 def swap(block):
     return lax.ppermute(block, "zh", [(0, 1), (1, 0)])
+
+
+def split_float(value):
+    high = lax.reduce_precision(value, 8, 7)
+    return high, value - high
 
 
 def shards(inputs, ln_gain, ln_bias, weight_in, up_bias, grad_hidden):
@@ -76,12 +81,44 @@
         ]
     ).astype(f32)
 
-    partial_hidden = jnp.dot(normed, weight, preferred_element_type=f32).astype(bf16)
-    arrived = exchange(partial_hidden.reshape(around, halves * rows, hidden_width), "x")
+    extra_rows = 8
+    block = halves * rows
+    affine = jnp.stack([*split_float(ln_gain), *split_float(ln_bias)]).astype(bf16)
+    affine = jnp.pad(affine, ((0, extra_rows - 4), (0, 0)))
+    stacked = jnp.concatenate(
+        [
+            normed.reshape(around, block, width),
+            jnp.broadcast_to(affine[None], (around,) + affine.shape),
+        ],
+        axis=1,
+    )
+    partial_hidden = jnp.dot(
+        stacked.reshape(-1, width), weight, preferred_element_type=f32
+    ).astype(bf16)
+    arrived = exchange(partial_hidden.reshape(around, block + extra_rows, hidden_width), "x")
     half_sum = lax.reduce_precision(jnp.sum(arrived.astype(f32), axis=0), 8, 7)
-    hidden = half_sum + swap(half_sum.astype(bf16)).astype(f32) + up_bias
-    grad_pre = (cotangent * gelu_slope(hidden)).astype(bf16)
-    grad_local = spread(grad_pre, "x").reshape(local, hidden_width)
+    products = half_sum + swap(half_sum.astype(bf16)).astype(f32)
+    product = products[:block]
+    gain_product = products[block] + products[block + 1]
+    bias_product = products[block + 2] + products[block + 3]
+    grad_pre = (cotangent * gelu_slope(product + up_bias)).astype(bf16)
+    grad_pre_float = grad_pre.astype(f32)
+    token_sums = jnp.stack(
+        [
+            jnp.sum(grad_pre_float * gain_product, axis=1),
+            jnp.sum(grad_pre_float * (product - bias_product), axis=1),
+        ]
+    )
+    token_rows = jnp.concatenate(split_float(token_sums)).astype(bf16)
+    token_rows = jnp.pad(token_rows, ((0, extra_rows - 4), (0, hidden_width - block)))
+    around_rows = spread(jnp.concatenate([grad_pre, token_rows]), "x")
+    grad_local = around_rows[:, :block].reshape(local, hidden_width)
+    token_parts = (
+        around_rows[:, block : block + 4, :block]
+        .reshape(around, 4, halves, rows)
+        .transpose(2, 0, 3, 1)
+        .reshape(depth, rows, 4)
+    )
 
     all_normed = lax.all_gather(normed, gx, axis=0, tiled=True)
     portion = lax.all_gather(grad_local, gx, axis=0, tiled=True)
@@ -91,8 +128,7 @@
     )
     sums = jnp.stack([jnp.sum(back * x_hat, axis=0), jnp.sum(back, axis=0)]).astype(bf16)
     packed = 2 * width // rows
-    padding = -packed % 128
-    extra = jnp.pad(sums.reshape(rows, packed), ((0, 0), (0, padding)))
+    padding = -(packed + 4) % 128
     ordered = (
         back.astype(bf16)
         .reshape(around, halves, rows, width)
@@ -100,7 +136,15 @@
         .reshape(depth, rows, width)
     )
     landed = exchange(
-        jnp.concatenate([ordered, jnp.broadcast_to(extra[None], (depth,) + extra.shape)], axis=2),
+        jnp.concatenate(
+            [
+                ordered,
+                jnp.broadcast_to(sums.reshape(1, rows, packed), (depth, rows, packed)),
+                token_parts,
+                jnp.zeros((depth, rows, padding), bf16),
+            ],
+            axis=2,
+        ),
         "gz",
     )
     total = jnp.sum(landed.astype(f32), axis=0)
@@ -111,10 +155,7 @@
             jnp.sum(grad_local.astype(f32), axis=0),
         ]
     ).reshape(-1, 128)
-    small = small + lax.ppermute(small, "core", [(0, 1), (1, 0)])
-    small = small + lax.ppermute(small, "y", [(0, 1), (1, 0), (2, 3), (3, 2)])
-    small = small + lax.ppermute(small, "y", [(0, 3), (3, 0), (1, 2), (2, 1)])
-    small = small.reshape(-1)
+    small = jnp.sum(spread(small, gx), axis=0).reshape(-1)
     grad_ln_gain, grad_ln_bias = small[:width], small[width : 2 * width]
     grad_up_bias = small[2 * width :]
 
@@ -125,8 +166,9 @@
     own_inv = mine(inv_std)
     own_hat = (inputs.astype(f32) - mine(mean)) * own_inv
     scaled = grad_float * ln_gain
-    token_sums = jnp.stack([jnp.sum(scaled, axis=1), jnp.sum(scaled * own_hat, axis=1)])
-    first_total, second_total = jnp.sum(spread(token_sums, gy), axis=0)
+    parts = total[:, width + packed : width + packed + 4]
+    first_total = parts[:, 0] + parts[:, 2]
+    second_total = parts[:, 1] + parts[:, 3]
     grad_inputs = (
         own_inv * (scaled - first_total[:, None] / D - own_hat * (second_total[:, None] / D))
     ).astype(bf16)

time: 237 us -> 257 us (1.084)
  waiting for transfers between devices: 82.9 us -> 106 us
  starting transfers between devices: 96.7 us -> 91.7 us
    all_gather x1, waiting for transfers between devices: 0.01 us -> 34.5 us  [shards(): portion = lax.all_gather(grad_local, gx, axis=0, tiled=True)]
    ppermute x3 -> x0, starting transfers between devices: 14.3 us -> none  [the longest x1 9.75 us: shards(): small = small + lax.ppermute(small, 'core', [(0, 1), (1, 0)])]
    all_to_all x5, starting transfers between devices: 58.4 us -> 67 us  [exchange(): return lax.all_to_all(blocks, axis, split_axis=0, concat_axis=0, tiled=True)]
    all_to_all x5, waiting for transfers between devices: 60.1 us -> 52.9 us  [exchange(): return lax.all_to_all(blocks, axis, split_axis=0, concat_axis=0, tiled=True)]
    ppermute x3 -> x0, waiting for transfers between devices: 5.07 us -> none  [the longest x1 2.63 us: shards(): small = small + lax.ppermute(small, 'y', [(0, 1), (1, 0), (2, 3), (3, 2)])]
  transfers between devices with their start and end apart: 13 -> 10, of which waited for: 10 -> 9; matrix products, arithmetic and copies ran while one was open for 10% -> 4% of each run, Pallas kernels for 0% -> 0%
where the time goes in v4:
time: 257 us; the launch traced here: 256 us
  waiting for transfers between devices  106 us (41%)
  starting transfers between devices  91.7 us (36%)
  matrix products  19.8 us (8%)
  between operations  14.7 us (6%)
  blocking collectives  11.8 us (5%)
  local copies, waits for them, and re-layouts  6.75 us (3%)
  other arithmetic  4.89 us (2%)
    all_to_all x5, starting transfers between devices, exchange(): return lax.all_to_all(blocks, axis, split_axis=0, concat_axis=0, tiled=True)  67 us
    all_to_all x5, waiting for transfers between devices, exchange(): return lax.all_to_all(blocks, axis, split_axis=0, concat_axis=0, tiled=True)  52.9 us
    all_gather x1, waiting for transfers between devices, shards(): portion = lax.all_gather(grad_local, gx, axis=0, tiled=True)  34.5 us
    ppermute x2, starting transfers between devices, swap(): return lax.ppermute(block, 'zh', [(0, 1), (1, 0)])  24.6 us
    all_to_all x1, blocking collectives, exchange(): return lax.all_to_all(blocks, axis, split_axis=0, concat_axis=0, tiled=True)  11.8 us
    ppermute x2, waiting for transfers between devices, swap(): return lax.ppermute(block, 'zh', [(0, 1), (1, 0)])  11 us
    dot_general x1, matrix products, shards(): lax.dot_general(grad_local, weight, (((1,), (1,)), ((), ())), preferred_e...  7.91 us
    all_gather x1, waiting for transfers between devices, shards(): weight = lax.all_gather(weight_in, gx, axis=0, tiled=True)  6.61 us
  transfers between devices with their start and end apart: 10, of which 9 were waited for; matrix products, arithmetic and copies ran while one was open for 4% of the time, Pallas kernels for 0%

profile of v4, /device:TPU:1, one launch (start us, length us, event | category | flops | bytes accessed | tf_op | source)
XLA Modules:
  0.0 256.1 jit_solution(12403878749764026514)
XLA Ops:
  7.9 1.6 broadcast_in_dim.14
  9.5 13.1 %all-to-all-start = ((bf16[8,16,1536]{2,1,0:T(8,128)(2,1)}), bf16[8,16,1536]{2,1,0:T(8,128)(2,1)S(1)}, u32[]{:S(2)}, u32[]{:S(2)}) async-start(bf16[8,16,1536]{2,1,0:T(8,128)(2,1)} %broadcast_in_dim.14), calls=%async_computation | async-start | bytes 786432 | tf_op jit(solution)/shard_map/all_to_all | solution.py:28
  22.5 7.9 %collective-permute-start = (bf16[16,3072]{1,0:T(8,128)(2,1)}, bf16[16,3072]{1,0:T(8,128)(2,1)S(1)}, u32[]{:S(2)}, u32[]{:S(2)}) collective-permute-start(bf16[16,3072]{1,0:T(8,128)(2,1)} %param.11), channel_id=1, source_target_pairs={{0,32},{32,0},{1,33},{33,1},{2,34},{34,2},{3,35},{35,3},{4,36},{36... | collective-permute-start | bytes 294920 | tf_op jit(solution)/shard_map/ppermute | solution.py:37
  32.0 6.2 %collective-permute-done = bf16[16,3072]{1,0:T(8,128)(2,1)S(1)} collective-permute-done((bf16[16,3072]{1,0:T(8,128)(2,1)}, bf16[16,3072]{1,0:T(8,128)(2,1)S(1)}, u32[]{:S(2)}, u32[]{:S(2)}) %collective-permute-start) | collective-permute-done | bytes 98336 | tf_op jit(solution)/shard_map/ppermute | solution.py:37
  39.3 5.8 %all-to-all-done = bf16[8,16,1536]{2,1,0:T(8,128)(2,1)S(1)} async-done(((bf16[8,16,1536]{2,1,0:T(8,128)(2,1)}), bf16[8,16,1536]{2,1,0:T(8,128)(2,1)S(1)}, u32[]{:S(2)}, u32[]{:S(2)}) %all-to-all-start) | async-done | bytes 393248 | tf_op jit(solution)/shard_map/all_to_all | solution.py:28
  46.3 9.8 %all-to-all-start.1 = ((f32[8,2,128]{2,1,0:T(2,128)}), f32[8,2,128]{2,1,0:T(2,128)S(1)}, u32[]{:S(2)}, u32[]{:S(2)}) async-start(f32[8,2,128]{2,1,0:T(2,128)} %broadcast_in_dim.15), calls=%async_computation.1 | async-start | bytes 16384 | tf_op jit(solution)/shard_map/all_to_all | solution.py:28
  56.2 13.6 %all-to-all-done.1 = f32[8,2,128]{2,1,0:T(2,128)S(1)} async-done(((f32[8,2,128]{2,1,0:T(2,128)}), f32[8,2,128]{2,1,0:T(2,128)S(1)}, u32[]{:S(2)}, u32[]{:S(2)}) %all-to-all-start.1) | async-done | bytes 8224 | tf_op jit(solution)/shard_map/all_to_all | solution.py:28
  70.1 0.9 fusion.4
  71.1 6.6 %all-gather.4.cloned.1.call-done = bf16[1536,3072]{1,0:T(8,128)(2,1)} async-done(((bf16[192,3072]{1,0:T(8,128)(2,1)}), bf16[1536,3072]{1,0:T(8,128)(2,1)}) %all-gather.4.cloned.1.call-update) | async-done | bytes 9437200 | tf_op jit(solution)/shard_map/all_gather | solution.py:54
  77.7 6.4 %convolution_convert_fusion.1 = bf16[160,3072]{1,0:T(8,128)(2,1)} fusion(bf16[160,1536]{1,0:T(8,128)(2,1)S(1)} %bitcast.70, bf16[1536,3072]{1,0:T(8,128)(2,1)} %all-gather.4.cloned.1.call-done), kind=kOutput, calls=%fused_computation.1 | convolution fusion | flops 1510440960 | bytes 10911744 | tf_op jit(solution)/shard_map/dot_general | solution.py:95
  84.1 4.1 %all-to-all-start.2 = ((bf16[4,40,3072]{2,1,0:T(8,128)(2,1)}), bf16[4,40,3072]{2,1,0:T(8,128)(2,1)S(1)}, u32[]{:S(2)}, u32[]{:S(2)}) async-start(bf16[4,40,3072]{2,1,0:T(8,128)(2,1)} %bitcast.12), calls=%async_computation.2 | async-start | bytes 1966080 | tf_op jit(solution)/shard_map/all_to_all | solution.py:28
  88.2 9.8 %all-to-all-done.2 = bf16[4,40,3072]{2,1,0:T(8,128)(2,1)S(1)} async-done(((bf16[4,40,3072]{2,1,0:T(8,128)(2,1)}), bf16[4,40,3072]{2,1,0:T(8,128)(2,1)S(1)}, u32[]{:S(2)}, u32[]{:S(2)}) %all-to-all-start.2) | async-done | bytes 983072 | tf_op jit(solution)/shard_map/all_to_all | solution.py:28
  98.2 16.7 %collective-permute-start.1 = (bf16[40,3072]{1,0:T(8,128)(2,1)S(1)}, bf16[40,3072]{1,0:T(8,128)(2,1)S(1)}, u32[]{:S(2)}, u32[]{:S(2)}) collective-permute-start(bf16[40,3072]{1,0:T(8,128)(2,1)S(1)} %reduce-precision_convert_fusion), channel_id=1, source_target_pairs={{0,32},{32,0},{1,33},{33,1},{2,34},{34,2},{3,35},{35,3},{4,36},{36... | collective-permute-start | bytes 737288 | tf_op jit(solution)/shard_map/ppermute | solution.py:37
  114.9 4.8 %collective-permute-done.1 = bf16[40,3072]{1,0:T(8,128)(2,1)S(1)} collective-permute-done((bf16[40,3072]{1,0:T(8,128)(2,1)S(1)}, bf16[40,3072]{1,0:T(8,128)(2,1)S(1)}, u32[]{:S(2)}, u32[]{:S(2)}) %collective-permute-start.1) | collective-permute-done | bytes 245792 | tf_op jit(solution)/shard_map/ppermute | solution.py:37
  120.5 11.8 %all_to_all.30 = bf16[4,40,3072]{2,1,0:T(8,128)(2,1)S(1)} all-to-all(bf16[4,40,3072]{2,1,0:T(8,128)(2,1)S(1)} %broadcast_in_dim.17), channel_id=1, replica_groups=mesh['y'=4,'core'=2,'zh'=2,'x'=4,'gz'=8] {'x'}, dimensions={0} | all-to-all | bytes 1966080 | tf_op jit(solution)/shard_map/all_to_all | solution.py:28
  132.4 7.9 %multiply_reduce_fusion = (bf16[1536]{0:T(1024)(128)(2,1)S(1)}, bf16[1536]{0:T(1024)(128)(2,1)S(1)}, bf16[128,1536]{1,0:T(8,128)(2,1)}, bf16[128,1536]{1,0:T(8,128)(2,1)S(1)}) fusion(f32[4,2,16,1536]{3,2,1,0:T(8,128)S(1)} %copy.50, f32[128]{0:T(128)S(1)} %add_rsqrt_fusion, f32[128]{0:T(128)S(1)} %broadcast_multiply_fusion.1, f32[1536]{0:T(1024)S(1)} %copy-done.4, ...), kind=kOutput, calls=%fused_computation.14 | convolution fusion | flops 1209725952 | bytes 11815936 | tf_op jit(solution)/shard_map/dot_general | solution.py:126
  141.5 0.9 concatenate.28
  142.4 28.9 %all-to-all-start.4 = ((bf16[8,16,1792]{2,1,0:T(8,128)(2,1)}), bf16[8,16,1792]{2,1,0:T(8,128)(2,1)S(1)}, u32[]{:S(2)}, u32[]{:S(2)}) async-start(bf16[8,16,1792]{2,1,0:T(8,128)(2,1)} %concatenate.28), calls=%async_computation.4 | async-start | bytes 917504 | tf_op jit(solution)/shard_map/all_to_all | solution.py:28
  171.6 18.7 %all-to-all-done.4 = bf16[8,16,1792]{2,1,0:T(8,128)(2,1)S(1)} async-done(((bf16[8,16,1792]{2,1,0:T(8,128)(2,1)}), bf16[8,16,1792]{2,1,0:T(8,128)(2,1)S(1)}, u32[]{:S(2)}, u32[]{:S(2)}) %all-to-all-start.4) | async-done | bytes 458784 | tf_op jit(solution)/shard_map/all_to_all | solution.py:28
  191.2 11.1 %all-to-all-start.5 = ((f32[8,48,128]{2,1,0:T(8,128)}), f32[8,48,128]{2,1,0:T(8,128)S(1)}, u32[]{:S(2)}, u32[]{:S(2)}) async-start(f32[8,48,128]{2,1,0:T(8,128)} %broadcast_in_dim.20), calls=%async_computation.5 | async-start | bytes 393216 | tf_op jit(solution)/shard_map/all_to_all | solution.py:28
  202.5 0.7 multiply_convert_fusion
  203.2 5.0 %all-to-all-done.5 = f32[8,48,128]{2,1,0:T(8,128)S(1)} async-done(((f32[8,48,128]{2,1,0:T(8,128)}), f32[8,48,128]{2,1,0:T(8,128)S(1)}, u32[]{:S(2)}, u32[]{:S(2)}) %all-to-all-start.5) | async-done | bytes 196640 | tf_op jit(solution)/shard_map/all_to_all | solution.py:28
  209.5 34.5 %all-gather.8.cloned.1.call-done = bf16[1024,3072]{1,0:T(8,128)(2,1)} async-done(((bf16[128,3072]{1,0:T(8,128)(2,1)}), bf16[1024,3072]{1,0:T(8,128)(2,1)}) %all-gather.8.cloned.1.call-update) | async-done | bytes 6291472 | tf_op jit(solution)/shard_map/all_gather | solution.py:124
  244.0 5.6 %convolution_convert_fusion = bf16[192,3072]{1,0:T(8,128)(2,1)} fusion(bf16[1024,3072]{1,0:T(8,128)(2,1)} %all-gather.8.cloned.1.call-done, bf16[1024,1536]{1,0:T(8,128)(2,1)} %all-gather.6.cloned.1.call-done, s32[]{:T(128)S(6)} %select_n.24), kind=kOutput, calls=%fused_computation | convolution fusion | flops 1208549376 | bytes 7995396 | tf_op jit(solution)/shard_map/dot_general | solution.py:178
  (86 shorter events, 9.0 us)
Async XLA Ops:
  7.2 70.5 %all-gather.4.cloned.1.call-start = ((), (), s32[]{:S(2)}) async-start(), calls=%async_computation.6 | async-start | bytes 10616832 | tf_op jit(solution)/shard_map/all_gather | solution.py:54
  9.5 35.6 %all-to-all-start = ((bf16[8,16,1536]{2,1,0:T(8,128)(2,1)}), bf16[8,16,1536]{2,1,0:T(8,128)(2,1)S(1)}, u32[]{:S(2)}, u32[]{:S(2)}) async-start(bf16[8,16,1536]{2,1,0:T(8,128)(2,1)} %broadcast_in_dim.14), calls=%async_computation | async-start | bytes 786432 | tf_op jit(solution)/shard_map/all_to_all | solution.py:28
  22.5 15.6 %collective-permute-start = (bf16[16,3072]{1,0:T(8,128)(2,1)}, bf16[16,3072]{1,0:T(8,128)(2,1)S(1)}, u32[]{:S(2)}, u32[]{:S(2)}) collective-permute-start(bf16[16,3072]{1,0:T(8,128)(2,1)} %param.11), channel_id=1, source_target_pairs={{0,32},{32,0},{1,33},{33,1},{2,34},{34,2},{3,35},{35,3},{4,36},{36... | collective-permute-start | bytes 294920 | tf_op jit(solution)/shard_map/ppermute | solution.py:37
  46.3 23.5 %all-to-all-start.1 = ((f32[8,2,128]{2,1,0:T(2,128)}), f32[8,2,128]{2,1,0:T(2,128)S(1)}, u32[]{:S(2)}, u32[]{:S(2)}) async-start(f32[8,2,128]{2,1,0:T(2,128)} %broadcast_in_dim.15), calls=%async_computation.1 | async-start | bytes 16384 | tf_op jit(solution)/shard_map/all_to_all | solution.py:28
  77.7 37.2 %copy-start.3 = (bf16[16,3072]{1,0:T(8,128)(2,1)S(1)}, bf16[16,3072]{1,0:T(8,128)(2,1)}, u32[]{:S(2)}) copy-start(bf16[16,3072]{1,0:T(8,128)(2,1)} %param.11) | copy-start | bytes 294916
  77.7 42.1 %copy-start.5 = (f32[3072]{0:T(1024)S(1)}, f32[3072]{0:T(1024)}, u32[]{:S(2)}) copy-start(f32[3072]{0:T(1024)} %param.10) | copy-start | bytes 36868
  84.1 48.3 %copy-start.2 = (f32[1536]{0:T(1024)S(1)}, f32[1536]{0:T(1024)}, u32[]{:S(2)}) copy-start(f32[1536]{0:T(1024)} %param.7) | copy-start | bytes 18436
  84.1 48.3 %copy-start.4 = (f32[1536]{0:T(1024)S(1)}, f32[1536]{0:T(1024)}, u32[]{:S(2)}) copy-start(f32[1536]{0:T(1024)} %param.8) | copy-start | bytes 18436
  84.1 13.9 %all-to-all-start.2 = ((bf16[4,40,3072]{2,1,0:T(8,128)(2,1)}), bf16[4,40,3072]{2,1,0:T(8,128)(2,1)S(1)}, u32[]{:S(2)}, u32[]{:S(2)}) async-start(bf16[4,40,3072]{2,1,0:T(8,128)(2,1)} %bitcast.12), calls=%async_computation.2 | async-start | bytes 1966080 | tf_op jit(solution)/shard_map/all_to_all | solution.py:28
  88.2 121.3 %all-gather.6.cloned.1.call-start = ((), (), s32[]{:S(2)}) async-start(), calls=%async_computation.7 | async-start | bytes 3538944 | tf_op jit(solution)/shard_map/all_gather | solution.py:123
  98.2 21.6 %collective-permute-start.1 = (bf16[40,3072]{1,0:T(8,128)(2,1)S(1)}, bf16[40,3072]{1,0:T(8,128)(2,1)S(1)}, u32[]{:S(2)}, u32[]{:S(2)}) collective-permute-start(bf16[40,3072]{1,0:T(8,128)(2,1)S(1)} %reduce-precision_convert_fusion), channel_id=1, source_target_pairs={{0,32},{32,0},{1,33},{33,1},{2,34},{34,2},{3,35},{35,3},{4,36},{36... | collective-permute-start | bytes 737288 | tf_op jit(solution)/shard_map/ppermute | solution.py:37
  132.3 8.0 %copy-start = (bf16[4,32,3072]{2,1,0:T(8,128)(2,1)}, bf16[4,32,3072]{2,1,0:T(8,128)(2,1)S(1)}, u32[]{:S(2)}) copy-start(bf16[4,32,3072]{2,1,0:T(8,128)(2,1)S(1)} %slice.103) | copy-start | bytes 2359300
  132.4 70.1 %copy-start.1 = (bf16[16,1536]{1,0:T(8,128)(2,1)S(1)}, bf16[16,1536]{1,0:T(8,128)(2,1)}, u32[]{:S(2)}) copy-start(bf16[16,1536]{1,0:T(8,128)(2,1)} %param.6) | copy-start | bytes 147460
  140.3 103.7 %all-gather.8.cloned.1.call-start = ((), (), s32[]{:S(2)}) async-start(), calls=%async_computation.8 | async-start | bytes 7077888 | tf_op jit(solution)/shard_map/all_gather | solution.py:124
  142.4 47.9 %all-to-all-start.4 = ((bf16[8,16,1792]{2,1,0:T(8,128)(2,1)}), bf16[8,16,1792]{2,1,0:T(8,128)(2,1)S(1)}, u32[]{:S(2)}, u32[]{:S(2)}) async-start(bf16[8,16,1792]{2,1,0:T(8,128)(2,1)} %concatenate.28), calls=%async_computation.4 | async-start | bytes 917504 | tf_op jit(solution)/shard_map/all_to_all | solution.py:28
  191.2 17.1 %all-to-all-start.5 = ((f32[8,48,128]{2,1,0:T(8,128)}), f32[8,48,128]{2,1,0:T(8,128)S(1)}, u32[]{:S(2)}, u32[]{:S(2)}) async-start(f32[8,48,128]{2,1,0:T(8,128)} %broadcast_in_dim.20), calls=%async_computation.5 | async-start | bytes 393216 | tf_op jit(solution)/shard_map/all_to_all | solution.py:28
Sparse Core Ops, SparseCore 0:
  10.1 67.5 all-gather.3
  140.4 52.0 all-gather.5
  195.3 48.7 all-gather.7

commit v5 on v4

--- a/solution.py
+++ b/solution.py
@@ -92,9 +92,9 @@
         ],
         axis=1,
     )
-    partial_hidden = jnp.dot(
-        stacked.reshape(-1, width), weight, preferred_element_type=f32
-    ).astype(bf16)
+    stacked = stacked.reshape(-1, width)
+    all_stacked = lax.all_gather(stacked, gx, axis=0, tiled=True)
+    partial_hidden = jnp.dot(stacked, weight, preferred_element_type=f32).astype(bf16)
     arrived = exchange(partial_hidden.reshape(around, block + extra_rows, hidden_width), "x")
     half_sum = lax.reduce_precision(jnp.sum(arrived.astype(f32), axis=0), 8, 7)
     products = half_sum + swap(half_sum.astype(bf16)).astype(f32)
@@ -120,7 +120,6 @@
         .reshape(depth, rows, 4)
     )
 
-    all_normed = lax.all_gather(normed, gx, axis=0, tiled=True)
     portion = lax.all_gather(grad_local, gx, axis=0, tiled=True)
 
     back = lax.dot_general(
@@ -172,8 +171,10 @@
     grad_inputs = (
         own_inv * (scaled - first_total[:, None] / D - own_hat * (second_total[:, None] / D))
     ).astype(bf16)
-    feature_rows = lax.dynamic_slice_in_dim(
-        all_normed, lax.axis_index(gx) * sub_width, sub_width, axis=1
+    feature_rows = (
+        lax.dynamic_slice_in_dim(all_stacked, lax.axis_index(gx) * sub_width, sub_width, axis=1)
+        .reshape(-1, block + extra_rows, sub_width)[:, :block]
+        .reshape(-1, sub_width)
     )
     grad_weight = lax.dot_general(
         feature_rows, portion, (((0,), (0,)), ((), ())), preferred_element_type=f32

time: 257 us -> 222 us (0.86)
  waiting for transfers between devices: 106 us -> 68.2 us
    all_gather x1, waiting for transfers between devices: 34.5 us -> 0.01 us  [shards(): portion = lax.all_gather(grad_local, gx, axis=0, tiled=True)]
  transfers between devices with their start and end apart: 10 -> 10, of which waited for: 9 -> 8; matrix products, arithmetic and copies ran while one was open for 4% -> 13% of each run, Pallas kernels for 0% -> 0%
where the time goes in v5:
time: 222 us; the launch traced here: 221 us
  starting transfers between devices  92.7 us (42%)
  waiting for transfers between devices  68.2 us (31%)
  matrix products  18.9 us (9%)
  between operations  14.7 us (7%)
  blocking collectives  11.8 us (5%)
  local copies, waits for them, and re-layouts  9.15 us (4%)
  other arithmetic  5.66 us (3%)
    all_to_all x5, starting transfers between devices, exchange(): return lax.all_to_all(blocks, axis, split_axis=0, concat_axis=0, tiled=True)  67.6 us
    all_to_all x5, waiting for transfers between devices, exchange(): return lax.all_to_all(blocks, axis, split_axis=0, concat_axis=0, tiled=True)  50.8 us
    ppermute x2, starting transfers between devices, swap(): return lax.ppermute(block, 'zh', [(0, 1), (1, 0)])  25 us
    all_to_all x1, blocking collectives, exchange(): return lax.all_to_all(blocks, axis, split_axis=0, concat_axis=0, tiled=True)  11.8 us
    ppermute x2, waiting for transfers between devices, swap(): return lax.ppermute(block, 'zh', [(0, 1), (1, 0)])  10.8 us
    dot_general x1, matrix products, shards(): lax.dot_general(grad_local, weight, (((1,), (1,)), ((), ())), preferred_e...  7.23 us
    dot_general x1, matrix products, shards(): jnp.dot(stacked, weight, preferred_element_type=f32).astype(bf16)  6.5 us
    all_gather x1, waiting for transfers between devices, shards(): weight = lax.all_gather(weight_in, gx, axis=0, tiled=True)  5.78 us
  transfers between devices with their start and end apart: 10, of which 8 were waited for; matrix products, arithmetic and copies ran while one was open for 13% of the time, Pallas kernels for 0%

profile of v5, /device:TPU:1, one launch (start us, length us, event | category | flops | bytes accessed | tf_op | source)
XLA Modules:
  0.0 221.2 jit_solution(8772823345659891739)
XLA Ops:
  7.9 1.6 broadcast_in_dim.14
  9.5 13.1 %all-to-all-start = ((bf16[8,16,1536]{2,1,0:T(8,128)(2,1)}), bf16[8,16,1536]{2,1,0:T(8,128)(2,1)S(1)}, u32[]{:S(2)}, u32[]{:S(2)}) async-start(bf16[8,16,1536]{2,1,0:T(8,128)(2,1)} %broadcast_in_dim.14), calls=%async_computation | async-start | bytes 786432 | tf_op jit(solution)/shard_map/all_to_all | solution.py:28
  22.5 7.9 %collective-permute-start = (bf16[16,3072]{1,0:T(8,128)(2,1)}, bf16[16,3072]{1,0:T(8,128)(2,1)S(1)}, u32[]{:S(2)}, u32[]{:S(2)}) collective-permute-start(bf16[16,3072]{1,0:T(8,128)(2,1)} %param.11), channel_id=1, source_target_pairs={{0,32},{32,0},{1,33},{33,1},{2,34},{34,2},{3,35},{35,3},{4,36},{36... | collective-permute-start | bytes 294920 | tf_op jit(solution)/shard_map/ppermute | solution.py:37
  32.0 6.2 %collective-permute-done = bf16[16,3072]{1,0:T(8,128)(2,1)S(1)} collective-permute-done((bf16[16,3072]{1,0:T(8,128)(2,1)}, bf16[16,3072]{1,0:T(8,128)(2,1)S(1)}, u32[]{:S(2)}, u32[]{:S(2)}) %collective-permute-start) | collective-permute-done | bytes 98336 | tf_op jit(solution)/shard_map/ppermute | solution.py:37
  39.3 5.8 %all-to-all-done = bf16[8,16,1536]{2,1,0:T(8,128)(2,1)S(1)} async-done(((bf16[8,16,1536]{2,1,0:T(8,128)(2,1)}), bf16[8,16,1536]{2,1,0:T(8,128)(2,1)S(1)}, u32[]{:S(2)}, u32[]{:S(2)}) %all-to-all-start) | async-done | bytes 393248 | tf_op jit(solution)/shard_map/all_to_all | solution.py:28
  46.3 9.8 %all-to-all-start.1 = ((f32[8,2,128]{2,1,0:T(2,128)}), f32[8,2,128]{2,1,0:T(2,128)S(1)}, u32[]{:S(2)}, u32[]{:S(2)}) async-start(f32[8,2,128]{2,1,0:T(2,128)} %broadcast_in_dim.15), calls=%async_computation.1 | async-start | bytes 16384 | tf_op jit(solution)/shard_map/all_to_all | solution.py:28
  56.3 13.6 %all-to-all-done.1 = f32[8,2,128]{2,1,0:T(2,128)S(1)} async-done(((f32[8,2,128]{2,1,0:T(2,128)}), f32[8,2,128]{2,1,0:T(2,128)S(1)}, u32[]{:S(2)}, u32[]{:S(2)}) %all-to-all-start.1) | async-done | bytes 8224 | tf_op jit(solution)/shard_map/all_to_all | solution.py:28
  70.1 0.9 fusion.6
  71.9 5.8 %all-gather.4.cloned.1.call-done = bf16[1536,3072]{1,0:T(8,128)(2,1)} async-done(((bf16[192,3072]{1,0:T(8,128)(2,1)}), bf16[1536,3072]{1,0:T(8,128)(2,1)}) %all-gather.4.cloned.1.call-update) | async-done | bytes 9437200 | tf_op jit(solution)/shard_map/all_gather | solution.py:54
  77.7 6.5 %convolution_convert_fusion.1 = bf16[160,3072]{1,0:T(8,128)(2,1)} fusion(bf16[160,1536]{1,0:T(8,128)(2,1)} %bitcast.74, bf16[1536,3072]{1,0:T(8,128)(2,1)} %all-gather.4.cloned.1.call-done), kind=kOutput, calls=%fused_computation.1 | convolution fusion | flops 1510440960 | bytes 10911744 | tf_op jit(solution)/shard_map/dot_general | solution.py:97
  84.2 4.0 %all-to-all-start.2 = ((bf16[4,40,3072]{2,1,0:T(8,128)(2,1)}), bf16[4,40,3072]{2,1,0:T(8,128)(2,1)S(1)}, u32[]{:S(2)}, u32[]{:S(2)}) async-start(bf16[4,40,3072]{2,1,0:T(8,128)(2,1)} %bitcast.12), calls=%async_computation.2 | async-start | bytes 1966080 | tf_op jit(solution)/shard_map/all_to_all | solution.py:28
  88.2 9.4 %all-to-all-done.2 = bf16[4,40,3072]{2,1,0:T(8,128)(2,1)S(1)} async-done(((bf16[4,40,3072]{2,1,0:T(8,128)(2,1)}), bf16[4,40,3072]{2,1,0:T(8,128)(2,1)S(1)}, u32[]{:S(2)}, u32[]{:S(2)}) %all-to-all-start.2) | async-done | bytes 983072 | tf_op jit(solution)/shard_map/all_to_all | solution.py:28
  97.7 17.1 %collective-permute-start.1 = (bf16[40,3072]{1,0:T(8,128)(2,1)S(1)}, bf16[40,3072]{1,0:T(8,128)(2,1)S(1)}, u32[]{:S(2)}, u32[]{:S(2)}) collective-permute-start(bf16[40,3072]{1,0:T(8,128)(2,1)S(1)} %reduce-precision_convert_fusion), channel_id=1, source_target_pairs={{0,32},{32,0},{1,33},{33,1},{2,34},{34,2},{3,35},{35,3},{4,36},{36... | collective-permute-start | bytes 737288 | tf_op jit(solution)/shard_map/ppermute | solution.py:37
  114.9 4.7 %collective-permute-done.1 = bf16[40,3072]{1,0:T(8,128)(2,1)S(1)} collective-permute-done((bf16[40,3072]{1,0:T(8,128)(2,1)S(1)}, bf16[40,3072]{1,0:T(8,128)(2,1)S(1)}, u32[]{:S(2)}, u32[]{:S(2)}) %collective-permute-start.1) | collective-permute-done | bytes 245792 | tf_op jit(solution)/shard_map/ppermute | solution.py:37
  120.3 11.8 %all_to_all.30 = bf16[4,40,3072]{2,1,0:T(8,128)(2,1)S(1)} all-to-all(bf16[4,40,3072]{2,1,0:T(8,128)(2,1)S(1)} %broadcast_in_dim.17), channel_id=1, replica_groups=mesh['y'=4,'core'=2,'zh'=2,'x'=4,'gz'=8] {'x'}, dimensions={0} | all-to-all | bytes 1966080 | tf_op jit(solution)/shard_map/all_to_all | solution.py:28
  132.1 0.9 slice.107
  133.1 7.2 %fusion.2 = (bf16[1536]{0:T(1024)(128)(2,1)S(1)}, bf16[1536]{0:T(1024)(128)(2,1)S(1)}, bf16[128,1536]{1,0:T(8,128)(2,1)S(1)}) fusion(f32[4,2,16,1536]{3,2,1,0:T(8,128)S(1)} %copy.50, f32[128]{0:T(128)S(1)} %add_rsqrt_fusion, f32[128]{0:T(128)S(1)} %broadcast_multiply_fusion.1, bf16[128,3072]{1,0:T(8,128)(2,1)} %bitcast.70, ...), kind=kOutput, calls=%fused_computation.8 | convolution fusion | flops 1209136128 | bytes 11410432 | tf_op jit(solution)/shard_map/dot_general | solution.py:125
  140.8 0.9 concatenate.28
  141.7 28.4 %all-to-all-start.4 = ((bf16[8,16,1792]{2,1,0:T(8,128)(2,1)}), bf16[8,16,1792]{2,1,0:T(8,128)(2,1)S(1)}, u32[]{:S(2)}, u32[]{:S(2)}) async-start(bf16[8,16,1792]{2,1,0:T(8,128)(2,1)} %concatenate.28), calls=%async_computation.4 | async-start | bytes 917504 | tf_op jit(solution)/shard_map/all_to_all | solution.py:28
  170.3 1.5 constant_dynamic-slice_fusion
  172.0 17.1 %all-to-all-done.4 = bf16[8,16,1792]{2,1,0:T(8,128)(2,1)S(1)} async-done(((bf16[8,16,1792]{2,1,0:T(8,128)(2,1)}), bf16[8,16,1792]{2,1,0:T(8,128)(2,1)S(1)}, u32[]{:S(2)}, u32[]{:S(2)}) %all-to-all-start.4) | async-done | bytes 458784 | tf_op jit(solution)/shard_map/all_to_all | solution.py:28
  190.0 12.4 %all-to-all-start.5 = ((f32[8,48,128]{2,1,0:T(8,128)}), f32[8,48,128]{2,1,0:T(8,128)S(1)}, u32[]{:S(2)}, u32[]{:S(2)}) async-start(f32[8,48,128]{2,1,0:T(8,128)} %broadcast_in_dim.20), calls=%async_computation.5 | async-start | bytes 393216 | tf_op jit(solution)/shard_map/all_to_all | solution.py:28
  203.3 5.0 %all-to-all-done.5 = f32[8,48,128]{2,1,0:T(8,128)S(1)} async-done(((f32[8,48,128]{2,1,0:T(8,128)}), f32[8,48,128]{2,1,0:T(8,128)S(1)}, u32[]{:S(2)}, u32[]{:S(2)}) %all-to-all-start.5) | async-done | bytes 196640 | tf_op jit(solution)/shard_map/all_to_all | solution.py:28
  209.5 5.2 %convolution_convert_fusion = bf16[192,3072]{1,0:T(8,128)(2,1)} fusion(bf16[1024,192]{1,0:T(8,128)(2,1)S(1)} %bitcast.75, bf16[1024,3072]{1,0:T(8,128)(2,1)} %all-gather.8.cloned.1.call-done), kind=kOutput, calls=%fused_computation | convolution fusion | flops 1208549376 | bytes 7864320 | tf_op jit(solution)/shard_map/dot_general | solution.py:179
  (84 shorter events, 9.8 us)
Async XLA Ops:
  7.2 70.5 %all-gather.4.cloned.1.call-start = ((), (), s32[]{:S(2)}) async-start(), calls=%async_computation.6 | async-start | bytes 10616832 | tf_op jit(solution)/shard_map/all_gather | solution.py:54
  9.5 35.6 %all-to-all-start = ((bf16[8,16,1536]{2,1,0:T(8,128)(2,1)}), bf16[8,16,1536]{2,1,0:T(8,128)(2,1)S(1)}, u32[]{:S(2)}, u32[]{:S(2)}) async-start(bf16[8,16,1536]{2,1,0:T(8,128)(2,1)} %broadcast_in_dim.14), calls=%async_computation | async-start | bytes 786432 | tf_op jit(solution)/shard_map/all_to_all | solution.py:28
  22.5 15.6 %collective-permute-start = (bf16[16,3072]{1,0:T(8,128)(2,1)}, bf16[16,3072]{1,0:T(8,128)(2,1)S(1)}, u32[]{:S(2)}, u32[]{:S(2)}) collective-permute-start(bf16[16,3072]{1,0:T(8,128)(2,1)} %param.11), channel_id=1, source_target_pairs={{0,32},{32,0},{1,33},{33,1},{2,34},{34,2},{3,35},{35,3},{4,36},{36... | collective-permute-start | bytes 294920 | tf_op jit(solution)/shard_map/ppermute | solution.py:37
  46.3 23.5 %all-to-all-start.1 = ((f32[8,2,128]{2,1,0:T(2,128)}), f32[8,2,128]{2,1,0:T(2,128)S(1)}, u32[]{:S(2)}, u32[]{:S(2)}) async-start(f32[8,2,128]{2,1,0:T(2,128)} %broadcast_in_dim.15), calls=%async_computation.1 | async-start | bytes 16384 | tf_op jit(solution)/shard_map/all_to_all | solution.py:28
  56.1 114.2 %all-gather.6.cloned.1.call-start = ((), (), s32[]{:S(2)}) async-start(), calls=%async_computation.7 | async-start | bytes 4423680 | tf_op jit(solution)/shard_map/all_gather | solution.py:96
  71.9 43.0 %copy-start.1 = (bf16[16,3072]{1,0:T(8,128)(2,1)S(1)}, bf16[16,3072]{1,0:T(8,128)(2,1)}, u32[]{:S(2)}) copy-start(bf16[16,3072]{1,0:T(8,128)(2,1)} %param.11) | copy-start | bytes 294916
  71.9 47.8 %copy-start.3 = (f32[3072]{0:T(1024)S(1)}, f32[3072]{0:T(1024)}, u32[]{:S(2)}) copy-start(f32[3072]{0:T(1024)} %param.10) | copy-start | bytes 36868
  84.2 13.4 %all-to-all-start.2 = ((bf16[4,40,3072]{2,1,0:T(8,128)(2,1)}), bf16[4,40,3072]{2,1,0:T(8,128)(2,1)S(1)}, u32[]{:S(2)}, u32[]{:S(2)}) async-start(bf16[4,40,3072]{2,1,0:T(8,128)(2,1)} %bitcast.12), calls=%async_computation.2 | async-start | bytes 1966080 | tf_op jit(solution)/shard_map/all_to_all | solution.py:28
  88.2 121.3 %all-gather.8.cloned.1.call-start = ((), (), s32[]{:S(2)}) async-start(), calls=%async_computation.8 | async-start | bytes 7077888 | tf_op jit(solution)/shard_map/all_gather | solution.py:123
  97.7 21.8 %collective-permute-start.1 = (bf16[40,3072]{1,0:T(8,128)(2,1)S(1)}, bf16[40,3072]{1,0:T(8,128)(2,1)S(1)}, u32[]{:S(2)}, u32[]{:S(2)}) collective-permute-start(bf16[40,3072]{1,0:T(8,128)(2,1)S(1)} %reduce-precision_convert_fusion), channel_id=1, source_target_pairs={{0,32},{32,0},{1,33},{33,1},{2,34},{34,2},{3,35},{35,3},{4,36},{36... | collective-permute-start | bytes 737288 | tf_op jit(solution)/shard_map/ppermute | solution.py:37
  140.3 62.2 %copy-start = (bf16[16,1536]{1,0:T(8,128)(2,1)S(1)}, bf16[16,1536]{1,0:T(8,128)(2,1)}, u32[]{:S(2)}) copy-start(bf16[16,1536]{1,0:T(8,128)(2,1)} %param.6) | copy-start | bytes 147460
  140.3 62.2 %copy-start.2 = (f32[1536]{0:T(1024)S(1)}, f32[1536]{0:T(1024)}, u32[]{:S(2)}) copy-start(f32[1536]{0:T(1024)} %param.7) | copy-start | bytes 18436
  141.7 47.5 %all-to-all-start.4 = ((bf16[8,16,1792]{2,1,0:T(8,128)(2,1)}), bf16[8,16,1792]{2,1,0:T(8,128)(2,1)S(1)}, u32[]{:S(2)}, u32[]{:S(2)}) async-start(bf16[8,16,1792]{2,1,0:T(8,128)(2,1)} %concatenate.28), calls=%async_computation.4 | async-start | bytes 917504 | tf_op jit(solution)/shard_map/all_to_all | solution.py:28
  190.0 18.3 %all-to-all-start.5 = ((f32[8,48,128]{2,1,0:T(8,128)}), f32[8,48,128]{2,1,0:T(8,128)S(1)}, u32[]{:S(2)}, u32[]{:S(2)}) async-start(f32[8,48,128]{2,1,0:T(8,128)} %broadcast_in_dim.20), calls=%async_computation.5 | async-start | bytes 393216 | tf_op jit(solution)/shard_map/all_to_all | solution.py:28
Sparse Core Ops, SparseCore 0:
  10.1 67.5 all-gather.3
  79.8 38.9 all-gather.5
  133.2 66.1 all-gather.7

commit v6 on v5

--- a/solution.py
+++ b/solution.py
@@ -94,25 +94,37 @@
     )
     stacked = stacked.reshape(-1, width)
     all_stacked = lax.all_gather(stacked, gx, axis=0, tiled=True)
-    partial_hidden = jnp.dot(stacked, weight, preferred_element_type=f32).astype(bf16)
-    arrived = exchange(partial_hidden.reshape(around, block + extra_rows, hidden_width), "x")
-    half_sum = lax.reduce_precision(jnp.sum(arrived.astype(f32), axis=0), 8, 7)
-    products = half_sum + swap(half_sum.astype(bf16)).astype(f32)
-    product = products[:block]
-    gain_product = products[block] + products[block + 1]
-    bias_product = products[block + 2] + products[block + 3]
-    grad_pre = (cotangent * gelu_slope(product + up_bias)).astype(bf16)
-    grad_pre_float = grad_pre.astype(f32)
-    token_sums = jnp.stack(
-        [
-            jnp.sum(grad_pre_float * gain_product, axis=1),
-            jnp.sum(grad_pre_float * (product - bias_product), axis=1),
-        ]
-    )
-    token_rows = jnp.concatenate(split_float(token_sums)).astype(bf16)
-    token_rows = jnp.pad(token_rows, ((0, extra_rows - 4), (0, hidden_width - block)))
-    around_rows = spread(jnp.concatenate([grad_pre, token_rows]), "x")
-    grad_local = around_rows[:, :block].reshape(local, hidden_width)
+    pieces = 2
+    piece = hidden_width // pieces
+    local_parts, sums_parts = [], []
+    for index in range(pieces):
+        span = slice(index * piece, (index + 1) * piece)
+        partial_hidden = jnp.dot(stacked, weight[:, span], preferred_element_type=f32).astype(bf16)
+        arrived = exchange(partial_hidden.reshape(around, block + extra_rows, piece), "x")
+        half_sum = lax.reduce_precision(jnp.sum(arrived.astype(f32), axis=0), 8, 7)
+        products = half_sum + swap(half_sum.astype(bf16)).astype(f32)
+        if index:
+            products = products + 0.0 * local_parts[-1][0, 0].astype(f32)
+        product = products[:block]
+        gain_product = products[block] + products[block + 1]
+        bias_product = products[block + 2] + products[block + 3]
+        grad_pre = (cotangent[:, span] * gelu_slope(product + up_bias[span])).astype(bf16)
+        grad_pre_float = grad_pre.astype(f32)
+        sums_parts.append(
+            jnp.stack(
+                [
+                    jnp.sum(grad_pre_float * gain_product, axis=1),
+                    jnp.sum(grad_pre_float * (product - bias_product), axis=1),
+                ]
+            )
+        )
+        if index == pieces - 1:
+            token_rows = jnp.concatenate(split_float(sum(sums_parts))).astype(bf16)
+            token_rows = jnp.pad(token_rows, ((0, extra_rows - 4), (0, piece - block)))
+            grad_pre = jnp.concatenate([grad_pre, token_rows])
+        around_rows = spread(grad_pre, "x")
+        local_parts.append(around_rows[:, :block].reshape(local, piece))
+    grad_local = jnp.concatenate(local_parts, axis=1)
     token_parts = (
         around_rows[:, block : block + 4, :block]
         .reshape(around, 4, halves, rows)
@@ -179,6 +191,7 @@
     grad_weight = lax.dot_general(
         feature_rows, portion, (((0,), (0,)), ((), ())), preferred_element_type=f32
     ).astype(bf16)
+    grad_up_bias = grad_up_bias + 0.0 * grad_weight[0, 0].astype(f32)
     return (grad_inputs, grad_weight, grad_up_bias, grad_ln_gain, grad_ln_bias)
 
 

time: 222 us -> 224 us (level)
  waiting for transfers between devices: 68.2 us -> 63.7 us
  starting transfers between devices: 92.7 us -> 96.7 us
    ppermute x2 -> x3, starting transfers between devices: 25 us -> 38.7 us  [swap(): return lax.ppermute(block, 'zh', [(0, 1), (1, 0)])]
    all_to_all x5 -> x7, starting transfers between devices: 67.6 us -> 57.9 us  [exchange(): return lax.all_to_all(blocks, axis, split_axis=0, concat_axis=0, tiled=True)]
    all_to_all x5 -> x7, waiting for transfers between devices: 50.8 us -> 44.2 us  [exchange(): return lax.all_to_all(blocks, axis, split_axis=0, concat_axis=0, tiled=True)]
    dot_general x1 -> x2, matrix products: 6.5 us -> 8.26 us  [shards(): jnp.dot(stacked, weight[:, span], preferred_element_type=f32).astype(bf16)]
    ppermute x2 -> x3, waiting for transfers between devices: 10.8 us -> 12.4 us  [swap(): return lax.ppermute(block, 'zh', [(0, 1), (1, 0)])]
  transfers between devices with their start and end apart: 10 -> 13, of which waited for: 8 -> 9; matrix products, arithmetic and copies ran while one was open for 13% -> 14% of each run, Pallas kernels for 0% -> 0%
where the time goes in v6:
time: 224 us; the launch traced here: 223 us
  starting transfers between devices  96.7 us (43%)
  waiting for transfers between devices  63.7 us (28%)
  matrix products  19.4 us (9%)
  between operations  16.1 us (7%)
  blocking collectives  10.8 us (5%)
  local copies, waits for them, and re-layouts  9.45 us (4%)
  other arithmetic  6.71 us (3%)
    all_to_all x7, starting transfers between devices, exchange(): return lax.all_to_all(blocks, axis, split_axis=0, concat_axis=0, tiled=True)  57.9 us
    all_to_all x7, waiting for transfers between devices, exchange(): return lax.all_to_all(blocks, axis, split_axis=0, concat_axis=0, tiled=True)  44.2 us
    ppermute x3, starting transfers between devices, swap(): return lax.ppermute(block, 'zh', [(0, 1), (1, 0)])  38.7 us
    ppermute x3, waiting for transfers between devices, swap(): return lax.ppermute(block, 'zh', [(0, 1), (1, 0)])  12.4 us
    all_to_all x1, blocking collectives, exchange(): return lax.all_to_all(blocks, axis, split_axis=0, concat_axis=0, tiled=True)  10.8 us
    dot_general x2, matrix products, shards(): jnp.dot(stacked, weight[:, span], preferred_element_type=f32).astype(bf16)  8.26 us
    dot_general x1, matrix products, shards(): lax.dot_general(grad_local, weight, (((1,), (1,)), ((), ())), preferred_e...  6.95 us
    all_gather x1, waiting for transfers between devices, shards(): weight = lax.all_gather(weight_in, gx, axis=0, tiled=True)  6.4 us
  transfers between devices with their start and end apart: 13, of which 9 were waited for; matrix products, arithmetic and copies ran while one was open for 14% of the time, Pallas kernels for 0%

profile of v6, /device:TPU:1, one launch (start us, length us, event | category | flops | bytes accessed | tf_op | source)
XLA Modules:
  0.0 222.9 jit_solution(17538070253402201052)
XLA Ops:
  9.5 13.1 %all-to-all-start = ((bf16[8,16,1536]{2,1,0:T(8,128)(2,1)}), bf16[8,16,1536]{2,1,0:T(8,128)(2,1)S(1)}, u32[]{:S(2)}, u32[]{:S(2)}) async-start(bf16[8,16,1536]{2,1,0:T(8,128)(2,1)} %broadcast_in_dim.16), calls=%async_computation | async-start | bytes 786432 | tf_op jit(solution)/shard_map/all_to_all | solution.py:28
  22.6 7.9 %collective-permute-start = (bf16[16,3072]{1,0:T(8,128)(2,1)}, bf16[16,3072]{1,0:T(8,128)(2,1)S(1)}, u32[]{:S(2)}, u32[]{:S(2)}) collective-permute-start(bf16[16,3072]{1,0:T(8,128)(2,1)} %param.11), channel_id=1, source_target_pairs={{0,32},{32,0},{1,33},{33,1},{2,34},{34,2},{3,35},{35,3},{4,36},{36... | collective-permute-start | bytes 294920 | tf_op jit(solution)/shard_map/ppermute | solution.py:37
  32.0 6.2 %collective-permute-done = bf16[16,3072]{1,0:T(8,128)(2,1)S(1)} collective-permute-done((bf16[16,3072]{1,0:T(8,128)(2,1)}, bf16[16,3072]{1,0:T(8,128)(2,1)S(1)}, u32[]{:S(2)}, u32[]{:S(2)}) %collective-permute-start) | collective-permute-done | bytes 98336 | tf_op jit(solution)/shard_map/ppermute | solution.py:37
  39.4 5.8 %all-to-all-done = bf16[8,16,1536]{2,1,0:T(8,128)(2,1)S(1)} async-done(((bf16[8,16,1536]{2,1,0:T(8,128)(2,1)}), bf16[8,16,1536]{2,1,0:T(8,128)(2,1)S(1)}, u32[]{:S(2)}, u32[]{:S(2)}) %all-to-all-start) | async-done | bytes 393248 | tf_op jit(solution)/shard_map/all_to_all | solution.py:28
  46.4 9.8 %all-to-all-start.1 = ((f32[8,2,128]{2,1,0:T(2,128)}), f32[8,2,128]{2,1,0:T(2,128)S(1)}, u32[]{:S(2)}, u32[]{:S(2)}) async-start(f32[8,2,128]{2,1,0:T(2,128)} %broadcast_in_dim.17), calls=%async_computation.1 | async-start | bytes 16384 | tf_op jit(solution)/shard_map/all_to_all | solution.py:28
  56.3 13.6 %all-to-all-done.1 = f32[8,2,128]{2,1,0:T(2,128)S(1)} async-done(((f32[8,2,128]{2,1,0:T(2,128)}), f32[8,2,128]{2,1,0:T(2,128)S(1)}, u32[]{:S(2)}, u32[]{:S(2)}) %all-to-all-start.1) | async-done | bytes 8224 | tf_op jit(solution)/shard_map/all_to_all | solution.py:28
  71.4 6.4 %all-gather.4.cloned.1.call-done = bf16[1536,3072]{1,0:T(8,128)(2,1)} async-done(((bf16[192,3072]{1,0:T(8,128)(2,1)}), bf16[1536,3072]{1,0:T(8,128)(2,1)}) %all-gather.4.cloned.1.call-update) | async-done | bytes 9437200 | tf_op jit(solution)/shard_map/all_gather | solution.py:54
  77.8 4.2 %fusion.4 = bf16[160,1536]{1,0:T(8,128)(2,1)} fusion(bf16[160,1536]{1,0:T(8,128)(2,1)} %bitcast.84, bf16[1536,3072]{1,0:T(8,128)(2,1)} %all-gather.4.cloned.1.call-done), kind=kOutput, calls=%fused_computation.5 | convolution fusion | flops 755220480 | bytes 5701632 | tf_op jit(solution)/shard_map/dot_general | solution.py:102
  82.0 4.0 %all-to-all-start.2 = ((bf16[4,40,1536]{2,1,0:T(8,128)(2,1)}), bf16[4,40,1536]{2,1,0:T(8,128)(2,1)S(1)}, u32[]{:S(2)}, u32[]{:S(2)}) async-start(bf16[4,40,1536]{2,1,0:T(8,128)(2,1)} %bitcast.12), calls=%async_computation.2 | async-start | bytes 983040 | tf_op jit(solution)/shard_map/all_to_all | solution.py:28
  85.9 4.1 %fusion.7 = bf16[160,1536]{1,0:T(8,128)(2,1)} fusion(bf16[160,1536]{1,0:T(8,128)(2,1)S(1)} %bitcast.85, bf16[1536,3072]{1,0:T(8,128)(2,1)} %all-gather.4.cloned.1.call-done), kind=kOutput, calls=%fused_computation.6 | convolution fusion | flops 755220480 | bytes 5701632 | tf_op jit(solution)/shard_map/dot_general | solution.py:102
  90.0 2.7 %all-to-all-done.2 = bf16[4,40,1536]{2,1,0:T(8,128)(2,1)S(1)} async-done(((bf16[4,40,1536]{2,1,0:T(8,128)(2,1)}), bf16[4,40,1536]{2,1,0:T(8,128)(2,1)S(1)}, u32[]{:S(2)}, u32[]{:S(2)}) %all-to-all-start.2) | async-done | bytes 491552 | tf_op jit(solution)/shard_map/all_to_all | solution.py:28
  92.7 3.5 %all-to-all-start.4 = ((bf16[4,40,1536]{2,1,0:T(8,128)(2,1)}), bf16[4,40,1536]{2,1,0:T(8,128)(2,1)S(1)}, u32[]{:S(2)}, u32[]{:S(2)}) async-start(bf16[4,40,1536]{2,1,0:T(8,128)(2,1)} %bitcast.14), calls=%async_computation.4 | async-start | bytes 983040 | tf_op jit(solution)/shard_map/all_to_all | solution.py:28
  96.3 14.5 %collective-permute-start.1 = (bf16[40,1536]{1,0:T(8,128)(2,1)S(1)}, bf16[40,1536]{1,0:T(8,128)(2,1)S(1)}, u32[]{:S(2)}, u32[]{:S(2)}) collective-permute-start(bf16[40,1536]{1,0:T(8,128)(2,1)S(1)} %reduce-precision_convert_fusion.1), channel_id=1, source_target_pairs={{0,32},{32,0},{1,33},{33,1},{2,34},{34,2},{3,35},{35,3},{4,36},{36... | collective-permute-start | bytes 368648 | tf_op jit(solution)/shard_map/ppermute | solution.py:37
  110.9 2.3 %collective-permute-done.1 = bf16[40,1536]{1,0:T(8,128)(2,1)S(1)} collective-permute-done((bf16[40,1536]{1,0:T(8,128)(2,1)S(1)}, bf16[40,1536]{1,0:T(8,128)(2,1)S(1)}, u32[]{:S(2)}, u32[]{:S(2)}) %collective-permute-start.1) | collective-permute-done | bytes 122912 | tf_op jit(solution)/shard_map/ppermute | solution.py:37
  114.3 4.2 %all-to-all-start.3 = ((bf16[4,32,1536]{2,1,0:T(8,128)(2,1)}), bf16[4,32,1536]{2,1,0:T(8,128)(2,1)S(1)}, u32[]{:S(2)}, u32[]{:S(2)}) async-start(bf16[4,32,1536]{2,1,0:T(8,128)(2,1)} %broadcast_in_dim.19), calls=%async_computation.3 | async-start | bytes 786432 | tf_op jit(solution)/shard_map/all_to_all | solution.py:28
  118.5 16.3 %collective-permute-start.2 = (bf16[40,1536]{1,0:T(8,128)(2,1)S(1)}, bf16[40,1536]{1,0:T(8,128)(2,1)S(1)}, u32[]{:S(2)}, u32[]{:S(2)}) collective-permute-start(bf16[40,1536]{1,0:T(8,128)(2,1)S(1)} %reduce-precision_convert_fusion), channel_id=1, source_target_pairs={{0,32},{32,0},{1,33},{33,1},{2,34},{34,2},{3,35},{35,3},{4,36},{36... | collective-permute-start | bytes 368648 | tf_op jit(solution)/shard_map/ppermute | solution.py:37
  136.0 3.9 %collective-permute-done.2 = bf16[40,1536]{1,0:T(8,128)(2,1)S(1)} collective-permute-done((bf16[40,1536]{1,0:T(8,128)(2,1)S(1)}, bf16[40,1536]{1,0:T(8,128)(2,1)S(1)}, u32[]{:S(2)}, u32[]{:S(2)}) %collective-permute-start.2) | collective-permute-done | bytes 122912 | tf_op jit(solution)/shard_map/ppermute | solution.py:37
  140.4 10.8 %all_to_all.40 = bf16[4,40,1536]{2,1,0:T(8,128)(2,1)S(1)} all-to-all(bf16[4,40,1536]{2,1,0:T(8,128)(2,1)S(1)} %broadcast_in_dim.20), channel_id=1, replica_groups=mesh['y'=4,'core'=2,'zh'=2,'x'=4,'gz'=8] {'x'}, dimensions={0} | all-to-all | bytes 983040 | tf_op jit(solution)/shard_map/all_to_all | solution.py:28
  152.2 7.0 %fusion.12 = (bf16[1536]{0:T(1024)(128)(2,1)S(1)}, bf16[1536]{0:T(1024)(128)(2,1)S(1)}, bf16[128,1536]{1,0:T(8,128)(2,1)S(1)}) fusion(f32[4,2,16,1536]{3,2,1,0:T(8,128)S(1)} %copy.50, f32[128]{0:T(128)S(1)} %add_rsqrt_fusion, f32[128]{0:T(128)S(1)} %broadcast_multiply_fusion.1, bf16[1536,3072]{1,0:T(8,128)(2,1)} %all-gather.4.cloned.1.call-done, ...), kind=kOutput, calls=%fused_computation.15 | convolution fusion | flops 1210708992 | bytes 11410432 | tf_op jit(solution)/shard_map/dot_general | solution.py:137
  160.5 10.2 %all-to-all-start.6 = ((bf16[8,16,1792]{2,1,0:T(8,128)(2,1)}), bf16[8,16,1792]{2,1,0:T(8,128)(2,1)S(1)}, u32[]{:S(2)}, u32[]{:S(2)}) async-start(bf16[8,16,1792]{2,1,0:T(8,128)(2,1)} %concatenate.32), calls=%async_computation.6 | async-start | bytes 917504 | tf_op jit(solution)/shard_map/all_to_all | solution.py:28
  172.6 17.2 %all-to-all-done.6 = bf16[8,16,1792]{2,1,0:T(8,128)(2,1)S(1)} async-done(((bf16[8,16,1792]{2,1,0:T(8,128)(2,1)}), bf16[8,16,1792]{2,1,0:T(8,128)(2,1)S(1)}, u32[]{:S(2)}, u32[]{:S(2)}) %all-to-all-start.6) | async-done | bytes 458784 | tf_op jit(solution)/shard_map/all_to_all | solution.py:28
  190.7 13.2 %all-to-all-start.7 = ((f32[8,48,128]{2,1,0:T(8,128)}), f32[8,48,128]{2,1,0:T(8,128)S(1)}, u32[]{:S(2)}, u32[]{:S(2)}) async-start(f32[8,48,128]{2,1,0:T(8,128)} %broadcast_in_dim.23), calls=%async_computation.7 | async-start | bytes 393216 | tf_op jit(solution)/shard_map/all_to_all | solution.py:28
  204.8 5.0 %all-to-all-done.7 = f32[8,48,128]{2,1,0:T(8,128)S(1)} async-done(((f32[8,48,128]{2,1,0:T(8,128)}), f32[8,48,128]{2,1,0:T(8,128)S(1)}, u32[]{:S(2)}, u32[]{:S(2)}) %all-to-all-start.7) | async-done | bytes 196640 | tf_op jit(solution)/shard_map/all_to_all | solution.py:28
  210.4 4.2 %convolution_convert_fusion = bf16[192,3072]{1,0:T(8,128)(2,1)S(1)} fusion(bf16[1024,192]{1,0:T(8,128)(2,1)S(1)} %bitcast.81, bf16[1024,3072]{1,0:T(8,128)(2,1)} %all-gather.8.cloned.1.call-done), kind=kOutput, calls=%fused_computation.4 | convolution fusion | flops 1208549376 | bytes 7864320 | tf_op jit(solution)/shard_map/dot_general | solution.py:191
  (109 shorter events, 17.0 us)
Async XLA Ops:
  7.2 64.1 %copy-start.3 = (bf16[16,3072]{1,0:T(8,128)(2,1)S(1)}, bf16[16,3072]{1,0:T(8,128)(2,1)}, u32[]{:S(2)}) copy-start(bf16[16,3072]{1,0:T(8,128)(2,1)} %param.11) | copy-start | bytes 294916
  7.2 63.0 %copy-start.5 = (f32[1536]{0:T(1024)S(1)}, f32[1536]{0:T(1024)}, u32[]{:S(2)}) copy-start(f32[1536]{0:T(1024)} %param.8) | copy-start | bytes 18436
  7.2 63.0 %copy-start.4 = (f32[1536]{0:T(1024)S(1)}, f32[1536]{0:T(1024)}, u32[]{:S(2)}) copy-start(f32[1536]{0:T(1024)} %param.7) | copy-start | bytes 18436
  7.2 64.0 %copy-start.6 = (f32[3072]{0:T(1024)S(1)}, f32[3072]{0:T(1024)}, u32[]{:S(2)}) copy-start(f32[3072]{0:T(1024)} %param.10) | copy-start | bytes 36868
  7.2 70.5 %all-gather.4.cloned.1.call-start = ((), (), s32[]{:S(2)}) async-start(), calls=%async_computation.8 | async-start | bytes 10616832 | tf_op jit(solution)/shard_map/all_gather | solution.py:54
  9.5 35.6 %all-to-all-start = ((bf16[8,16,1536]{2,1,0:T(8,128)(2,1)}), bf16[8,16,1536]{2,1,0:T(8,128)(2,1)S(1)}, u32[]{:S(2)}, u32[]{:S(2)}) async-start(bf16[8,16,1536]{2,1,0:T(8,128)(2,1)} %broadcast_in_dim.16), calls=%async_computation | async-start | bytes 786432 | tf_op jit(solution)/shard_map/all_to_all | solution.py:28
  22.6 15.6 %collective-permute-start = (bf16[16,3072]{1,0:T(8,128)(2,1)}, bf16[16,3072]{1,0:T(8,128)(2,1)S(1)}, u32[]{:S(2)}, u32[]{:S(2)}) collective-permute-start(bf16[16,3072]{1,0:T(8,128)(2,1)} %param.11), channel_id=1, source_target_pairs={{0,32},{32,0},{1,33},{33,1},{2,34},{34,2},{3,35},{35,3},{4,36},{36... | collective-permute-start | bytes 294920 | tf_op jit(solution)/shard_map/ppermute | solution.py:37
  46.4 23.5 %all-to-all-start.1 = ((f32[8,2,128]{2,1,0:T(2,128)}), f32[8,2,128]{2,1,0:T(2,128)S(1)}, u32[]{:S(2)}, u32[]{:S(2)}) async-start(f32[8,2,128]{2,1,0:T(2,128)} %broadcast_in_dim.17), calls=%async_computation.1 | async-start | bytes 16384 | tf_op jit(solution)/shard_map/all_to_all | solution.py:28
  56.1 114.8 %all-gather.6.cloned.1.call-start = ((), (), s32[]{:S(2)}) async-start(), calls=%async_computation.9 | async-start | bytes 4423680 | tf_op jit(solution)/shard_map/all_gather | solution.py:96
  71.3 14.7 %copy-start = (bf16[4,40,1536]{2,1,0:T(8,128)(2,1)S(1)}, bf16[4,40,1536]{2,1,0:T(8,128)(2,1)}, u32[]{:S(2)}) copy-start(bf16[4,40,1536]{2,1,0:T(8,128)(2,1)} %pad_maximum_fusion.1) | copy-start | bytes 1474564
  82.0 10.7 %all-to-all-start.2 = ((bf16[4,40,1536]{2,1,0:T(8,128)(2,1)}), bf16[4,40,1536]{2,1,0:T(8,128)(2,1)S(1)}, u32[]{:S(2)}, u32[]{:S(2)}) async-start(bf16[4,40,1536]{2,1,0:T(8,128)(2,1)} %bitcast.12), calls=%async_computation.2 | async-start | bytes 983040 | tf_op jit(solution)/shard_map/all_to_all | solution.py:28
  92.7 18.1 %all-to-all-start.4 = ((bf16[4,40,1536]{2,1,0:T(8,128)(2,1)}), bf16[4,40,1536]{2,1,0:T(8,128)(2,1)S(1)}, u32[]{:S(2)}, u32[]{:S(2)}) async-start(bf16[4,40,1536]{2,1,0:T(8,128)(2,1)} %bitcast.14), calls=%async_computation.4 | async-start | bytes 983040 | tf_op jit(solution)/shard_map/all_to_all | solution.py:28
  96.3 16.9 %collective-permute-start.1 = (bf16[40,1536]{1,0:T(8,128)(2,1)S(1)}, bf16[40,1536]{1,0:T(8,128)(2,1)S(1)}, u32[]{:S(2)}, u32[]{:S(2)}) collective-permute-start(bf16[40,1536]{1,0:T(8,128)(2,1)S(1)} %reduce-precision_convert_fusion.1), channel_id=1, source_target_pairs={{0,32},{32,0},{1,33},{33,1},{2,34},{34,2},{3,35},{35,3},{4,36},{36... | collective-permute-start | bytes 368648 | tf_op jit(solution)/shard_map/ppermute | solution.py:37
  114.3 20.5 %all-to-all-start.3 = ((bf16[4,32,1536]{2,1,0:T(8,128)(2,1)}), bf16[4,32,1536]{2,1,0:T(8,128)(2,1)S(1)}, u32[]{:S(2)}, u32[]{:S(2)}) async-start(bf16[4,32,1536]{2,1,0:T(8,128)(2,1)} %broadcast_in_dim.19), calls=%async_computation.3 | async-start | bytes 786432 | tf_op jit(solution)/shard_map/all_to_all | solution.py:28
  118.5 91.9 %all-gather.8.cloned.1.call-start = ((), (), s32[]{:S(2)}) async-start(), calls=%async_computation.10 | async-start | bytes 7077888 | tf_op jit(solution)/shard_map/all_gather | solution.py:135
  118.5 21.4 %collective-permute-start.2 = (bf16[40,1536]{1,0:T(8,128)(2,1)S(1)}, bf16[40,1536]{1,0:T(8,128)(2,1)S(1)}, u32[]{:S(2)}, u32[]{:S(2)}) collective-permute-start(bf16[40,1536]{1,0:T(8,128)(2,1)S(1)} %reduce-precision_convert_fusion), channel_id=1, source_target_pairs={{0,32},{32,0},{1,33},{33,1},{2,34},{34,2},{3,35},{35,3},{4,36},{36... | collective-permute-start | bytes 368648 | tf_op jit(solution)/shard_map/ppermute | solution.py:37
  159.2 44.9 %copy-start.2 = (bf16[16,1536]{1,0:T(8,128)(2,1)S(1)}, bf16[16,1536]{1,0:T(8,128)(2,1)}, u32[]{:S(2)}) copy-start(bf16[16,1536]{1,0:T(8,128)(2,1)} %param.6) | copy-start | bytes 147460
  160.5 29.3 %all-to-all-start.6 = ((bf16[8,16,1792]{2,1,0:T(8,128)(2,1)}), bf16[8,16,1792]{2,1,0:T(8,128)(2,1)S(1)}, u32[]{:S(2)}, u32[]{:S(2)}) async-start(bf16[8,16,1792]{2,1,0:T(8,128)(2,1)} %concatenate.32), calls=%async_computation.6 | async-start | bytes 917504 | tf_op jit(solution)/shard_map/all_to_all | solution.py:28
  190.7 19.1 %all-to-all-start.7 = ((f32[8,48,128]{2,1,0:T(8,128)}), f32[8,48,128]{2,1,0:T(8,128)S(1)}, u32[]{:S(2)}, u32[]{:S(2)}) async-start(f32[8,48,128]{2,1,0:T(8,128)} %broadcast_in_dim.23), calls=%async_computation.7 | async-start | bytes 393216 | tf_op jit(solution)/shard_map/all_to_all | solution.py:28
  214.6 1.8 copy-start.1
Sparse Core Ops, SparseCore 0:
  10.2 67.5 all-gather.3
  79.9 38.9 all-gather.5
  152.3 55.8 all-gather.7

commit v7 on v5

--- a/solution.py
+++ b/solution.py
@@ -84,39 +84,45 @@
     extra_rows = 8
     block = halves * rows
     affine = jnp.stack([*split_float(ln_gain), *split_float(ln_bias)]).astype(bf16)
-    affine = jnp.pad(affine, ((0, extra_rows - 4), (0, 0)))
-    stacked = jnp.concatenate(
-        [
-            normed.reshape(around, block, width),
-            jnp.broadcast_to(affine[None], (around,) + affine.shape),
-        ],
-        axis=1,
-    )
-    stacked = stacked.reshape(-1, width)
+    stacked = jnp.concatenate([normed, jnp.pad(affine, ((0, extra_rows - 4), (0, 0)))])
     all_stacked = lax.all_gather(stacked, gx, axis=0, tiled=True)
     partial_hidden = jnp.dot(stacked, weight, preferred_element_type=f32).astype(bf16)
-    arrived = exchange(partial_hidden.reshape(around, block + extra_rows, hidden_width), "x")
+    affine_parts = partial_hidden[local : local + 4].astype(f32)
+    affine_parts = (affine_parts[0::2] + affine_parts[1::2]).astype(bf16)
+    share = 2 * hidden_width // block
+    affine_parts = jnp.pad(affine_parts.reshape(block, share), ((0, 0), (0, -share % 128)))
+    arrived = exchange(
+        jnp.concatenate(
+            [
+                partial_hidden[:local].reshape(around, block, hidden_width),
+                jnp.broadcast_to(affine_parts[None], (around,) + affine_parts.shape),
+            ],
+            axis=2,
+        ),
+        "x",
+    )
     half_sum = lax.reduce_precision(jnp.sum(arrived.astype(f32), axis=0), 8, 7)
     products = half_sum + swap(half_sum.astype(bf16)).astype(f32)
-    product = products[:block]
-    gain_product = products[block] + products[block + 1]
-    bias_product = products[block + 2] + products[block + 3]
+    product = products[:, :hidden_width]
+    affine_product = products[:, hidden_width : hidden_width + share].reshape(2, hidden_width)
     grad_pre = (cotangent * gelu_slope(product + up_bias)).astype(bf16)
     grad_pre_float = grad_pre.astype(f32)
     token_sums = jnp.stack(
         [
-            jnp.sum(grad_pre_float * gain_product, axis=1),
-            jnp.sum(grad_pre_float * (product - bias_product), axis=1),
-        ]
-    )
-    token_rows = jnp.concatenate(split_float(token_sums)).astype(bf16)
-    token_rows = jnp.pad(token_rows, ((0, extra_rows - 4), (0, hidden_width - block)))
-    around_rows = spread(jnp.concatenate([grad_pre, token_rows]), "x")
-    grad_local = around_rows[:, :block].reshape(local, hidden_width)
+            jnp.sum(grad_pre_float * affine_product[0], axis=1),
+            jnp.sum(grad_pre_float * (product - affine_product[1]), axis=1),
+        ],
+        axis=1,
+    )
+    token_columns = jnp.concatenate(split_float(token_sums), axis=1).astype(bf16)
+    around_rows = spread(
+        jnp.concatenate([grad_pre, jnp.pad(token_columns, ((0, 0), (0, 124)))], axis=1), "x"
+    )
+    grad_local = around_rows[:, :, :hidden_width].reshape(local, hidden_width)
     token_parts = (
-        around_rows[:, block : block + 4, :block]
-        .reshape(around, 4, halves, rows)
-        .transpose(2, 0, 3, 1)
+        around_rows[:, :, hidden_width : hidden_width + 4]
+        .reshape(around, halves, rows, 4)
+        .transpose(1, 0, 2, 3)
         .reshape(depth, rows, 4)
     )
 
@@ -173,7 +179,7 @@
     ).astype(bf16)
     feature_rows = (
         lax.dynamic_slice_in_dim(all_stacked, lax.axis_index(gx) * sub_width, sub_width, axis=1)
-        .reshape(-1, block + extra_rows, sub_width)[:, :block]
+        .reshape(-1, local + extra_rows, sub_width)[:, :local]
         .reshape(-1, sub_width)
     )
     grad_weight = lax.dot_general(

time: 222 us -> 216 us (0.973)
  starting transfers between devices: 92.7 us -> 88.3 us
    all_to_all x5, starting transfers between devices: 67.6 us -> 63.9 us  [exchange(): return lax.all_to_all(blocks, axis, split_axis=0, concat_axis=0, tiled=True)]
where the time goes in v7:
time: 216 us; the launch traced here: 215 us
  starting transfers between devices  88.3 us (41%)
  waiting for transfers between devices  68 us (31%)
  matrix products  17.6 us (8%)
  between operations  14.8 us (7%)
  blocking collectives  10.9 us (5%)
  local copies, waits for them, and re-layouts  9.41 us (4%)
  other arithmetic  5.83 us (3%)
    all_to_all x5, starting transfers between devices, exchange(): return lax.all_to_all(blocks, axis, split_axis=0, concat_axis=0, tiled=True)  63.9 us
    all_to_all x5, waiting for transfers between devices, exchange(): return lax.all_to_all(blocks, axis, split_axis=0, concat_axis=0, tiled=True)  50.3 us
    ppermute x2, starting transfers between devices, swap(): return lax.ppermute(block, 'zh', [(0, 1), (1, 0)])  24.3 us
    all_to_all x1, blocking collectives, exchange(): return lax.all_to_all(blocks, axis, split_axis=0, concat_axis=0, tiled=True)  10.9 us
    ppermute x2, waiting for transfers between devices, swap(): return lax.ppermute(block, 'zh', [(0, 1), (1, 0)])  10.3 us
    dot_general x1, matrix products, shards(): lax.dot_general(grad_local, weight, (((1,), (1,)), ((), ())), preferred_e...  7.23 us
    all_gather x1, waiting for transfers between devices, shards(): weight = lax.all_gather(weight_in, gx, axis=0, tiled=True)  6.73 us
    dot_general x1, matrix products, shards(): lax.dot_general(feature_rows, portion, (((0,), (0,)), ((), ())), preferre...  5.23 us
  transfers between devices with their start and end apart: 10, of which 8 were waited for; matrix products, arithmetic and copies ran while one was open for 13% of the time, Pallas kernels for 0%

profile of v7, /device:TPU:1, one launch (start us, length us, event | category | flops | bytes accessed | tf_op | source)
XLA Modules:
  0.0 214.8 jit_solution(2052219645046906625)
XLA Ops:
  7.9 1.6 broadcast_in_dim.14
  9.5 13.1 %all-to-all-start = ((bf16[8,16,1536]{2,1,0:T(8,128)(2,1)}), bf16[8,16,1536]{2,1,0:T(8,128)(2,1)S(1)}, u32[]{:S(2)}, u32[]{:S(2)}) async-start(bf16[8,16,1536]{2,1,0:T(8,128)(2,1)} %broadcast_in_dim.14), calls=%async_computation | async-start | bytes 786432 | tf_op jit(solution)/shard_map/all_to_all | solution.py:28
  22.6 7.9 %collective-permute-start = (bf16[16,3072]{1,0:T(8,128)(2,1)}, bf16[16,3072]{1,0:T(8,128)(2,1)S(1)}, u32[]{:S(2)}, u32[]{:S(2)}) collective-permute-start(bf16[16,3072]{1,0:T(8,128)(2,1)} %param.11), channel_id=1, source_target_pairs={{0,32},{32,0},{1,33},{33,1},{2,34},{34,2},{3,35},{35,3},{4,36},{36... | collective-permute-start | bytes 294920 | tf_op jit(solution)/shard_map/ppermute | solution.py:37
  32.0 6.2 %collective-permute-done = bf16[16,3072]{1,0:T(8,128)(2,1)S(1)} collective-permute-done((bf16[16,3072]{1,0:T(8,128)(2,1)}, bf16[16,3072]{1,0:T(8,128)(2,1)S(1)}, u32[]{:S(2)}, u32[]{:S(2)}) %collective-permute-start) | collective-permute-done | bytes 98336 | tf_op jit(solution)/shard_map/ppermute | solution.py:37
  39.3 5.8 %all-to-all-done = bf16[8,16,1536]{2,1,0:T(8,128)(2,1)S(1)} async-done(((bf16[8,16,1536]{2,1,0:T(8,128)(2,1)}), bf16[8,16,1536]{2,1,0:T(8,128)(2,1)S(1)}, u32[]{:S(2)}, u32[]{:S(2)}) %all-to-all-start) | async-done | bytes 393248 | tf_op jit(solution)/shard_map/all_to_all | solution.py:28
  46.3 9.8 %all-to-all-start.1 = ((f32[8,2,128]{2,1,0:T(2,128)}), f32[8,2,128]{2,1,0:T(2,128)S(1)}, u32[]{:S(2)}, u32[]{:S(2)}) async-start(f32[8,2,128]{2,1,0:T(2,128)} %broadcast_in_dim.15), calls=%async_computation.1 | async-start | bytes 16384 | tf_op jit(solution)/shard_map/all_to_all | solution.py:28
  56.3 13.6 %all-to-all-done.1 = f32[8,2,128]{2,1,0:T(2,128)S(1)} async-done(((f32[8,2,128]{2,1,0:T(2,128)}), f32[8,2,128]{2,1,0:T(2,128)S(1)}, u32[]{:S(2)}, u32[]{:S(2)}) %all-to-all-start.1) | async-done | bytes 8224 | tf_op jit(solution)/shard_map/all_to_all | solution.py:28
  71.0 6.7 %all-gather.4.cloned.1.call-done = bf16[1536,3072]{1,0:T(8,128)(2,1)} async-done(((bf16[192,3072]{1,0:T(8,128)(2,1)}), bf16[1536,3072]{1,0:T(8,128)(2,1)}) %all-gather.4.cloned.1.call-update) | async-done | bytes 9437200 | tf_op jit(solution)/shard_map/all_gather | solution.py:54
  77.7 5.1 %convolution_convert_fusion.1 = bf16[136,3072]{1,0:T(8,128)(2,1)S(1)} fusion(bf16[1536,3072]{1,0:T(8,128)(2,1)} %all-gather.4.cloned.1.call-done, bf16[8,1536]{1,0:T(8,128)(2,1)S(1)} %fusion.19, bf16[128,1536]{1,0:T(8,128)(2,1)S(1)} %add_convert_fusion), kind=kOutput, calls=%fused_computation.1 | convolution fusion | flops 1284710400 | bytes 10690560 | tf_op jit(solution)/shard_map/dot_general | solution.py:89
  83.2 1.0 pad_maximum_fusion
  84.2 4.0 %all-to-all-start.2 = ((bf16[4,32,3328]{2,1,0:T(8,128)(2,1)}), bf16[4,32,3328]{2,1,0:T(8,128)(2,1)S(1)}, u32[]{:S(2)}, u32[]{:S(2)}) async-start(bf16[4,32,3328]{2,1,0:T(8,128)(2,1)} %pad_maximum_fusion), calls=%async_computation.2 | async-start | bytes 1703936 | tf_op jit(solution)/shard_map/all_to_all | solution.py:28
  88.2 8.7 %all-to-all-done.2 = bf16[4,32,3328]{2,1,0:T(8,128)(2,1)S(1)} async-done(((bf16[4,32,3328]{2,1,0:T(8,128)(2,1)}), bf16[4,32,3328]{2,1,0:T(8,128)(2,1)S(1)}, u32[]{:S(2)}, u32[]{:S(2)}) %all-to-all-start.2) | async-done | bytes 852000 | tf_op jit(solution)/shard_map/all_to_all | solution.py:28
  97.0 16.4 %collective-permute-start.1 = (bf16[32,3328]{1,0:T(8,128)(2,1)S(1)}, bf16[32,3328]{1,0:T(8,128)(2,1)S(1)}, u32[]{:S(2)}, u32[]{:S(2)}) collective-permute-start(bf16[32,3328]{1,0:T(8,128)(2,1)S(1)} %reduce-precision_convert_fusion), channel_id=1, source_target_pairs={{0,32},{32,0},{1,33},{33,1},{2,34},{34,2},{3,35},{35,3},{4,36},{36... | collective-permute-start | bytes 638984 | tf_op jit(solution)/shard_map/ppermute | solution.py:37
  113.4 4.1 %collective-permute-done.1 = bf16[32,3328]{1,0:T(8,128)(2,1)S(1)} collective-permute-done((bf16[32,3328]{1,0:T(8,128)(2,1)S(1)}, bf16[32,3328]{1,0:T(8,128)(2,1)S(1)}, u32[]{:S(2)}, u32[]{:S(2)}) %collective-permute-start.1) | collective-permute-done | bytes 213024 | tf_op jit(solution)/shard_map/ppermute | solution.py:37
  118.5 10.9 %all_to_all.30 = bf16[4,32,3200]{2,1,0:T(8,128)(2,1)S(1)} all-to-all(bf16[4,32,3200]{2,1,0:T(8,128)(2,1)S(1)} %broadcast_in_dim.17), channel_id=1, replica_groups=mesh['y'=4,'core'=2,'zh'=2,'x'=4,'gz'=8] {'x'}, dimensions={0} | all-to-all | bytes 1638400 | tf_op jit(solution)/shard_map/all_to_all | solution.py:28
  129.4 1.0 slice.120
  130.4 7.2 %multiply_reduce_fusion = (bf16[1536]{0:T(1024)(128)(2,1)S(1)}, bf16[1536]{0:T(1024)(128)(2,1)S(1)}, bf16[128,1536]{1,0:T(8,128)(2,1)S(1)}) fusion(f32[4,2,16,1536]{3,2,1,0:T(8,128)S(1)} %copy.64, f32[128]{0:T(128)S(1)} %add_rsqrt_fusion, f32[128]{0:T(128)S(1)} %broadcast_multiply_fusion.1, bf16[128,3072]{1,0:T(8,128)(2,1)} %bitcast.57, ...), kind=kOutput, calls=%fused_computation.9 | convolution fusion | flops 1209136128 | bytes 11410432 | tf_op jit(solution)/shard_map/dot_general | solution.py:131
  138.1 0.9 concatenate.32
  139.0 25.9 %all-to-all-start.4 = ((bf16[8,16,1792]{2,1,0:T(8,128)(2,1)}), bf16[8,16,1792]{2,1,0:T(8,128)(2,1)S(1)}, u32[]{:S(2)}, u32[]{:S(2)}) async-start(bf16[8,16,1792]{2,1,0:T(8,128)(2,1)} %concatenate.32), calls=%async_computation.4 | async-start | bytes 917504 | tf_op jit(solution)/shard_map/all_to_all | solution.py:28
  165.1 1.4 constant_dynamic-slice_fusion
  166.7 17.2 %all-to-all-done.4 = bf16[8,16,1792]{2,1,0:T(8,128)(2,1)S(1)} async-done(((bf16[8,16,1792]{2,1,0:T(8,128)(2,1)}), bf16[8,16,1792]{2,1,0:T(8,128)(2,1)S(1)}, u32[]{:S(2)}, u32[]{:S(2)}) %all-to-all-start.4) | async-done | bytes 458784 | tf_op jit(solution)/shard_map/all_to_all | solution.py:28
  184.8 11.1 %all-to-all-start.5 = ((f32[8,48,128]{2,1,0:T(8,128)}), f32[8,48,128]{2,1,0:T(8,128)S(1)}, u32[]{:S(2)}, u32[]{:S(2)}) async-start(f32[8,48,128]{2,1,0:T(8,128)} %broadcast_in_dim.20), calls=%async_computation.5 | async-start | bytes 393216 | tf_op jit(solution)/shard_map/all_to_all | solution.py:28
  196.8 5.0 %all-to-all-done.5 = f32[8,48,128]{2,1,0:T(8,128)S(1)} async-done(((f32[8,48,128]{2,1,0:T(8,128)}), f32[8,48,128]{2,1,0:T(8,128)S(1)}, u32[]{:S(2)}, u32[]{:S(2)}) %all-to-all-start.5) | async-done | bytes 196640 | tf_op jit(solution)/shard_map/all_to_all | solution.py:28
  203.1 5.2 %convolution_convert_fusion = bf16[192,3072]{1,0:T(8,128)(2,1)} fusion(bf16[1024,192]{1,0:T(8,128)(2,1)S(1)} %bitcast.60, bf16[1024,3072]{1,0:T(8,128)(2,1)} %all-gather.8.cloned.1.call-done), kind=kOutput, calls=%fused_computation | convolution fusion | flops 1208549376 | bytes 7864320 | tf_op jit(solution)/shard_map/dot_general | solution.py:185
  (95 shorter events, 10.3 us)
Async XLA Ops:
  7.2 62.8 %copy-start.2 = (f32[1536]{0:T(1024)S(1)}, f32[1536]{0:T(1024)}, u32[]{:S(2)}) copy-start(f32[1536]{0:T(1024)} %param.7) | copy-start | bytes 18436
  7.2 62.8 %copy-start.3 = (f32[1536]{0:T(1024)S(1)}, f32[1536]{0:T(1024)}, u32[]{:S(2)}) copy-start(f32[1536]{0:T(1024)} %param.8) | copy-start | bytes 18436
  7.2 70.5 %all-gather.4.cloned.1.call-start = ((), (), s32[]{:S(2)}) async-start(), calls=%async_computation.6 | async-start | bytes 10616832 | tf_op jit(solution)/shard_map/all_gather | solution.py:54
  9.5 35.6 %all-to-all-start = ((bf16[8,16,1536]{2,1,0:T(8,128)(2,1)}), bf16[8,16,1536]{2,1,0:T(8,128)(2,1)S(1)}, u32[]{:S(2)}, u32[]{:S(2)}) async-start(bf16[8,16,1536]{2,1,0:T(8,128)(2,1)} %broadcast_in_dim.14), calls=%async_computation | async-start | bytes 786432 | tf_op jit(solution)/shard_map/all_to_all | solution.py:28
  22.6 15.6 %collective-permute-start = (bf16[16,3072]{1,0:T(8,128)(2,1)}, bf16[16,3072]{1,0:T(8,128)(2,1)S(1)}, u32[]{:S(2)}, u32[]{:S(2)}) collective-permute-start(bf16[16,3072]{1,0:T(8,128)(2,1)} %param.11), channel_id=1, source_target_pairs={{0,32},{32,0},{1,33},{33,1},{2,34},{34,2},{3,35},{35,3},{4,36},{36... | collective-permute-start | bytes 294920 | tf_op jit(solution)/shard_map/ppermute | solution.py:37
  46.3 23.5 %all-to-all-start.1 = ((f32[8,2,128]{2,1,0:T(2,128)}), f32[8,2,128]{2,1,0:T(2,128)S(1)}, u32[]{:S(2)}, u32[]{:S(2)}) async-start(f32[8,2,128]{2,1,0:T(2,128)} %broadcast_in_dim.15), calls=%async_computation.1 | async-start | bytes 16384 | tf_op jit(solution)/shard_map/all_to_all | solution.py:28
  56.1 109.0 %all-gather.6.cloned.1.call-start = ((), (), s32[]{:S(2)}) async-start(), calls=%async_computation.7 | async-start | bytes 3760128 | tf_op jit(solution)/shard_map/all_gather | solution.py:88
  83.0 30.4 %copy-start.1 = (bf16[16,3072]{1,0:T(8,128)(2,1)S(1)}, bf16[16,3072]{1,0:T(8,128)(2,1)}, u32[]{:S(2)}) copy-start(bf16[16,3072]{1,0:T(8,128)(2,1)} %param.11) | copy-start | bytes 294916
  83.2 34.6 %copy-start.4 = (f32[3072]{0:T(1024)S(1)}, f32[3072]{0:T(1024)}, u32[]{:S(2)}) copy-start(f32[3072]{0:T(1024)} %param.10) | copy-start | bytes 36868
  84.2 12.7 %all-to-all-start.2 = ((bf16[4,32,3328]{2,1,0:T(8,128)(2,1)}), bf16[4,32,3328]{2,1,0:T(8,128)(2,1)S(1)}, u32[]{:S(2)}, u32[]{:S(2)}) async-start(bf16[4,32,3328]{2,1,0:T(8,128)(2,1)} %pad_maximum_fusion), calls=%async_computation.2 | async-start | bytes 1703936 | tf_op jit(solution)/shard_map/all_to_all | solution.py:28
  88.1 114.9 %all-gather.8.cloned.1.call-start = ((), (), s32[]{:S(2)}) async-start(), calls=%async_computation.8 | async-start | bytes 7077888 | tf_op jit(solution)/shard_map/all_gather | solution.py:129
  97.0 20.6 %collective-permute-start.1 = (bf16[32,3328]{1,0:T(8,128)(2,1)S(1)}, bf16[32,3328]{1,0:T(8,128)(2,1)S(1)}, u32[]{:S(2)}, u32[]{:S(2)}) collective-permute-start(bf16[32,3328]{1,0:T(8,128)(2,1)S(1)} %reduce-precision_convert_fusion), channel_id=1, source_target_pairs={{0,32},{32,0},{1,33},{33,1},{2,34},{34,2},{3,35},{35,3},{4,36},{36... | collective-permute-start | bytes 638984 | tf_op jit(solution)/shard_map/ppermute | solution.py:37
  137.8 58.3 %copy-start = (bf16[16,1536]{1,0:T(8,128)(2,1)S(1)}, bf16[16,1536]{1,0:T(8,128)(2,1)}, u32[]{:S(2)}) copy-start(bf16[16,1536]{1,0:T(8,128)(2,1)} %param.6) | copy-start | bytes 147460
  139.0 45.0 %all-to-all-start.4 = ((bf16[8,16,1792]{2,1,0:T(8,128)(2,1)}), bf16[8,16,1792]{2,1,0:T(8,128)(2,1)S(1)}, u32[]{:S(2)}, u32[]{:S(2)}) async-start(bf16[8,16,1792]{2,1,0:T(8,128)(2,1)} %concatenate.32), calls=%async_computation.4 | async-start | bytes 917504 | tf_op jit(solution)/shard_map/all_to_all | solution.py:28
  184.8 17.1 %all-to-all-start.5 = ((f32[8,48,128]{2,1,0:T(8,128)}), f32[8,48,128]{2,1,0:T(8,128)S(1)}, u32[]{:S(2)}, u32[]{:S(2)}) async-start(f32[8,48,128]{2,1,0:T(8,128)} %broadcast_in_dim.20), calls=%async_computation.5 | async-start | bytes 393216 | tf_op jit(solution)/shard_map/all_to_all | solution.py:28
Sparse Core Ops, SparseCore 0:
  10.1 67.5 all-gather.3
  79.9 36.5 all-gather.5
  130.5 62.4 all-gather.7

commit v8 on v7

--- a/solution.py
+++ b/solution.py
@@ -63,11 +63,12 @@
     own_mean = jnp.mean(x_float, axis=1)
     own_centered = x_float - own_mean[:, None]
     own_square = jnp.sum(own_centered * own_centered, axis=1)
-    other_cotangent = swap(grad_hidden)
-    own_square = own_square + 0.0 * other_cotangent[0, 0].astype(f32)
+    late_cotangent = grad_hidden + (0.0 * x_float[0, 0]).astype(bf16)
+    other_cotangent = swap(late_cotangent)
     moments = spread(jnp.stack([own_mean, own_square]), gy)
     mean = jnp.mean(moments[:, 0], axis=0)
     shift = moments[:, 0] - mean
+    shift = shift + 0.0 * other_cotangent[0, 0].astype(f32)
     variance = (jnp.sum(moments[:, 1], axis=0) + width * jnp.sum(shift * shift, axis=0)) / D
     inv_std = lax.rsqrt(variance + epsilon)
     x_hat = (x_float - mean[:, None]) * inv_std[:, None]
@@ -160,9 +161,7 @@
             jnp.sum(grad_local.astype(f32), axis=0),
         ]
     ).reshape(-1, 128)
-    small = jnp.sum(spread(small, gx), axis=0).reshape(-1)
-    grad_ln_gain, grad_ln_bias = small[:width], small[width : 2 * width]
-    grad_up_bias = small[2 * width :]
+    small_parts = spread(small, gx)
 
     def mine(value):
         ordered = value.reshape(around, halves, rows).transpose(1, 0, 2).reshape(depth, rows)
@@ -185,6 +184,10 @@
     grad_weight = lax.dot_general(
         feature_rows, portion, (((0,), (0,)), ((), ())), preferred_element_type=f32
     ).astype(bf16)
+    tie = 0.0 * grad_weight[0, 0].astype(f32)
+    small = jnp.sum(small_parts + tie, axis=0).reshape(-1)
+    grad_ln_gain, grad_ln_bias = small[:width], small[width : 2 * width]
+    grad_up_bias = small[2 * width :]
     return (grad_inputs, grad_weight, grad_up_bias, grad_ln_gain, grad_ln_bias)
 
 

time: 216 us -> 212 us (0.981)
  waiting for transfers between devices: 68 us -> 61.1 us
    all_to_all x5, waiting for transfers between devices: 50.3 us -> 45.5 us  [exchange(): return lax.all_to_all(blocks, axis, split_axis=0, concat_axis=0, tiled=True)]
    ppermute x2, waiting for transfers between devices: 10.3 us -> 5.93 us  [swap(): return lax.ppermute(block, 'zh', [(0, 1), (1, 0)])]
  transfers between devices with their start and end apart: 10 -> 10, of which waited for: 8 -> 7; matrix products, arithmetic and copies ran while one was open for 13% -> 15% of each run, Pallas kernels for 0% -> 0%
where the time goes in v8:
time: 212 us; the launch traced here: 211 us
  starting transfers between devices  89.9 us (42%)
  waiting for transfers between devices  61.1 us (29%)
  matrix products  16.6 us (8%)
  between operations  16.1 us (8%)
  blocking collectives  10.9 us (5%)
  local copies, waits for them, and re-layouts  10.5 us (5%)
  other arithmetic  5.83 us (3%)
    all_to_all x5, starting transfers between devices, exchange(): return lax.all_to_all(blocks, axis, split_axis=0, concat_axis=0, tiled=True)  64.7 us
    all_to_all x5, waiting for transfers between devices, exchange(): return lax.all_to_all(blocks, axis, split_axis=0, concat_axis=0, tiled=True)  45.5 us
    ppermute x2, starting transfers between devices, swap(): return lax.ppermute(block, 'zh', [(0, 1), (1, 0)])  25.1 us
    all_to_all x1, blocking collectives, exchange(): return lax.all_to_all(blocks, axis, split_axis=0, concat_axis=0, tiled=True)  10.9 us
    all_gather x1, waiting for transfers between devices, shards(): weight = lax.all_gather(weight_in, gx, axis=0, tiled=True)  8.87 us
    dot_general x1, matrix products, shards(): lax.dot_general(grad_local, weight, (((1,), (1,)), ((), ())), preferred_e...  7.23 us
    ppermute x2, waiting for transfers between devices, swap(): return lax.ppermute(block, 'zh', [(0, 1), (1, 0)])  5.93 us
    dot_general x1, matrix products, shards(): jnp.dot(stacked, weight, preferred_element_type=f32).astype(bf16)  5.14 us
  transfers between devices with their start and end apart: 10, of which 7 were waited for; matrix products, arithmetic and copies ran while one was open for 15% of the time, Pallas kernels for 0%

profile of v8, /device:TPU:1, one launch (start us, length us, event | category | flops | bytes accessed | tf_op | source)
XLA Modules:
  0.0 210.9 jit_solution(7325053693507718710)
XLA Ops:
  7.9 1.6 broadcast_in_dim.14
  9.5 13.1 %all-to-all-start = ((bf16[8,16,1536]{2,1,0:T(8,128)(2,1)}), bf16[8,16,1536]{2,1,0:T(8,128)(2,1)S(1)}, u32[]{:S(2)}, u32[]{:S(2)}) async-start(bf16[8,16,1536]{2,1,0:T(8,128)(2,1)} %broadcast_in_dim.14), calls=%async_computation | async-start | bytes 786432 | tf_op jit(solution)/shard_map/all_to_all | solution.py:28
  24.1 15.9 %all-to-all-done = bf16[8,16,1536]{2,1,0:T(8,128)(2,1)S(1)} async-done(((bf16[8,16,1536]{2,1,0:T(8,128)(2,1)}), bf16[8,16,1536]{2,1,0:T(8,128)(2,1)S(1)}, u32[]{:S(2)}, u32[]{:S(2)}) %all-to-all-start) | async-done | bytes 393248 | tf_op jit(solution)/shard_map/all_to_all | solution.py:28
  41.2 9.8 %all-to-all-start.1 = ((f32[8,2,128]{2,1,0:T(2,128)}), f32[8,2,128]{2,1,0:T(2,128)S(1)}, u32[]{:S(2)}, u32[]{:S(2)}) async-start(f32[8,2,128]{2,1,0:T(2,128)} %broadcast_in_dim.15), calls=%async_computation.1 | async-start | bytes 16384 | tf_op jit(solution)/shard_map/all_to_all | solution.py:28
  52.4 12.0 %collective-permute-start = (bf16[16,3072]{1,0:T(8,128)(2,1)S(1)}, bf16[16,3072]{1,0:T(8,128)(2,1)S(1)}, u32[]{:S(2)}, u32[]{:S(2)}) collective-permute-start(bf16[16,3072]{1,0:T(8,128)(2,1)S(1)} %broadcast_add_fusion), channel_id=1, source_target_pairs={{0,32},{32,0},{1,33},{33,1},{2,34},{34,2},{3,35},{35,3},{4,36},{36... | collective-permute-start | bytes 294920 | tf_op jit(solution)/shard_map/ppermute | solution.py:37
  64.8 1.8 collective-permute-done
  68.1 0.8 pad_maximum_fusion.1
  68.9 8.9 %all-gather.4.cloned.1.call-done = bf16[1536,3072]{1,0:T(8,128)(2,1)} async-done(((bf16[192,3072]{1,0:T(8,128)(2,1)}), bf16[1536,3072]{1,0:T(8,128)(2,1)}) %all-gather.4.cloned.1.call-update) | async-done | bytes 9437200 | tf_op jit(solution)/shard_map/all_gather | solution.py:54
  77.7 5.1 %convolution_convert_fusion.1 = bf16[136,3072]{1,0:T(8,128)(2,1)S(1)} fusion(bf16[1536,3072]{1,0:T(8,128)(2,1)} %all-gather.4.cloned.1.call-done, bf16[8,1536]{1,0:T(8,128)(2,1)S(1)} %fusion.18, bf16[128,1536]{1,0:T(8,128)(2,1)S(1)} %add_convert_fusion), kind=kOutput, calls=%fused_computation.1 | convolution fusion | flops 1284710400 | bytes 10690560 | tf_op jit(solution)/shard_map/dot_general | solution.py:90
  83.2 1.0 pad_maximum_fusion
  84.2 4.0 %all-to-all-start.2 = ((bf16[4,32,3328]{2,1,0:T(8,128)(2,1)}), bf16[4,32,3328]{2,1,0:T(8,128)(2,1)S(1)}, u32[]{:S(2)}, u32[]{:S(2)}) async-start(bf16[4,32,3328]{2,1,0:T(8,128)(2,1)} %pad_maximum_fusion), calls=%async_computation.2 | async-start | bytes 1703936 | tf_op jit(solution)/shard_map/all_to_all | solution.py:28
  88.1 12.0 %all-to-all-done.2 = bf16[4,32,3328]{2,1,0:T(8,128)(2,1)S(1)} async-done(((bf16[4,32,3328]{2,1,0:T(8,128)(2,1)}), bf16[4,32,3328]{2,1,0:T(8,128)(2,1)S(1)}, u32[]{:S(2)}, u32[]{:S(2)}) %all-to-all-start.2) | async-done | bytes 852000 | tf_op jit(solution)/shard_map/all_to_all | solution.py:28
  100.3 13.1 %collective-permute-start.1 = (bf16[32,3328]{1,0:T(8,128)(2,1)S(1)}, bf16[32,3328]{1,0:T(8,128)(2,1)S(1)}, u32[]{:S(2)}, u32[]{:S(2)}) collective-permute-start(bf16[32,3328]{1,0:T(8,128)(2,1)S(1)} %reduce-precision_convert_fusion), channel_id=1, source_target_pairs={{0,32},{32,0},{1,33},{33,1},{2,34},{34,2},{3,35},{35,3},{4,36},{36... | collective-permute-start | bytes 638984 | tf_op jit(solution)/shard_map/ppermute | solution.py:37
  113.4 4.1 %collective-permute-done.1 = bf16[32,3328]{1,0:T(8,128)(2,1)S(1)} collective-permute-done((bf16[32,3328]{1,0:T(8,128)(2,1)S(1)}, bf16[32,3328]{1,0:T(8,128)(2,1)S(1)}, u32[]{:S(2)}, u32[]{:S(2)}) %collective-permute-start.1) | collective-permute-done | bytes 213024 | tf_op jit(solution)/shard_map/ppermute | solution.py:37
  118.5 10.9 %all_to_all.30 = bf16[4,32,3200]{2,1,0:T(8,128)(2,1)S(1)} all-to-all(bf16[4,32,3200]{2,1,0:T(8,128)(2,1)S(1)} %broadcast_in_dim.17), channel_id=1, replica_groups=mesh['y'=4,'core'=2,'zh'=2,'x'=4,'gz'=8] {'x'}, dimensions={0} | all-to-all | bytes 1638400 | tf_op jit(solution)/shard_map/all_to_all | solution.py:28
  129.4 1.0 slice.129
  130.4 7.2 %multiply_reduce_fusion = (bf16[1536]{0:T(1024)(128)(2,1)S(1)}, bf16[1536]{0:T(1024)(128)(2,1)S(1)}, bf16[128,1536]{1,0:T(8,128)(2,1)S(1)}) fusion(f32[128]{0:T(128)S(1)} %add_rsqrt_fusion, f32[128]{0:T(128)S(1)} %broadcast_multiply_fusion.1, f32[4,2,16,1536]{3,2,1,0:T(8,128)S(1)} %copy.67, bf16[128,3072]{1,0:T(8,128)(2,1)} %bitcast.53, ...), kind=kOutput, calls=%fused_computation.7 | convolution fusion | flops 1209136128 | bytes 11410432 | tf_op jit(solution)/shard_map/dot_general | solution.py:132
  138.1 0.9 concatenate.32
  139.0 26.8 %all-to-all-start.4 = ((bf16[8,16,1792]{2,1,0:T(8,128)(2,1)}), bf16[8,16,1792]{2,1,0:T(8,128)(2,1)S(1)}, u32[]{:S(2)}, u32[]{:S(2)}) async-start(bf16[8,16,1792]{2,1,0:T(8,128)(2,1)} %concatenate.32), calls=%async_computation.4 | async-start | bytes 917504 | tf_op jit(solution)/shard_map/all_to_all | solution.py:28
  166.0 1.4 constant_dynamic-slice_fusion
  167.5 17.2 %all-to-all-done.4 = bf16[8,16,1792]{2,1,0:T(8,128)(2,1)S(1)} async-done(((bf16[8,16,1792]{2,1,0:T(8,128)(2,1)}), bf16[8,16,1792]{2,1,0:T(8,128)(2,1)S(1)}, u32[]{:S(2)}, u32[]{:S(2)}) %all-to-all-start.4) | async-done | bytes 458784 | tf_op jit(solution)/shard_map/all_to_all | solution.py:28
  185.6 11.1 %all-to-all-start.5 = ((f32[8,48,128]{2,1,0:T(8,128)}), f32[8,48,128]{2,1,0:T(8,128)S(1)}, u32[]{:S(2)}, u32[]{:S(2)}) async-start(f32[8,48,128]{2,1,0:T(8,128)} %broadcast_in_dim.20), calls=%async_computation.5 | async-start | bytes 393216 | tf_op jit(solution)/shard_map/all_to_all | solution.py:28
  196.9 0.7 multiply_convert_fusion
  197.7 4.2 %convolution_convert_fusion = bf16[192,3072]{1,0:T(8,128)(2,1)S(1)} fusion(bf16[1024,192]{1,0:T(8,128)(2,1)S(1)} %bitcast.56, bf16[1024,3072]{1,0:T(8,128)(2,1)} %all-gather.8.cloned.1.call-done), kind=kOutput, calls=%fused_computation | convolution fusion | flops 1208549376 | bytes 7864320 | tf_op jit(solution)/shard_map/dot_general | solution.py:184
  (99 shorter events, 10.2 us)
Async XLA Ops:
  7.2 60.7 %copy-start.3 = (f32[1536]{0:T(1024)S(1)}, f32[1536]{0:T(1024)}, u32[]{:S(2)}) copy-start(f32[1536]{0:T(1024)} %param.7) | copy-start | bytes 18436
  7.2 60.7 %copy-start.4 = (f32[1536]{0:T(1024)S(1)}, f32[1536]{0:T(1024)}, u32[]{:S(2)}) copy-start(f32[1536]{0:T(1024)} %param.8) | copy-start | bytes 18436
  7.2 45.2 %copy-start.1 = (bf16[16,3072]{1,0:T(8,128)(2,1)S(1)}, bf16[16,3072]{1,0:T(8,128)(2,1)}, u32[]{:S(2)}) copy-start(bf16[16,3072]{1,0:T(8,128)(2,1)} %param.11) | copy-start | bytes 294916
  7.2 70.5 %all-gather.4.cloned.1.call-start = ((), (), s32[]{:S(2)}) async-start(), calls=%async_computation.6 | async-start | bytes 10616832 | tf_op jit(solution)/shard_map/all_gather | solution.py:54
  9.5 30.5 %all-to-all-start = ((bf16[8,16,1536]{2,1,0:T(8,128)(2,1)}), bf16[8,16,1536]{2,1,0:T(8,128)(2,1)S(1)}, u32[]{:S(2)}, u32[]{:S(2)}) async-start(bf16[8,16,1536]{2,1,0:T(8,128)(2,1)} %broadcast_in_dim.14), calls=%async_computation | async-start | bytes 786432 | tf_op jit(solution)/shard_map/all_to_all | solution.py:28
  41.2 23.6 %all-to-all-start.1 = ((f32[8,2,128]{2,1,0:T(2,128)}), f32[8,2,128]{2,1,0:T(2,128)S(1)}, u32[]{:S(2)}, u32[]{:S(2)}) async-start(f32[8,2,128]{2,1,0:T(2,128)} %broadcast_in_dim.15), calls=%async_computation.1 | async-start | bytes 16384 | tf_op jit(solution)/shard_map/all_to_all | solution.py:28
  51.0 114.9 %all-gather.6.cloned.1.call-start = ((), (), s32[]{:S(2)}) async-start(), calls=%async_computation.7 | async-start | bytes 3760128 | tf_op jit(solution)/shard_map/all_gather | solution.py:89
  52.4 14.3 %collective-permute-start = (bf16[16,3072]{1,0:T(8,128)(2,1)S(1)}, bf16[16,3072]{1,0:T(8,128)(2,1)S(1)}, u32[]{:S(2)}, u32[]{:S(2)}) collective-permute-start(bf16[16,3072]{1,0:T(8,128)(2,1)S(1)} %broadcast_add_fusion), channel_id=1, source_target_pairs={{0,32},{32,0},{1,33},{33,1},{2,34},{34,2},{3,35},{35,3},{4,36},{36... | collective-permute-start | bytes 294920 | tf_op jit(solution)/shard_map/ppermute | solution.py:37
  83.2 34.6 %copy-start.5 = (f32[3072]{0:T(1024)S(1)}, f32[3072]{0:T(1024)}, u32[]{:S(2)}) copy-start(f32[3072]{0:T(1024)} %param.10) | copy-start | bytes 36868
  84.2 16.0 %all-to-all-start.2 = ((bf16[4,32,3328]{2,1,0:T(8,128)(2,1)}), bf16[4,32,3328]{2,1,0:T(8,128)(2,1)S(1)}, u32[]{:S(2)}, u32[]{:S(2)}) async-start(bf16[4,32,3328]{2,1,0:T(8,128)(2,1)} %pad_maximum_fusion), calls=%async_computation.2 | async-start | bytes 1703936 | tf_op jit(solution)/shard_map/all_to_all | solution.py:28
  88.1 109.5 %all-gather.8.cloned.1.call-start = ((), (), s32[]{:S(2)}) async-start(), calls=%async_computation.8 | async-start | bytes 7077888 | tf_op jit(solution)/shard_map/all_gather | solution.py:130
  100.3 17.2 %collective-permute-start.1 = (bf16[32,3328]{1,0:T(8,128)(2,1)S(1)}, bf16[32,3328]{1,0:T(8,128)(2,1)S(1)}, u32[]{:S(2)}, u32[]{:S(2)}) collective-permute-start(bf16[32,3328]{1,0:T(8,128)(2,1)S(1)} %reduce-precision_convert_fusion), channel_id=1, source_target_pairs={{0,32},{32,0},{1,33},{33,1},{2,34},{34,2},{3,35},{35,3},{4,36},{36... | collective-permute-start | bytes 638984 | tf_op jit(solution)/shard_map/ppermute | solution.py:37
  137.8 59.2 %copy-start.2 = (bf16[16,1536]{1,0:T(8,128)(2,1)S(1)}, bf16[16,1536]{1,0:T(8,128)(2,1)}, u32[]{:S(2)}) copy-start(bf16[16,1536]{1,0:T(8,128)(2,1)} %param.6) | copy-start | bytes 147460
  139.0 45.8 %all-to-all-start.4 = ((bf16[8,16,1792]{2,1,0:T(8,128)(2,1)}), bf16[8,16,1792]{2,1,0:T(8,128)(2,1)S(1)}, u32[]{:S(2)}, u32[]{:S(2)}) async-start(bf16[8,16,1792]{2,1,0:T(8,128)(2,1)} %concatenate.32), calls=%async_computation.4 | async-start | bytes 917504 | tf_op jit(solution)/shard_map/all_to_all | solution.py:28
  185.6 17.5 %all-to-all-start.5 = ((f32[8,48,128]{2,1,0:T(8,128)}), f32[8,48,128]{2,1,0:T(8,128)S(1)}, u32[]{:S(2)}, u32[]{:S(2)}) async-start(f32[8,48,128]{2,1,0:T(8,128)} %broadcast_in_dim.20), calls=%async_computation.5 | async-start | bytes 393216 | tf_op jit(solution)/shard_map/all_to_all | solution.py:28
  201.9 2.5 %copy-start = (bf16[192,3072]{1,0:T(8,128)(2,1)}, bf16[192,3072]{1,0:T(8,128)(2,1)S(1)}, u32[]{:S(2)}) copy-start(bf16[192,3072]{1,0:T(8,128)(2,1)S(1)} %convolution_convert_fusion) | copy-start | bytes 3538948
Sparse Core Ops, SparseCore 0:
  10.2 67.5 all-gather.3
  79.9 36.5 all-gather.5
  130.5 63.0 all-gather.7

commit v9 on v8

--- a/solution.py
+++ b/solution.py
@@ -68,7 +68,6 @@
     moments = spread(jnp.stack([own_mean, own_square]), gy)
     mean = jnp.mean(moments[:, 0], axis=0)
     shift = moments[:, 0] - mean
-    shift = shift + 0.0 * other_cotangent[0, 0].astype(f32)
     variance = (jnp.sum(moments[:, 1], axis=0) + width * jnp.sum(shift * shift, axis=0)) / D
     inv_std = lax.rsqrt(variance + epsilon)
     x_hat = (x_float - mean[:, None]) * inv_std[:, None]
@@ -89,7 +88,8 @@
     all_stacked = lax.all_gather(stacked, gx, axis=0, tiled=True)
     partial_hidden = jnp.dot(stacked, weight, preferred_element_type=f32).astype(bf16)
     affine_parts = partial_hidden[local : local + 4].astype(f32)
-    affine_parts = (affine_parts[0::2] + affine_parts[1::2]).astype(bf16)
+    affine_parts = affine_parts[0::2] + affine_parts[1::2]
+    affine_parts = (affine_parts + 0.0 * other_cotangent[0, 0].astype(f32)).astype(bf16)
     share = 2 * hidden_width // block
     affine_parts = jnp.pad(affine_parts.reshape(block, share), ((0, 0), (0, -share % 128)))
     arrived = exchange(

time: 212 us -> 212 us (level)
  no operation moved by 1% of the time
where the time goes in v9:
time: 212 us; the launch traced here: 211 us
  starting transfers between devices  89.3 us (42%)
  waiting for transfers between devices  61.6 us (29%)
  matrix products  16.6 us (8%)
  between operations  16.1 us (8%)
  blocking collectives  10.9 us (5%)
  local copies, waits for them, and re-layouts  10.5 us (5%)
  other arithmetic  5.83 us (3%)
    all_to_all x5, starting transfers between devices, exchange(): return lax.all_to_all(blocks, axis, split_axis=0, concat_axis=0, tiled=True)  64.7 us
    all_to_all x5, waiting for transfers between devices, exchange(): return lax.all_to_all(blocks, axis, split_axis=0, concat_axis=0, tiled=True)  46.1 us
    ppermute x2, starting transfers between devices, swap(): return lax.ppermute(block, 'zh', [(0, 1), (1, 0)])  24.6 us
    all_to_all x1, blocking collectives, exchange(): return lax.all_to_all(blocks, axis, split_axis=0, concat_axis=0, tiled=True)  10.9 us
    all_gather x1, waiting for transfers between devices, shards(): weight = lax.all_gather(weight_in, gx, axis=0, tiled=True)  9.93 us
    dot_general x1, matrix products, shards(): lax.dot_general(grad_local, weight, (((1,), (1,)), ((), ())), preferred_e...  7.23 us
    dot_general x1, matrix products, shards(): jnp.dot(stacked, weight, preferred_element_type=f32).astype(bf16)  5.14 us
    ppermute x2, waiting for transfers between devices, swap(): return lax.ppermute(block, 'zh', [(0, 1), (1, 0)])  4.87 us
  transfers between devices with their start and end apart: 10, of which 7 were waited for; matrix products, arithmetic and copies ran while one was open for 15% of the time, Pallas kernels for 0%

profile of v9, /device:TPU:1, one launch (start us, length us, event | category | flops | bytes accessed | tf_op | source)
XLA Modules:
  0.0 210.9 jit_solution(5454085333455816127)
XLA Ops:
  7.9 1.6 broadcast_in_dim.14
  9.5 13.1 %all-to-all-start = ((bf16[8,16,1536]{2,1,0:T(8,128)(2,1)}), bf16[8,16,1536]{2,1,0:T(8,128)(2,1)S(1)}, u32[]{:S(2)}, u32[]{:S(2)}) async-start(bf16[8,16,1536]{2,1,0:T(8,128)(2,1)} %broadcast_in_dim.14), calls=%async_computation | async-start | bytes 786432 | tf_op jit(solution)/shard_map/all_to_all | solution.py:28
  24.1 15.9 %all-to-all-done = bf16[8,16,1536]{2,1,0:T(8,128)(2,1)S(1)} async-done(((bf16[8,16,1536]{2,1,0:T(8,128)(2,1)}), bf16[8,16,1536]{2,1,0:T(8,128)(2,1)S(1)}, u32[]{:S(2)}, u32[]{:S(2)}) %all-to-all-start) | async-done | bytes 393248 | tf_op jit(solution)/shard_map/all_to_all | solution.py:28
  41.2 9.8 %all-to-all-start.1 = ((f32[8,2,128]{2,1,0:T(2,128)}), f32[8,2,128]{2,1,0:T(2,128)S(1)}, u32[]{:S(2)}, u32[]{:S(2)}) async-start(f32[8,2,128]{2,1,0:T(2,128)} %broadcast_in_dim.15), calls=%async_computation.1 | async-start | bytes 16384 | tf_op jit(solution)/shard_map/all_to_all | solution.py:28
  52.4 12.0 %collective-permute-start = (bf16[16,3072]{1,0:T(8,128)(2,1)S(1)}, bf16[16,3072]{1,0:T(8,128)(2,1)S(1)}, u32[]{:S(2)}, u32[]{:S(2)}) collective-permute-start(bf16[16,3072]{1,0:T(8,128)(2,1)S(1)} %broadcast_add_fusion), channel_id=1, source_target_pairs={{0,32},{32,0},{1,33},{33,1},{2,34},{34,2},{3,35},{35,3},{4,36},{36... | collective-permute-start | bytes 294920 | tf_op jit(solution)/shard_map/ppermute | solution.py:37
  65.1 0.8 pad_maximum_fusion.1
  65.9 0.7 collective-permute-done
  67.8 9.9 %all-gather.4.cloned.1.call-done = bf16[1536,3072]{1,0:T(8,128)(2,1)} async-done(((bf16[192,3072]{1,0:T(8,128)(2,1)}), bf16[1536,3072]{1,0:T(8,128)(2,1)}) %all-gather.4.cloned.1.call-update) | async-done | bytes 9437200 | tf_op jit(solution)/shard_map/all_gather | solution.py:54
  77.7 5.1 %convolution_convert_fusion.1 = bf16[136,3072]{1,0:T(8,128)(2,1)S(1)} fusion(bf16[1536,3072]{1,0:T(8,128)(2,1)} %all-gather.4.cloned.1.call-done, bf16[8,1536]{1,0:T(8,128)(2,1)S(1)} %fusion.18, bf16[128,1536]{1,0:T(8,128)(2,1)S(1)} %add_convert_fusion), kind=kOutput, calls=%fused_computation.1 | convolution fusion | flops 1284710400 | bytes 10690560 | tf_op jit(solution)/shard_map/dot_general | solution.py:89
  83.2 1.0 pad_maximum_fusion
  84.2 4.0 %all-to-all-start.2 = ((bf16[4,32,3328]{2,1,0:T(8,128)(2,1)}), bf16[4,32,3328]{2,1,0:T(8,128)(2,1)S(1)}, u32[]{:S(2)}, u32[]{:S(2)}) async-start(bf16[4,32,3328]{2,1,0:T(8,128)(2,1)} %pad_maximum_fusion), calls=%async_computation.2 | async-start | bytes 1703936 | tf_op jit(solution)/shard_map/all_to_all | solution.py:28
  88.1 12.6 %all-to-all-done.2 = bf16[4,32,3328]{2,1,0:T(8,128)(2,1)S(1)} async-done(((bf16[4,32,3328]{2,1,0:T(8,128)(2,1)}), bf16[4,32,3328]{2,1,0:T(8,128)(2,1)S(1)}, u32[]{:S(2)}, u32[]{:S(2)}) %all-to-all-start.2) | async-done | bytes 852000 | tf_op jit(solution)/shard_map/all_to_all | solution.py:28
  100.9 12.5 %collective-permute-start.1 = (bf16[32,3328]{1,0:T(8,128)(2,1)S(1)}, bf16[32,3328]{1,0:T(8,128)(2,1)S(1)}, u32[]{:S(2)}, u32[]{:S(2)}) collective-permute-start(bf16[32,3328]{1,0:T(8,128)(2,1)S(1)} %reduce-precision_convert_fusion), channel_id=1, source_target_pairs={{0,32},{32,0},{1,33},{33,1},{2,34},{34,2},{3,35},{35,3},{4,36},{36... | collective-permute-start | bytes 638984 | tf_op jit(solution)/shard_map/ppermute | solution.py:37
  113.4 4.1 %collective-permute-done.1 = bf16[32,3328]{1,0:T(8,128)(2,1)S(1)} collective-permute-done((bf16[32,3328]{1,0:T(8,128)(2,1)S(1)}, bf16[32,3328]{1,0:T(8,128)(2,1)S(1)}, u32[]{:S(2)}, u32[]{:S(2)}) %collective-permute-start.1) | collective-permute-done | bytes 213024 | tf_op jit(solution)/shard_map/ppermute | solution.py:37
  118.5 10.9 %all_to_all.30 = bf16[4,32,3200]{2,1,0:T(8,128)(2,1)S(1)} all-to-all(bf16[4,32,3200]{2,1,0:T(8,128)(2,1)S(1)} %broadcast_in_dim.17), channel_id=1, replica_groups=mesh['y'=4,'core'=2,'zh'=2,'x'=4,'gz'=8] {'x'}, dimensions={0} | all-to-all | bytes 1638400 | tf_op jit(solution)/shard_map/all_to_all | solution.py:28
  129.4 1.0 slice.129
  130.4 7.2 %multiply_reduce_fusion = (bf16[1536]{0:T(1024)(128)(2,1)S(1)}, bf16[1536]{0:T(1024)(128)(2,1)S(1)}, bf16[128,1536]{1,0:T(8,128)(2,1)S(1)}) fusion(f32[128]{0:T(128)S(1)} %add_rsqrt_fusion, f32[128]{0:T(128)S(1)} %broadcast_multiply_fusion.1, f32[4,2,16,1536]{3,2,1,0:T(8,128)S(1)} %copy.68, bf16[128,3072]{1,0:T(8,128)(2,1)} %bitcast.53, ...), kind=kOutput, calls=%fused_computation.7 | convolution fusion | flops 1209136128 | bytes 11410432 | tf_op jit(solution)/shard_map/dot_general | solution.py:132
  138.1 0.9 concatenate.32
  139.0 26.7 %all-to-all-start.4 = ((bf16[8,16,1792]{2,1,0:T(8,128)(2,1)}), bf16[8,16,1792]{2,1,0:T(8,128)(2,1)S(1)}, u32[]{:S(2)}, u32[]{:S(2)}) async-start(bf16[8,16,1792]{2,1,0:T(8,128)(2,1)} %concatenate.32), calls=%async_computation.4 | async-start | bytes 917504 | tf_op jit(solution)/shard_map/all_to_all | solution.py:28
  165.9 1.4 constant_dynamic-slice_fusion
  167.5 17.2 %all-to-all-done.4 = bf16[8,16,1792]{2,1,0:T(8,128)(2,1)S(1)} async-done(((bf16[8,16,1792]{2,1,0:T(8,128)(2,1)}), bf16[8,16,1792]{2,1,0:T(8,128)(2,1)S(1)}, u32[]{:S(2)}, u32[]{:S(2)}) %all-to-all-start.4) | async-done | bytes 458784 | tf_op jit(solution)/shard_map/all_to_all | solution.py:28
  185.6 11.1 %all-to-all-start.5 = ((f32[8,48,128]{2,1,0:T(8,128)}), f32[8,48,128]{2,1,0:T(8,128)S(1)}, u32[]{:S(2)}, u32[]{:S(2)}) async-start(f32[8,48,128]{2,1,0:T(8,128)} %broadcast_in_dim.20), calls=%async_computation.5 | async-start | bytes 393216 | tf_op jit(solution)/shard_map/all_to_all | solution.py:28
  196.9 0.7 multiply_convert_fusion
  197.6 4.2 %convolution_convert_fusion = bf16[192,3072]{1,0:T(8,128)(2,1)S(1)} fusion(bf16[1024,192]{1,0:T(8,128)(2,1)S(1)} %bitcast.56, bf16[1024,3072]{1,0:T(8,128)(2,1)} %all-gather.8.cloned.1.call-done), kind=kOutput, calls=%fused_computation | convolution fusion | flops 1208549376 | bytes 7864320 | tf_op jit(solution)/shard_map/dot_general | solution.py:184
  (99 shorter events, 10.2 us)
Async XLA Ops:
  7.2 57.7 %copy-start.3 = (f32[1536]{0:T(1024)S(1)}, f32[1536]{0:T(1024)}, u32[]{:S(2)}) copy-start(f32[1536]{0:T(1024)} %param.7) | copy-start | bytes 18436
  7.2 57.7 %copy-start.4 = (f32[1536]{0:T(1024)S(1)}, f32[1536]{0:T(1024)}, u32[]{:S(2)}) copy-start(f32[1536]{0:T(1024)} %param.8) | copy-start | bytes 18436
  7.2 45.2 %copy-start.1 = (bf16[16,3072]{1,0:T(8,128)(2,1)S(1)}, bf16[16,3072]{1,0:T(8,128)(2,1)}, u32[]{:S(2)}) copy-start(bf16[16,3072]{1,0:T(8,128)(2,1)} %param.11) | copy-start | bytes 294916
  7.2 70.5 %all-gather.4.cloned.1.call-start = ((), (), s32[]{:S(2)}) async-start(), calls=%async_computation.6 | async-start | bytes 10616832 | tf_op jit(solution)/shard_map/all_gather | solution.py:54
  9.5 30.5 %all-to-all-start = ((bf16[8,16,1536]{2,1,0:T(8,128)(2,1)}), bf16[8,16,1536]{2,1,0:T(8,128)(2,1)S(1)}, u32[]{:S(2)}, u32[]{:S(2)}) async-start(bf16[8,16,1536]{2,1,0:T(8,128)(2,1)} %broadcast_in_dim.14), calls=%async_computation | async-start | bytes 786432 | tf_op jit(solution)/shard_map/all_to_all | solution.py:28
  41.2 23.6 %all-to-all-start.1 = ((f32[8,2,128]{2,1,0:T(2,128)}), f32[8,2,128]{2,1,0:T(2,128)S(1)}, u32[]{:S(2)}, u32[]{:S(2)}) async-start(f32[8,2,128]{2,1,0:T(2,128)} %broadcast_in_dim.15), calls=%async_computation.1 | async-start | bytes 16384 | tf_op jit(solution)/shard_map/all_to_all | solution.py:28
  51.0 114.9 %all-gather.6.cloned.1.call-start = ((), (), s32[]{:S(2)}) async-start(), calls=%async_computation.7 | async-start | bytes 3760128 | tf_op jit(solution)/shard_map/all_gather | solution.py:88
  52.4 14.3 %collective-permute-start = (bf16[16,3072]{1,0:T(8,128)(2,1)S(1)}, bf16[16,3072]{1,0:T(8,128)(2,1)S(1)}, u32[]{:S(2)}, u32[]{:S(2)}) collective-permute-start(bf16[16,3072]{1,0:T(8,128)(2,1)S(1)} %broadcast_add_fusion), channel_id=1, source_target_pairs={{0,32},{32,0},{1,33},{33,1},{2,34},{34,2},{3,35},{35,3},{4,36},{36... | collective-permute-start | bytes 294920 | tf_op jit(solution)/shard_map/ppermute | solution.py:37
  83.2 34.6 %copy-start.5 = (f32[3072]{0:T(1024)S(1)}, f32[3072]{0:T(1024)}, u32[]{:S(2)}) copy-start(f32[3072]{0:T(1024)} %param.10) | copy-start | bytes 36868
  84.2 16.5 %all-to-all-start.2 = ((bf16[4,32,3328]{2,1,0:T(8,128)(2,1)}), bf16[4,32,3328]{2,1,0:T(8,128)(2,1)S(1)}, u32[]{:S(2)}, u32[]{:S(2)}) async-start(bf16[4,32,3328]{2,1,0:T(8,128)(2,1)} %pad_maximum_fusion), calls=%async_computation.2 | async-start | bytes 1703936 | tf_op jit(solution)/shard_map/all_to_all | solution.py:28
  88.1 109.5 %all-gather.8.cloned.1.call-start = ((), (), s32[]{:S(2)}) async-start(), calls=%async_computation.8 | async-start | bytes 7077888 | tf_op jit(solution)/shard_map/all_gather | solution.py:130
  100.9 16.7 %collective-permute-start.1 = (bf16[32,3328]{1,0:T(8,128)(2,1)S(1)}, bf16[32,3328]{1,0:T(8,128)(2,1)S(1)}, u32[]{:S(2)}, u32[]{:S(2)}) collective-permute-start(bf16[32,3328]{1,0:T(8,128)(2,1)S(1)} %reduce-precision_convert_fusion), channel_id=1, source_target_pairs={{0,32},{32,0},{1,33},{33,1},{2,34},{34,2},{3,35},{35,3},{4,36},{36... | collective-permute-start | bytes 638984 | tf_op jit(solution)/shard_map/ppermute | solution.py:37
  137.8 59.1 %copy-start.2 = (bf16[16,1536]{1,0:T(8,128)(2,1)S(1)}, bf16[16,1536]{1,0:T(8,128)(2,1)}, u32[]{:S(2)}) copy-start(bf16[16,1536]{1,0:T(8,128)(2,1)} %param.6) | copy-start | bytes 147460
  139.0 45.7 %all-to-all-start.4 = ((bf16[8,16,1792]{2,1,0:T(8,128)(2,1)}), bf16[8,16,1792]{2,1,0:T(8,128)(2,1)S(1)}, u32[]{:S(2)}, u32[]{:S(2)}) async-start(bf16[8,16,1792]{2,1,0:T(8,128)(2,1)} %concatenate.32), calls=%async_computation.4 | async-start | bytes 917504 | tf_op jit(solution)/shard_map/all_to_all | solution.py:28
  185.6 17.5 %all-to-all-start.5 = ((f32[8,48,128]{2,1,0:T(8,128)}), f32[8,48,128]{2,1,0:T(8,128)S(1)}, u32[]{:S(2)}, u32[]{:S(2)}) async-start(f32[8,48,128]{2,1,0:T(8,128)} %broadcast_in_dim.20), calls=%async_computation.5 | async-start | bytes 393216 | tf_op jit(solution)/shard_map/all_to_all | solution.py:28
  201.8 2.5 %copy-start = (bf16[192,3072]{1,0:T(8,128)(2,1)}, bf16[192,3072]{1,0:T(8,128)(2,1)S(1)}, u32[]{:S(2)}) copy-start(bf16[192,3072]{1,0:T(8,128)(2,1)S(1)} %convolution_convert_fusion) | copy-start | bytes 3538948
Sparse Core Ops, SparseCore 0:
  10.2 67.5 all-gather.3
  79.9 36.5 all-gather.5
  130.5 63.0 all-gather.7
